TPU v7x, 32 devices: a whole 2x2x4 slice. The times are simulated.
32 devices in a mesh: dp: 2 (over y), mp: 16 (over z, x, core).
Axes of the slice: x: 2, y: 2, z: 4, core: 2. Of those that a mesh axis runs over, the one named last changes fastest.
Arguments:
- queries: bfloat16 [2048, 4096], P('mp', 'dp'), may hold values from -200 to 200
- cache: bfloat16 [128, 128, 896], P('mp', 'dp'), may hold values from -6 to 6
- cache_scale: float32 [128, 128], P('mp', 'dp'), may hold values from 0.5 to 2
- w_kv: bfloat16 [2, 896, 2048], P(None, 'mp', 'dp'), may hold values from -0.1875 to 0.1875
- nbr_shard: int32 [64, 2], replicated, may hold values from 0 to 15, as said below
- nbr_row: int32 [64, 2], replicated, may hold values from 0 to 7
- grad_out: bfloat16 [2048, 4096], P('mp', 'dp'), may hold values from -6 to 6
Outputs:
- output: bfloat16 [2048, 4096], P('mp', 'dp')
- grad_queries: bfloat16 [2048, 4096], P('mp', 'dp')
Inputs may be any that keep to these rules, and one draw needn't show every extreme that they name: `nbr_shard`: span c belongs to device c // 2 in dp-major order. Among the 2 * 2 * 2 requests of the spans whose devices share one mp index, no shard is named more than 2 times, and some shard exactly 2 times.
All inputs are finite; a program needn't handle non-finite values.
Results may differ from a plain program's by a relative error of at most 0.012.
The roundings to bfloat16 on the way count: a program that leaves them out, or rounds other values in their place, can miss the bound.
Values may be sent and summed in bfloat16 or wider, within the bound.
No kernel may reach another device: no remote copies, remote signals or barrier semaphores. Data moves between devices by JAX's collectives and lax.ppermute only.
A program may use at most 64 MiB of HBM per device.

v0:
```python
import jax
import jax.numpy as jnp
from jax import lax
from jax.sharding import PartitionSpec as P

HEADS = 16
HEAD_DIM = 128
E = 896
NT = 128
SPAN = 64
NBR = 2
CH_DEV = 2


def shards(queries, cache, cache_scale, w_kv, nbr_shard, nbr_row, grad_out):
    dp_count = lax.axis_size("dp")
    mp_count = lax.axis_size("mp")
    my_mp = lax.axis_index("mp")
    slice_len = cache.shape[1]
    most_slots = 2 * ((dp_count * CH_DEV * NBR + mp_count - 1) // mp_count)
    block_size = dp_count * CH_DEV * NBR
    score_scale = HEAD_DIM ** (-0.5)
    local_query = lax.all_to_all(queries, "mp", split_axis=1, concat_axis=0, tiled=True)
    shard_blk = (
        nbr_shard.reshape(dp_count, mp_count, CH_DEV * NBR)
        .transpose(1, 0, 2)
        .reshape(mp_count, block_size)
    )
    row_blk = (
        nbr_row.reshape(dp_count, mp_count, CH_DEV * NBR)
        .transpose(1, 0, 2)
        .reshape(mp_count, block_size)
    )
    positions = jnp.arange(block_size, dtype=jnp.int32)
    earlier = positions[None, :] < positions[:, None]
    same_shard = shard_blk[:, :, None] == shard_blk[:, None, :]
    slot_blk = jnp.sum(jnp.logical_and(same_shard, earlier[None]), axis=2)
    to_me = shard_blk == my_mp
    slot_ids = jnp.arange(most_slots, dtype=jnp.int32)
    select = jnp.logical_and(to_me[:, None, :], slot_blk[:, None, :] == slot_ids[None, :, None])
    wanted = jnp.sum(jnp.where(select, row_blk[:, None, :], 0), axis=2)
    sending = (cache[wanted].astype(jnp.float32) * cache_scale[wanted][..., None]).astype(
        jnp.bfloat16
    )
    arrived = lax.all_to_all(sending, "mp", split_axis=0, concat_axis=0, tiled=True)
    flat_pieces = arrived.reshape(mp_count * most_slots, slice_len, E)
    own_shards = lax.dynamic_index_in_dim(shard_blk, my_mp, 0, keepdims=False)
    own_slots = lax.dynamic_index_in_dim(slot_blk, my_mp, 0, keepdims=False)
    pieces = jnp.take(flat_pieces, own_shards * most_slots + own_slots, axis=0)
    pieces = pieces.reshape(dp_count, CH_DEV * NBR, slice_len, E)
    gathered = lax.all_to_all(pieces, "dp", split_axis=0, concat_axis=2, tiled=True)
    neighbours = gathered.reshape(CH_DEV, NBR * NT, E)
    tall_weights = lax.all_gather(w_kv, "mp", axis=1, tiled=True)
    key_value = jnp.einsum(
        "cte,ken->kctn",
        neighbours,
        lax.all_gather(tall_weights, "dp", axis=2, tiled=True),
        preferred_element_type=jnp.float32,
    ).astype(jnp.bfloat16)
    key_rows = key_value[0].reshape(CH_DEV, NBR * NT, HEADS, HEAD_DIM)
    values = key_value[1].reshape(CH_DEV, NBR * NT, HEADS, HEAD_DIM)
    query_c = local_query.reshape(HEADS, HEAD_DIM, CH_DEV, SPAN)
    affinity_logits = (
        jnp.einsum("hdcq,ckhd->chqk", query_c, key_rows, preferred_element_type=jnp.float32)
        * score_scale
    )
    row_max = jnp.max(affinity_logits, axis=3, keepdims=True)
    exponent = jnp.exp(affinity_logits - row_max)
    attn_probs = exponent / jnp.sum(exponent, axis=3, keepdims=True)
    probs_low = attn_probs.astype(jnp.bfloat16)
    output_c = jnp.einsum(
        "chqk,ckhd->hdcq", probs_low, values, preferred_element_type=jnp.float32
    ).astype(jnp.bfloat16)
    output_rows = output_c.reshape(HEADS * HEAD_DIM, CH_DEV * SPAN)
    output_back = lax.all_to_all(output_rows, "mp", split_axis=0, concat_axis=1, tiled=True)
    local_grad = lax.all_to_all(grad_out, "mp", split_axis=1, concat_axis=0, tiled=True)
    grad_c = local_grad.reshape(HEADS, HEAD_DIM, CH_DEV, SPAN)
    dprobs = jnp.einsum("hdcq,ckhd->chqk", grad_c, values, preferred_element_type=jnp.float32)
    row_delta = jnp.einsum("hdcq,hdcq->chq", grad_c, output_c, preferred_element_type=jnp.float32)
    dscores = (attn_probs * (dprobs - row_delta[..., None]) * score_scale).astype(jnp.bfloat16)
    grad_query = jnp.einsum(
        "chqk,ckhd->hdcq", dscores, key_rows, preferred_element_type=jnp.float32
    ).astype(jnp.bfloat16)
    grad_rows = grad_query.reshape(HEADS * HEAD_DIM, CH_DEV * SPAN)
    grad_back = lax.all_to_all(grad_rows, "mp", split_axis=0, concat_axis=1, tiled=True)
    return (output_back, grad_back)


def solution(mesh):
    return jax.shard_map(
        shards,
        mesh=mesh,
        in_specs=(
            P("mp", "dp"),
            P("mp", "dp", None),
            P("mp", "dp"),
            P(None, "mp", "dp"),
            P(),
            P(),
            P("mp", "dp"),
        ),
        out_specs=(P("mp", "dp"), P("mp", "dp")),
        check_vma=False,
    )
```

profile of v0, /device:TPU:0, one launch (start us, length us, event | category | flops | bytes accessed | tf_op | source)
XLA Modules:
  0.0 289.8 jit_solution(15319696012019803790)
XLA Ops:
  7.2 0.0 copy-start
  7.2 0.0 all-gather.3.cloned.1.call-start
  7.2 0.7 all-gather.3.cloned.1.call-update
  7.9 0.8 copy.48
  8.7 0.1 reshape.130
  8.8 0.1 copy.49
  8.9 0.8 copy.50
  9.6 0.1 reshape.132
  9.7 0.1 copy.51
  9.8 0.1 convert_reduce_fusion
  9.9 0.1 copy.52
  10.0 0.1 reshape.139
  10.1 0.0 copy-done
  10.1 0.0 copy-start.1
  10.1 2.7 gather_fusion
  12.9 0.0 copy-done.1
  12.9 0.6 gather_fusion.1
  13.5 4.6 %fusion.1 = bf16[16,2,64,896]{3,2,1,0:T(8,128)(2,1)} fusion(bf16[16,2,64,896]{3,2,1,0:T(8,128)(2,1)} %bitcast.87, f32[16,2,64]{2,1,0:T(2,128)S(1)} %bitcast.105), kind=kLoop, calls=%fused_computation.5 | loop fusion | flops 5505024 | bytes 7348224 | tf_op jit(solution)/shard_map/convert_element_type | solution.py:42
  18.1 7.4 %all-to-all-start = ((bf16[16,2,64,896]{3,2,1,0:T(8,128)(2,1)}), bf16[16,2,64,896]{3,2,1,0:T(8,128)(2,1)}, u32[]{:S(2)}, u32[]{:S(2)}) async-start(bf16[16,2,64,896]{3,2,1,0:T(8,128)(2,1)} %fusion.1), calls=%async_computation | async-start | bytes 7340032 | tf_op jit(solution)/shard_map/all_to_all | solution.py:45
  25.5 0.0 all-gather.5.cloned.1.call-start
  25.5 79.6 %all-gather.3.cloned.1.call-done = bf16[2,896,1024]{2,1,0:T(8,128)(2,1)} async-done(((bf16[2,56,1024]{2,1,0:T(8,128)(2,1)}), bf16[2,896,1024]{2,1,0:T(8,128)(2,1)}) %all-gather.3.cloned.1.call-update) | async-done | bytes 3670032 | tf_op jit(solution)/shard_map/all_gather | solution.py:53
  105.1 0.0 all-gather.5.cloned.1.call-update
  105.1 0.2 add_reduce_fusion
  105.3 0.1 add.53
  105.4 7.4 %all-to-all-done = bf16[16,2,64,896]{3,2,1,0:T(8,128)(2,1)} async-done(((bf16[16,2,64,896]{3,2,1,0:T(8,128)(2,1)}), bf16[16,2,64,896]{3,2,1,0:T(8,128)(2,1)}, u32[]{:S(2)}, u32[]{:S(2)}) %all-to-all-start) | async-done | bytes 3670048 | tf_op jit(solution)/shard_map/all_to_all | solution.py:45
  112.8 3.3 %gather_fusion.2 = bf16[8,64,896]{2,1,0:T(8,128)(2,1)S(1)} fusion(bf16[32,64,896]{2,1,0:T(8,128)(2,1)} %bitcast.9, s32[1024]{0:T(1024)S(1)} %pad_clamp_fusion), kind=kCustom, calls=%fused_computation.2 | custom fusion | bytes 1835040 | tf_op jit(solution)/shard_map/jit(_take)/gather | solution.py:49
  116.1 0.0 copy-start.4
  116.2 1.1 broadcast_select_fusion
  117.2 0.0 copy-start.5
  117.2 3.7 %all-to-all-start.1 = ((bf16[2,4,64,896]{3,2,1,0:T(8,128)(2,1)}), bf16[2,4,64,896]{3,2,1,0:T(8,128)(2,1)S(1)}, u32[]{:S(2)}, u32[]{:S(2)}) async-start(bf16[2,4,64,896]{3,2,1,0:T(8,128)(2,1)} %broadcast_select_fusion), calls=%async_computation.1 | async-start | bytes 1835008 | tf_op jit(solution)/shard_map/all_to_all | solution.py:51
  121.0 0.0 copy-done.4
  121.0 1.0 copy.54
  122.0 22.1 %all-to-all-done.1 = bf16[2,4,64,896]{3,2,1,0:T(8,128)(2,1)S(1)} async-done(((bf16[2,4,64,896]{3,2,1,0:T(8,128)(2,1)}), bf16[2,4,64,896]{3,2,1,0:T(8,128)(2,1)S(1)}, u32[]{:S(2)}, u32[]{:S(2)}) %all-to-all-start.1) | async-done | bytes 917536 | tf_op jit(solution)/shard_map/all_to_all | solution.py:51
  144.1 17.2 %all-to-all-start.2 = ((bf16[128,16,128]{0,2,1:T(8,128)(2,1)}), bf16[128,16,128]{0,2,1:T(8,128)(2,1)S(1)}, u32[]{:S(2)}, u32[]{:S(2)}) async-start(bf16[128,16,128]{0,2,1:T(8,128)(2,1)} %bitcast.19), calls=%async_computation.2 | async-start | bytes 1048576 | tf_op jit(solution)/shard_map/all_to_all | solution.py:23
  161.3 0.0 copy-done.5
  161.3 1.0 copy.60
  162.3 0.1 copy.53
  162.4 46.0 %all-gather.5.cloned.1.call-done = bf16[2,896,2048]{2,1,0:T(8,128)(2,1)} async-done(((bf16[2,896,1024]{2,1,0:T(8,128)(2,1)}), bf16[2,896,2048]{2,1,0:T(8,128)(2,1)}) %all-gather.5.cloned.1.call-update) | async-done | bytes 7340048 | tf_op jit(solution)/shard_map/all_gather | solution.py:57
  208.4 9.1 %convert_bitcast_fusion = bf16[2,2,256,2048]{3,2,0,1:T(8,128)(2,1)} fusion(bf16[2,256,896,1]{2,1,3,0:T(8,128)(2,1)S(1)} %bitcast.99, bf16[2,896,2048]{2,1,0:T(8,128)(2,1)} %all-gather.5.cloned.1.call-done), kind=kOutput, calls=%fused_computation.8 | convolution fusion | flops 3760193536 | bytes 12451840 | tf_op jit(solution)/shard_map/cte,ken->kctn/dot_general | solution.py:54
  217.5 0.0 all-to-all-done.2
  217.5 5.7 %all-to-all-start.4 = ((bf16[128,16,128]{0,2,1:T(8,128)(2,1)}), bf16[128,16,128]{0,2,1:T(8,128)(2,1)}, u32[]{:S(2)}, u32[]{:S(2)}) async-start(bf16[128,16,128]{0,2,1:T(8,128)(2,1)} %bitcast.27), calls=%async_computation.4 | async-start | bytes 1048576 | tf_op jit(solution)/shard_map/all_to_all | solution.py:76
  223.2 2.7 fusion.39
  226.0 0.6 copy.77
  226.6 2.0 copy.78
  228.6 0.8 fusion.16
  229.4 1.8 fusion.40
  231.2 6.5 %all-to-all-done.4 = bf16[128,16,128]{0,2,1:T(8,128)(2,1)} async-done(((bf16[128,16,128]{0,2,1:T(8,128)(2,1)}), bf16[128,16,128]{0,2,1:T(8,128)(2,1)}, u32[]{:S(2)}, u32[]{:S(2)}) %all-to-all-start.4) | async-done | bytes 524320 | tf_op jit(solution)/shard_map/all_to_all | solution.py:76
  237.7 0.0 copy-start.2
  237.7 0.0 copy-start.3
  237.7 4.4 %fusion.29 = (f32[2,16,64]{2,0,1:T(2,128)S(1)}, bf16[16,2,128,64]{2,3,1,0:T(8,128)(2,1)}) fusion(bf16[2,16,64,128]{3,2,0,1:T(8,128)(2,1)} %bitcast.1, bf16[2,256,16,128]{3,2,1,0:T(8,128)(2,1)} %bitcast.95, f32[2,16,64,256]{3,2,1,0:T(8,128)} %get-tuple-element.5, f32[2,16,64]{2,1,0:T(8,128)S(1)} %get-tuple-element.4), kind=kOutput, calls=%fused_computation.28 | convolution fusion | flops 136574976 | bytes 5259264 | tf_op jit(solution)/shard_map/chqk,ckhd->hdcq/dot_general | solution.py:71
  242.1 0.0 copy-done.2
  242.1 0.0 copy-done.3
  242.2 2.0 fusion.7
  244.2 0.9 fusion.26
  245.1 18.4 %all_to_all.90 = bf16[16,128,128]{1,2,0:T(8,128)(2,1)S(1)} all-to-all(bf16[16,128,128]{1,2,0:T(8,128)(2,1)S(1)} %bitcast.101), channel_id=1, replica_groups=mesh['dp'=2,'mp'=16] {'mp'}, dimensions={0} | all-to-all | bytes 1048576 | tf_op jit(solution)/shard_map/all_to_all | solution.py:85
  263.4 4.1 %all-to-all-start.3 = ((bf16[16,128,128]{1,2,0:T(8,128)(2,1)}), bf16[16,128,128]{1,2,0:T(8,128)(2,1)S(1)}, u32[]{:S(2)}, u32[]{:S(2)}) async-start(bf16[16,128,128]{1,2,0:T(8,128)(2,1)} %bitcast.100), calls=%async_computation.3 | async-start | bytes 1048576 | tf_op jit(solution)/shard_map/all_to_all | solution.py:75
  267.5 1.0 copy.76
  268.5 13.5 %all-to-all-done.3 = bf16[16,128,128]{1,2,0:T(8,128)(2,1)S(1)} async-done(((bf16[16,128,128]{1,2,0:T(8,128)(2,1)}), bf16[16,128,128]{1,2,0:T(8,128)(2,1)S(1)}, u32[]{:S(2)}, u32[]{:S(2)}) %all-to-all-start.3) | async-done | bytes 524320 | tf_op jit(solution)/shard_map/all_to_all | solution.py:75
  282.0 1.0 copy.74
  (9 shorter events, 0.1 us)
Async XLA Ops:
  7.2 3.0 %copy-start = (bf16[8,64,896]{2,1,0:T(8,128)(2,1)S(1)}, bf16[8,64,896]{2,1,0:T(8,128)(2,1)}, u32[]{:S(2)}) copy-start(bf16[8,64,896]{2,1,0:T(8,128)(2,1)} %param.8) | copy-start | bytes 2752516
  7.2 97.9 %all-gather.3.cloned.1.call-start = ((), (), s32[]{:S(2)}) async-start(), calls=%async_computation.6 | async-start | bytes 3899392 | tf_op jit(solution)/shard_map/all_gather | solution.py:53
  10.1 2.8 copy-start.1
  18.1 94.7 %all-to-all-start = ((bf16[16,2,64,896]{3,2,1,0:T(8,128)(2,1)}), bf16[16,2,64,896]{3,2,1,0:T(8,128)(2,1)}, u32[]{:S(2)}, u32[]{:S(2)}) async-start(bf16[16,2,64,896]{3,2,1,0:T(8,128)(2,1)} %fusion.1), calls=%async_computation | async-start | bytes 7340032 | tf_op jit(solution)/shard_map/all_to_all | solution.py:45
  25.5 182.9 %all-gather.5.cloned.1.call-start = ((), (), s32[]{:S(2)}) async-start(), calls=%async_computation.7 | async-start | bytes 11010048 | tf_op jit(solution)/shard_map/all_gather | solution.py:57
  116.1 4.8 %copy-start.4 = (bf16[128,2048]{1,0:T(8,128)(2,1)S(1)}, bf16[128,2048]{1,0:T(8,128)(2,1)}, u32[]{:S(2)}) copy-start(bf16[128,2048]{1,0:T(8,128)(2,1)} %param.7) | copy-start | bytes 1572868
  117.2 44.0 %copy-start.5 = (bf16[128,2048]{1,0:T(8,128)(2,1)S(1)}, bf16[128,2048]{1,0:T(8,128)(2,1)}, u32[]{:S(2)}) copy-start(bf16[128,2048]{1,0:T(8,128)(2,1)} %param.13) | copy-start | bytes 1572868
  117.2 26.8 %all-to-all-start.1 = ((bf16[2,4,64,896]{3,2,1,0:T(8,128)(2,1)}), bf16[2,4,64,896]{3,2,1,0:T(8,128)(2,1)S(1)}, u32[]{:S(2)}, u32[]{:S(2)}) async-start(bf16[2,4,64,896]{3,2,1,0:T(8,128)(2,1)} %broadcast_select_fusion), calls=%async_computation.1 | async-start | bytes 1835008 | tf_op jit(solution)/shard_map/all_to_all | solution.py:51
  144.1 73.5 %all-to-all-start.2 = ((bf16[128,16,128]{0,2,1:T(8,128)(2,1)}), bf16[128,16,128]{0,2,1:T(8,128)(2,1)S(1)}, u32[]{:S(2)}, u32[]{:S(2)}) async-start(bf16[128,16,128]{0,2,1:T(8,128)(2,1)} %bitcast.19), calls=%async_computation.2 | async-start | bytes 1048576 | tf_op jit(solution)/shard_map/all_to_all | solution.py:23
  217.5 20.2 %all-to-all-start.4 = ((bf16[128,16,128]{0,2,1:T(8,128)(2,1)}), bf16[128,16,128]{0,2,1:T(8,128)(2,1)}, u32[]{:S(2)}, u32[]{:S(2)}) async-start(bf16[128,16,128]{0,2,1:T(8,128)(2,1)} %bitcast.27), calls=%async_computation.4 | async-start | bytes 1048576 | tf_op jit(solution)/shard_map/all_to_all | solution.py:76
  237.7 4.4 %copy-start.2 = (bf16[64,8,16,128]{3,2,1,0:T(8,128)(2,1)S(1)}, bf16[64,8,16,128]{3,2,1,0:T(8,128)(2,1)}, u32[]{:S(2)}) copy-start(bf16[64,8,16,128]{3,2,1,0:T(8,128)(2,1)} %copy.78) | copy-start | bytes 6291460
  237.7 4.4 %copy-start.3 = (f32[2,16,64,256]{3,2,1,0:T(8,128)S(1)}, f32[2,16,64,256]{3,2,1,0:T(8,128)}, u32[]{:S(2)}) copy-start(f32[2,16,64,256]{3,2,1,0:T(8,128)} %get-tuple-element.5) | copy-start | bytes 6291460
  263.4 18.6 %all-to-all-start.3 = ((bf16[16,128,128]{1,2,0:T(8,128)(2,1)}), bf16[16,128,128]{1,2,0:T(8,128)(2,1)S(1)}, u32[]{:S(2)}, u32[]{:S(2)}) async-start(bf16[16,128,128]{1,2,0:T(8,128)(2,1)} %bitcast.100), calls=%async_computation.3 | async-start | bytes 1048576 | tf_op jit(solution)/shard_map/all_to_all | solution.py:75
Sparse Core Ops, SparseCore 0:
  10.3 94.7 all-gather.2
  106.6 101.7 all-gather.4
where the time goes:
time: 291 us; the launch traced here: 290 us
  waiting for transfers between devices  176 us (60%)
  starting transfers between devices  38.2 us (13%)
  blocking collectives  18.4 us (6%)
  local copies, waits for them, and re-layouts  18.2 us (6%)
  matrix products  17.3 us (6%)
  between operations  14.2 us (5%)
  other arithmetic  7.84 us (3%)
    all_gather x1, waiting for transfers between devices, shards(): tall_weights = lax.all_gather(w_kv, 'mp', axis=1, tiled=True)  79.6 us
    all_gather x1, waiting for transfers between devices, shards(): lax.all_gather(tall_weights, 'dp', axis=2, tiled=True)  46 us
    all_to_all x1, waiting for transfers between devices, shards(): lax.all_to_all(pieces, 'dp', split_axis=0, concat_axis=2, tiled=True)  22.1 us
    all_to_all x1, blocking collectives, shards(): lax.all_to_all(grad_rows, 'mp', split_axis=0, concat_axis=1, tiled=True)  18.4 us
    all_to_all x1, starting transfers between devices, shards(): lax.all_to_all(queries, 'mp', split_axis=1, concat_axis=0, tiled=True)  17.2 us
    all_to_all x1, waiting for transfers between devices, shards(): lax.all_to_all(output_rows, 'mp', split_axis=0, concat_axis=1, tiled=True)  13.5 us
    dot_general x1, matrix products, shards(): jnp.einsum('cte,ken->kctn', neighbours, lax.all_gather(tall_weights, 'dp'...  9.13 us
    all_to_all x1, starting transfers between devices, shards(): lax.all_to_all(sending, 'mp', split_axis=0, concat_axis=0, tiled=True)  7.4 us
  transfers between devices with their start and end apart: 7, of which 6 were waited for; matrix products, arithmetic and copies ran while one was open for 12% of the time, Pallas kernels for 0%

commit v1 on v0

--- a/solution.py
+++ b/solution.py
@@ -50,12 +50,14 @@
     pieces = pieces.reshape(dp_count, CH_DEV * NBR, slice_len, E)
     gathered = lax.all_to_all(pieces, "dp", split_axis=0, concat_axis=2, tiled=True)
     neighbours = gathered.reshape(CH_DEV, NBR * NT, E)
-    tall_weights = lax.all_gather(w_kv, "mp", axis=1, tiled=True)
+    gathered_weights = lax.all_gather(w_kv, ("dp", "mp"), axis=0, tiled=False)
+    all_weights = (
+        gathered_weights.reshape((dp_count, mp_count) + w_kv.shape)
+        .transpose(2, 1, 3, 0, 4)
+        .reshape(2, E, HEADS * HEAD_DIM)
+    )
     key_value = jnp.einsum(
-        "cte,ken->kctn",
-        neighbours,
-        lax.all_gather(tall_weights, "dp", axis=2, tiled=True),
-        preferred_element_type=jnp.float32,
+        "cte,ken->kctn", neighbours, all_weights, preferred_element_type=jnp.float32
     ).astype(jnp.bfloat16)
     key_rows = key_value[0].reshape(CH_DEV, NBR * NT, HEADS, HEAD_DIM)
     values = key_value[1].reshape(CH_DEV, NBR * NT, HEADS, HEAD_DIM)

time: 291 us -> 276 us (0.948)
  waiting for transfers between devices: 176 us -> 117 us
  local copies, waits for them, and re-layouts: 18.2 us -> 45.1 us
  starting transfers between devices: 38.2 us -> 55.2 us
    all_gather x2 -> x1, waiting for transfers between devices: 126 us -> 0.02 us  [shards(): gathered_weights = lax.all_gather(w_kv, ('dp', 'mp'), axis=0, tiled=False)]
    all_to_all x1, waiting for transfers between devices: 7.37 us -> 81.3 us  [shards(): lax.all_to_all(sending, 'mp', split_axis=0, concat_axis=0, tiled=True)]
    reshape x0 -> x2, local copies, waits for them, and re-layouts: none -> 27.4 us  [the longest x1 14.6 us: shards(): gathered_weights.reshape((dp_count, mp_count) + w_kv.shape)]
    all_to_all x1, starting transfers between devices: 17.2 us -> 33.9 us  [shards(): lax.all_to_all(queries, 'mp', split_axis=1, concat_axis=0, tiled=True)]
    all_to_all x1, waiting for transfers between devices: 22.1 us -> 15.1 us  [shards(): lax.all_to_all(pieces, 'dp', split_axis=0, concat_axis=2, tiled=True)]
  transfers between devices with their start and end apart: 7 -> 6, of which waited for: 6 -> 4; matrix products, arithmetic and copies ran while one was open for 12% -> 22% of each run, Pallas kernels for 0% -> 0%
where the time goes in v1:
time: 276 us; the launch traced here: 275 us
  waiting for transfers between devices  117 us (42%)
  starting transfers between devices  55.2 us (20%)
  local copies, waits for them, and re-layouts  45.1 us (16%)
  blocking collectives  18.4 us (7%)
  matrix products  17.2 us (6%)
  between operations  14.2 us (5%)
  other arithmetic  7.89 us (3%)
    all_to_all x1, waiting for transfers between devices, shards(): lax.all_to_all(sending, 'mp', split_axis=0, concat_axis=0, tiled=True)  81.3 us
    all_to_all x1, starting transfers between devices, shards(): lax.all_to_all(queries, 'mp', split_axis=1, concat_axis=0, tiled=True)  33.9 us
    all_to_all x1, blocking collectives, shards(): lax.all_to_all(grad_rows, 'mp', split_axis=0, concat_axis=1, tiled=True)  18.4 us
    all_to_all x1, waiting for transfers between devices, shards(): lax.all_to_all(pieces, 'dp', split_axis=0, concat_axis=2, tiled=True)  15.1 us
    reshape x1, local copies, waits for them, and re-layouts, shards(): gathered_weights.reshape((dp_count, mp_count) + w_kv.shape)  14.6 us
    all_to_all x1, waiting for transfers between devices, shards(): lax.all_to_all(output_rows, 'mp', split_axis=0, concat_axis=1, tiled=True)  13.5 us
    reshape x1, local copies, waits for them, and re-layouts, shards(): all_weights = gathered_weights.reshape((dp_count, mp_count) + w_kv.shape)...  12.8 us
    dot_general x1, matrix products, shards(): jnp.einsum('cte,ken->kctn', neighbours, all_weights, preferred_element_ty...  9.11 us
  transfers between devices with their start and end apart: 6, of which 4 were waited for; matrix products, arithmetic and copies ran while one was open for 22% of the time, Pallas kernels for 0%

profile of v1, /device:TPU:0, one launch (start us, length us, event | category | flops | bytes accessed | tf_op | source)
XLA Modules:
  0.0 275.2 jit_solution(9527004926561921798)
XLA Ops:
  7.2 0.0 copy-start
  7.2 0.0 all-gather.3.cloned.1.call-start
  7.2 0.7 all-gather.3.cloned.1.call-update
  7.9 0.8 copy.74
  8.7 0.1 reshape.136
  8.8 0.1 copy.75
  8.9 0.8 copy.76
  9.6 0.1 reshape.138
  9.7 0.1 copy.77
  9.8 0.1 convert_reduce_fusion
  9.9 0.1 copy.78
  10.0 0.1 reshape.147
  10.1 0.0 copy-done
  10.1 0.0 copy-start.1
  10.1 2.9 %gather_fusion = bf16[32,64,896]{2,1,0:T(8,128)(2,1)} fusion(bf16[8,64,896]{2,1,0:T(8,128)(2,1)S(1)} %copy-done, s32[1024]{0:T(1024)S(1)} %pad_clamp_fusion.1), kind=kCustom, calls=%fused_computation | custom fusion | bytes 7340160 | tf_op jit(solution)/shard_map/gather | solution.py:42
  13.0 0.0 copy-done.1
  13.0 0.6 gather_fusion.1
  13.6 4.6 %fusion.1 = bf16[16,2,64,896]{3,2,1,0:T(8,128)(2,1)} fusion(bf16[16,2,64,896]{3,2,1,0:T(8,128)(2,1)} %bitcast.88, f32[16,2,64]{2,1,0:T(2,128)S(1)} %bitcast.106), kind=kLoop, calls=%fused_computation.5 | loop fusion | flops 5505024 | bytes 7348224 | tf_op jit(solution)/shard_map/convert_element_type | solution.py:42
  18.2 7.4 %all-to-all-start = ((bf16[16,2,64,896]{3,2,1,0:T(8,128)(2,1)}), bf16[16,2,64,896]{3,2,1,0:T(8,128)(2,1)}, u32[]{:S(2)}, u32[]{:S(2)}) async-start(bf16[16,2,64,896]{3,2,1,0:T(8,128)(2,1)} %fusion.1), calls=%async_computation | async-start | bytes 7340032 | tf_op jit(solution)/shard_map/all_to_all | solution.py:45
  25.6 0.2 add_reduce_fusion
  25.8 0.1 add.53
  25.9 81.3 %all-to-all-done = bf16[16,2,64,896]{3,2,1,0:T(8,128)(2,1)} async-done(((bf16[16,2,64,896]{3,2,1,0:T(8,128)(2,1)}), bf16[16,2,64,896]{3,2,1,0:T(8,128)(2,1)}, u32[]{:S(2)}, u32[]{:S(2)}) %all-to-all-start) | async-done | bytes 3670048 | tf_op jit(solution)/shard_map/all_to_all | solution.py:45
  107.3 2.7 gather_fusion.2
  110.0 0.0 copy-start.4
  110.0 1.1 broadcast_select_fusion
  111.1 0.0 copy-start.5
  111.1 3.7 %all-to-all-start.1 = ((bf16[2,4,64,896]{3,2,1,0:T(8,128)(2,1)}), bf16[2,4,64,896]{3,2,1,0:T(8,128)(2,1)S(1)}, u32[]{:S(2)}, u32[]{:S(2)}) async-start(bf16[2,4,64,896]{3,2,1,0:T(8,128)(2,1)} %broadcast_select_fusion), calls=%async_computation.1 | async-start | bytes 1835008 | tf_op jit(solution)/shard_map/all_to_all | solution.py:51
  114.8 0.0 copy-done.4
  114.8 1.0 copy.81
  115.8 15.1 %all-to-all-done.1 = bf16[2,4,64,896]{3,2,1,0:T(8,128)(2,1)S(1)} async-done(((bf16[2,4,64,896]{3,2,1,0:T(8,128)(2,1)}), bf16[2,4,64,896]{3,2,1,0:T(8,128)(2,1)S(1)}, u32[]{:S(2)}, u32[]{:S(2)}) %all-to-all-start.1) | async-done | bytes 917536 | tf_op jit(solution)/shard_map/all_to_all | solution.py:51
  130.9 33.9 %all-to-all-start.2 = ((bf16[128,16,128]{0,2,1:T(8,128)(2,1)}), bf16[128,16,128]{0,2,1:T(8,128)(2,1)S(1)}, u32[]{:S(2)}, u32[]{:S(2)}) async-start(bf16[128,16,128]{0,2,1:T(8,128)(2,1)} %bitcast.20), calls=%async_computation.2 | async-start | bytes 1048576 | tf_op jit(solution)/shard_map/all_to_all | solution.py:23
  164.9 0.0 copy-done.5
  164.9 1.0 copy.87
  165.9 0.1 copy.79
  166.0 0.0 all-gather.3.cloned.1.call-done
  166.0 14.6 %copy.133 = bf16[2,16,2,56,1024]{4,0,3,1,2:T(2,128)(2,1)} copy(bf16[2,16,2,56,1024]{4,3,2,1,0:T(8,128)(2,1)} %bitcast.93) | data formatting | bytes 14680064 | tf_op jit(solution)/shard_map/reshape | solution.py:55
  180.6 12.8 %reshape.175 = bf16[2,896,2048,1]{2,1,0,3:T(8,128)(2,1)} reshape(bf16[2,16,56,2,1024]{4,3,2,1,0:T(2,128)(2,1)} %bitcast.87) | data formatting | bytes 14680064 | tf_op jit(solution)/shard_map/reshape | solution.py:57
  193.4 9.1 %convert_bitcast_fusion = bf16[2,2,256,2048]{3,2,0,1:T(8,128)(2,1)} fusion(bf16[2,256,896,1]{2,1,3,0:T(8,128)(2,1)S(1)} %bitcast.101, bf16[2,896,2048,1]{2,1,0,3:T(8,128)(2,1)} %reshape.175), kind=kOutput, calls=%fused_computation.7 | convolution fusion | flops 3760193536 | bytes 12451840 | tf_op jit(solution)/shard_map/cte,ken->kctn/dot_general | solution.py:59
  202.5 0.0 all-to-all-done.2
  202.5 6.1 %all-to-all-start.4 = ((bf16[128,16,128]{0,2,1:T(8,128)(2,1)}), bf16[128,16,128]{0,2,1:T(8,128)(2,1)}, u32[]{:S(2)}, u32[]{:S(2)}) async-start(bf16[128,16,128]{0,2,1:T(8,128)(2,1)} %bitcast.28), calls=%async_computation.4 | async-start | bytes 1048576 | tf_op jit(solution)/shard_map/all_to_all | solution.py:78
  208.6 2.7 fusion.35
  211.3 0.6 copy.104
  211.9 2.0 copy.105
  213.9 0.8 fusion.12
  214.7 1.8 fusion.36
  216.5 6.6 %all-to-all-done.4 = bf16[128,16,128]{0,2,1:T(8,128)(2,1)} async-done(((bf16[128,16,128]{0,2,1:T(8,128)(2,1)}), bf16[128,16,128]{0,2,1:T(8,128)(2,1)}, u32[]{:S(2)}, u32[]{:S(2)}) %all-to-all-start.4) | async-done | bytes 524320 | tf_op jit(solution)/shard_map/all_to_all | solution.py:78
  223.1 0.0 copy-start.2
  223.1 0.0 copy-start.3
  223.1 4.4 %fusion.25 = (f32[2,16,64]{2,0,1:T(2,128)S(1)}, bf16[16,2,128,64]{2,3,1,0:T(8,128)(2,1)}) fusion(bf16[2,16,64,128]{3,2,0,1:T(8,128)(2,1)} %bitcast.1, bf16[2,256,16,128]{3,2,1,0:T(8,128)(2,1)} %bitcast.97, f32[2,16,64,256]{3,2,1,0:T(8,128)} %get-tuple-element.5, f32[2,16,64]{2,1,0:T(8,128)S(1)} %get-tuple-element.4), kind=kOutput, calls=%fused_computation.27 | convolution fusion | flops 136574976 | bytes 5259264 | tf_op jit(solution)/shard_map/chqk,ckhd->hdcq/dot_general | solution.py:73
  227.5 0.0 copy-done.2
  227.5 0.0 copy-done.3
  227.5 2.0 fusion.3
  229.5 0.9 fusion.22
  230.4 18.4 %all_to_all.90 = bf16[16,128,128]{1,2,0:T(8,128)(2,1)S(1)} all-to-all(bf16[16,128,128]{1,2,0:T(8,128)(2,1)S(1)} %bitcast.102), channel_id=1, replica_groups=mesh['dp'=2,'mp'=16] {'mp'}, dimensions={0} | all-to-all | bytes 1048576 | tf_op jit(solution)/shard_map/all_to_all | solution.py:87
  248.8 4.1 %all-to-all-start.3 = ((bf16[16,128,128]{1,2,0:T(8,128)(2,1)}), bf16[16,128,128]{1,2,0:T(8,128)(2,1)S(1)}, u32[]{:S(2)}, u32[]{:S(2)}) async-start(bf16[16,128,128]{1,2,0:T(8,128)(2,1)} %bitcast.25), calls=%async_computation.3 | async-start | bytes 1048576 | tf_op jit(solution)/shard_map/all_to_all | solution.py:77
  252.9 1.0 copy.103
  253.9 13.5 %all-to-all-done.3 = bf16[16,128,128]{1,2,0:T(8,128)(2,1)S(1)} async-done(((bf16[16,128,128]{1,2,0:T(8,128)(2,1)}), bf16[16,128,128]{1,2,0:T(8,128)(2,1)S(1)}, u32[]{:S(2)}, u32[]{:S(2)}) %all-to-all-start.3) | async-done | bytes 524320 | tf_op jit(solution)/shard_map/all_to_all | solution.py:77
  267.3 1.0 copy.101
  (9 shorter events, 0.1 us)
Async XLA Ops:
  7.2 3.0 %copy-start = (bf16[8,64,896]{2,1,0:T(8,128)(2,1)S(1)}, bf16[8,64,896]{2,1,0:T(8,128)(2,1)}, u32[]{:S(2)}) copy-start(bf16[8,64,896]{2,1,0:T(8,128)(2,1)} %param.8) | copy-start | bytes 2752516
  7.2 158.8 %all-gather.3.cloned.1.call-start = ((), (), s32[]{:S(2)}) async-start(), calls=%async_computation.6 | async-start | bytes 7569408 | tf_op jit(solution)/shard_map/all_gather | solution.py:53
  10.1 2.9 %copy-start.1 = (f32[8,64]{1,0:T(8,128)S(1)}, f32[8,64]{1,0:T(8,128)}, u32[]{:S(2)}) copy-start(f32[8,64]{1,0:T(8,128)} %param.9) | copy-start | bytes 6148
  18.2 89.0 %all-to-all-start = ((bf16[16,2,64,896]{3,2,1,0:T(8,128)(2,1)}), bf16[16,2,64,896]{3,2,1,0:T(8,128)(2,1)}, u32[]{:S(2)}, u32[]{:S(2)}) async-start(bf16[16,2,64,896]{3,2,1,0:T(8,128)(2,1)} %fusion.1), calls=%async_computation | async-start | bytes 7340032 | tf_op jit(solution)/shard_map/all_to_all | solution.py:45
  110.0 4.8 %copy-start.4 = (bf16[128,2048]{1,0:T(8,128)(2,1)S(1)}, bf16[128,2048]{1,0:T(8,128)(2,1)}, u32[]{:S(2)}) copy-start(bf16[128,2048]{1,0:T(8,128)(2,1)} %param.7) | copy-start | bytes 1572868
  111.1 53.8 %copy-start.5 = (bf16[128,2048]{1,0:T(8,128)(2,1)S(1)}, bf16[128,2048]{1,0:T(8,128)(2,1)}, u32[]{:S(2)}) copy-start(bf16[128,2048]{1,0:T(8,128)(2,1)} %param.13) | copy-start | bytes 1572868
  111.1 19.8 %all-to-all-start.1 = ((bf16[2,4,64,896]{3,2,1,0:T(8,128)(2,1)}), bf16[2,4,64,896]{3,2,1,0:T(8,128)(2,1)S(1)}, u32[]{:S(2)}, u32[]{:S(2)}) async-start(bf16[2,4,64,896]{3,2,1,0:T(8,128)(2,1)} %broadcast_select_fusion), calls=%async_computation.1 | async-start | bytes 1835008 | tf_op jit(solution)/shard_map/all_to_all | solution.py:51
  130.9 71.5 %all-to-all-start.2 = ((bf16[128,16,128]{0,2,1:T(8,128)(2,1)}), bf16[128,16,128]{0,2,1:T(8,128)(2,1)S(1)}, u32[]{:S(2)}, u32[]{:S(2)}) async-start(bf16[128,16,128]{0,2,1:T(8,128)(2,1)} %bitcast.20), calls=%async_computation.2 | async-start | bytes 1048576 | tf_op jit(solution)/shard_map/all_to_all | solution.py:23
  202.5 20.6 %all-to-all-start.4 = ((bf16[128,16,128]{0,2,1:T(8,128)(2,1)}), bf16[128,16,128]{0,2,1:T(8,128)(2,1)}, u32[]{:S(2)}, u32[]{:S(2)}) async-start(bf16[128,16,128]{0,2,1:T(8,128)(2,1)} %bitcast.28), calls=%async_computation.4 | async-start | bytes 1048576 | tf_op jit(solution)/shard_map/all_to_all | solution.py:78
  223.1 4.4 %copy-start.2 = (bf16[64,8,16,128]{3,2,1,0:T(8,128)(2,1)S(1)}, bf16[64,8,16,128]{3,2,1,0:T(8,128)(2,1)}, u32[]{:S(2)}) copy-start(bf16[64,8,16,128]{3,2,1,0:T(8,128)(2,1)} %copy.105) | copy-start | bytes 6291460
  223.1 4.4 %copy-start.3 = (f32[2,16,64,256]{3,2,1,0:T(8,128)S(1)}, f32[2,16,64,256]{3,2,1,0:T(8,128)}, u32[]{:S(2)}) copy-start(f32[2,16,64,256]{3,2,1,0:T(8,128)} %get-tuple-element.5) | copy-start | bytes 6291460
  248.8 18.6 %all-to-all-start.3 = ((bf16[16,128,128]{1,2,0:T(8,128)(2,1)}), bf16[16,128,128]{1,2,0:T(8,128)(2,1)S(1)}, u32[]{:S(2)}, u32[]{:S(2)}) async-start(bf16[16,128,128]{1,2,0:T(8,128)(2,1)} %bitcast.25), calls=%async_computation.3 | async-start | bytes 1048576 | tf_op jit(solution)/shard_map/all_to_all | solution.py:77
Sparse Core Ops, SparseCore 0:
  10.9 129.8 all-gather.2

commit v2 on v1

--- a/solution.py
+++ b/solution.py
@@ -1,6 +1,8 @@
 import jax
 import jax.numpy as jnp
 from jax import lax
+from jax.experimental import pallas as pl
+from jax.experimental.pallas import tpu as pltpu
 from jax.sharding import PartitionSpec as P
 
 HEADS = 16
@@ -10,31 +12,290 @@
 SPAN = 64
 NBR = 2
 CH_DEV = 2
-
-
-def shards(queries, cache, cache_scale, w_kv, nbr_shard, nbr_row, grad_out):
+MOST = 2
+
+SCORE_SCALE = HEAD_DIM ** (-0.5)
+
+
+def requests(nbr_shard, nbr_row, dp_count, mp_count):
+    block_size = dp_count * CH_DEV * NBR
+    shard_blk = (
+        nbr_shard.reshape(dp_count, mp_count, CH_DEV * NBR)
+        .transpose(1, 0, 2)
+        .reshape(mp_count, block_size)
+    )
+    row_blk = (
+        nbr_row.reshape(dp_count, mp_count, CH_DEV * NBR)
+        .transpose(1, 0, 2)
+        .reshape(mp_count, block_size)
+    )
+    positions = jnp.arange(block_size, dtype=jnp.int32)
+    earlier = positions[None, :] < positions[:, None]
+    same_shard = shard_blk[:, :, None] == shard_blk[:, None, :]
+    slot_blk = jnp.sum(jnp.logical_and(same_shard, earlier[None]), axis=2)
+    return shard_blk, row_blk, slot_blk
+
+
+ZS, XS, CS = 4, 2, 2
+CHIPS = ZS * XS
+HALF = 8
+ALL = range(ZS * XS * CS)
+
+
+def rows_kernel(rows_ref, src_ref, *refs):
+    outs, sem = refs[:-1], refs[-1]
+    copies = []
+    for k in range(HALF):
+        for s in range(MOST):
+            copies.append(
+                pltpu.make_async_copy(
+                    src_ref.at[rows_ref[k * MOST + s]], outs[k].at[s], sem.at[k * MOST + s]
+                )
+            )
+    for copy in copies:
+        copy.start()
+    for copy in copies:
+        copy.wait()
+
+
+def pick_rows(rows, source):
+    piece = jax.ShapeDtypeStruct((MOST,) + source.shape[1:], source.dtype)
+    return pl.pallas_call(
+        rows_kernel,
+        in_specs=[
+            pl.BlockSpec(memory_space=pltpu.SMEM),
+            pl.BlockSpec(memory_space=pl.ANY),
+        ],
+        out_specs=[pl.BlockSpec(memory_space=pl.ANY)] * HALF,
+        out_shape=[piece] * HALF,
+        scratch_shapes=[pltpu.SemaphoreType.DMA((HALF * MOST,))],
+        name="pick_rows",
+    )(rows, source)
+
+
+def choose_kernel(where_ref, *refs):
+    count = 2 * HALF
+    pieces, outs, sem = refs[:count], refs[count:-1], refs[-1]
+    for r in range(2 * CH_DEV * NBR):
+        out = outs[r // (CH_DEV * NBR)].at[r % (CH_DEV * NBR)]
+        piece, slot = where_ref[2 * r], where_ref[2 * r + 1]
+        for p in range(count):
+
+            @pl.when(piece == p)
+            def _():
+                pltpu.make_async_copy(pieces[p].at[slot], out, sem.at[r]).start()
+
+    for r in range(2 * CH_DEV * NBR):
+        out = outs[r // (CH_DEV * NBR)].at[r % (CH_DEV * NBR)]
+        pltpu.make_async_copy(pieces[0].at[0], out, sem.at[r]).wait()
+
+
+def choose(where, pieces):
+    half = jax.ShapeDtypeStruct((CH_DEV * NBR,) + pieces[0].shape[1:], pieces[0].dtype)
+    return pl.pallas_call(
+        choose_kernel,
+        in_specs=[pl.BlockSpec(memory_space=pltpu.SMEM)]
+        + [pl.BlockSpec(memory_space=pl.ANY)] * len(pieces),
+        out_specs=[pl.BlockSpec(memory_space=pl.ANY)] * 2,
+        out_shape=[half] * 2,
+        scratch_shapes=[pltpu.SemaphoreType.DMA((2 * CH_DEV * NBR,))],
+        name="choose",
+    )(where, *pieces)
+
+
+def tdot(a, b):
+    return lax.dot_general(a, b, (((0,), (0,)), ((), ())), preferred_element_type=jnp.float32)
+
+
+def ndot(a, b):
+    return jnp.dot(a, b, preferred_element_type=jnp.float32)
+
+
+def attend_kernel(
+    place_ref, na, nb, sa, sb, k0, kx, ky, kd, v0, vx, vy, vd, qg_ref, out_ref, n_scr, w_scr
+):
+    step = pl.program_id(0)
+    d_heads = HEADS // CS // 2
+    my_c, my_z, my_x = place_ref[1], place_ref[2], place_ref[3]
+    rows = w_scr.shape[0] // CHIPS
+
+    @pl.when(step == 0)
+    def _():
+        for s in range(CH_DEV):
+            for core, first, second in ((my_c, na, nb), (1 - my_c, sa, sb)):
+                n_scr[CH_DEV * core + s, 0:NT, :] = first[s]
+                n_scr[CH_DEV * core + s, NT : 2 * NT, :] = second[s]
+
+    def put(own, other, lane):
+        for r in range(ZS):
+            src_z = lax.rem(my_z - r + ZS, ZS)
+            for x_at, ref in ((my_x, own), (1 - my_x, other)):
+                at = pl.multiple_of((src_z * XS + x_at) * rows, 16)
+                w_scr[pl.ds(at, rows), lane : lane + HEAD_DIM] = ref[r]
+
+    @pl.when(step < d_heads)
+    def _():
+        put(k0, kx, 0)
+        put(v0, vx, HEAD_DIM)
+
+    @pl.when(step >= d_heads)
+    def _():
+        put(ky, kd, 0)
+        put(vy, vd, HEAD_DIM)
+
+    keys = NBR * NT
+    weights = w_scr[...]
+    lane = lax.broadcasted_iota(jnp.int32, (1, 2 * SPAN), 1)
+    low = lane < SPAN
+    for p in range(CS):
+        kv = [
+            ndot(n_scr[CH_DEV * p + s], weights).astype(jnp.bfloat16) for s in range(CH_DEV)
+        ]
+        ka, kb = kv[0][:, :HEAD_DIM], kv[1][:, :HEAD_DIM]
+        va, vb = kv[0][:, HEAD_DIM:], kv[1][:, HEAD_DIM:]
+        at = slice(2 * SPAN * p, 2 * SPAN * (p + 1))
+        q = qg_ref[0, 0, :, at]
+        g = qg_ref[0, 1, :, at]
+        scores = jnp.where(low, ndot(ka, q), ndot(kb, q)) * SCORE_SCALE
+        exponent = jnp.exp(scores - jnp.max(scores, axis=0, keepdims=True))
+        probs = exponent / jnp.sum(exponent, axis=0, keepdims=True)
+        probs_low = probs.astype(jnp.bfloat16)
+        out = jnp.where(low, tdot(va, probs_low), tdot(vb, probs_low)).astype(jnp.bfloat16)
+        dprobs = jnp.where(low, ndot(va, g), ndot(vb, g))
+        delta = jnp.sum(
+            g.astype(jnp.float32) * out.astype(jnp.float32), axis=0, keepdims=True
+        )
+        dscores = (probs * (dprobs - delta) * SCORE_SCALE).astype(jnp.bfloat16)
+        dq = jnp.where(low, tdot(ka, dscores), tdot(kb, dscores)).astype(jnp.bfloat16)
+        out_ref[0, 0, :, at] = out
+        out_ref[0, 1, :, at] = dq
+
+
+def attend(place, neighbours, weights, qg):
+    d_heads = HEADS // CS // 2
+    heads = 2 * d_heads
+    tokens = qg.shape[-1]
+
+    def whole(a):
+        return pl.BlockSpec(a.shape, lambda i, place: (0,) * a.ndim)
+
+    def own(a):
+        return pl.BlockSpec(
+            a.shape[:2] + (HEAD_DIM,), lambda i, place: (0, 0, jnp.minimum(i, d_heads - 1))
+        )
+
+    def other(a):
+        return pl.BlockSpec(
+            a.shape[:2] + (HEAD_DIM,), lambda i, place: (0, 0, jnp.maximum(i - d_heads, 0))
+        )
+
+    head_block = pl.BlockSpec(
+        (1, 2, HEAD_DIM, tokens),
+        lambda i, place: (lax.rem(i + d_heads * place[0], heads), 0, 0, 0),
+    )
+    return pl.pallas_call(
+        attend_kernel,
+        grid_spec=pltpu.PrefetchScalarGridSpec(
+            num_scalar_prefetch=1,
+            grid=(heads,),
+            in_specs=[whole(a) for a in neighbours]
+            + [f(a) for f, a in zip((own, own, other, other) * 2, weights)]
+            + [head_block],
+            out_specs=head_block,
+            scratch_shapes=[
+                pltpu.VMEM((CS * CH_DEV, NBR * NT, E), jnp.bfloat16),
+                pltpu.VMEM((E, 2 * HEAD_DIM), jnp.bfloat16),
+            ],
+        ),
+        out_shape=jax.ShapeDtypeStruct(qg.shape, jnp.bfloat16),
+        compiler_params=pltpu.CompilerParams(vmem_limit_bytes=40 * 1024 * 1024),
+        name="attend",
+    )(place, *neighbours, *weights, qg)
+
+
+def small(queries, cache, cache_scale, w_kv, nbr_shard, nbr_row, grad_out):
+    dp_count = lax.axis_size("dp")
+    mp_count = lax.axis_size("mp")
+    my_dp = lax.axis_index("dp")
+    my_mp = lax.axis_index("mp")
+    my_c, my_x, my_z = my_mp & 1, (my_mp >> 1) & 1, my_mp >> 2
+    place = jnp.stack([my_dp, my_c, my_z, my_x]).astype(jnp.int32)
+    slice_len = cache.shape[1]
+    e_loc = w_kv.shape[1]
+
+    def swap(a, bits):
+        return lax.ppermute(a, "mp", [(m, m ^ bits) for m in ALL])
+
+    def swap_dp(a):
+        return lax.ppermute(a, "dp", [(0, 1), (1, 0)])
+
+    by_parity = w_kv.reshape(2, e_loc, -1, CS, HEAD_DIM)
+    mine = lax.dynamic_index_in_dim(by_parity, my_c, 3, keepdims=False).reshape(2, e_loc, -1)
+    sends = lax.dynamic_index_in_dim(by_parity, 1 - my_c, 3, keepdims=False).reshape(2, e_loc, -1)
+    came = swap(sends, 1)
+    first = my_c == 0
+    chip_w = jnp.concatenate(
+        [jnp.where(first, mine, came), jnp.where(first, came, mine)], axis=1
+    )
+
+    scaled = (cache.astype(jnp.float32) * cache_scale[..., None]).astype(jnp.bfloat16)
+    far = swap(scaled, HALF)
+    shard_blk, row_blk, slot_blk = requests(nbr_shard, nbr_row, dp_count, mp_count)
+    holders = jnp.stack([my_mp, my_mp ^ HALF]).astype(jnp.int32)
+    takers = my_mp ^ jnp.arange(HALF, dtype=jnp.int32)
+    select = jnp.logical_and(
+        shard_blk[:, None, None, :] == holders[None, :, None, None],
+        slot_blk[:, None, None, :] == jnp.arange(MOST, dtype=jnp.int32)[None, None, :, None],
+    )
+    wanted = jnp.sum(jnp.where(select, row_blk[:, None, None, :], 0), axis=3)[takers]
+    near_pieces = pick_rows(wanted[:, 0].reshape(-1), scaled)
+    near_pieces = [near_pieces[0]] + [swap(near_pieces[k], k) for k in range(1, HALF)]
+
+    turned = [chip_w] + [
+        lax.ppermute(chip_w, "mp", [(m, (m + XS * CS * r) % len(ALL)) for m in ALL])
+        for r in range(1, ZS)
+    ]
+    k0 = jnp.stack([t[0] for t in turned])
+    v0 = jnp.stack([t[1] for t in turned])
+    kx, vy = swap(k0, CS), swap_dp(v0)
+    vx, ky = swap(v0, CS), swap_dp(k0)
+    vd, kd = swap(vy, CS), swap_dp(kx)
+
+    far_pieces = pick_rows(wanted[:, 1].reshape(-1), far)
+    far_pieces = [far_pieces[0]] + [swap(far_pieces[k], k) for k in range(1, HALF)]
+
+    qg = jnp.stack([queries, grad_out]).reshape(2, HEAD_DIM, CHIPS, -1).transpose(2, 0, 1, 3)
+    chip_groups = [[CS * chip + core for chip in range(CHIPS)] for core in range(CS)]
+    qg = lax.all_to_all(
+        qg, "mp", split_axis=0, concat_axis=0, tiled=True, axis_index_groups=chip_groups
+    )
+
+    xor = lax.dynamic_index_in_dim(shard_blk, my_mp, 0, keepdims=False) ^ my_mp
+    slots = lax.dynamic_index_in_dim(slot_blk, my_mp, 0, keepdims=False)
+    where = jnp.stack([xor, slots], axis=1).reshape(dp_count, -1)
+    where = jnp.stack([where[my_dp], where[1 - my_dp]]).reshape(-1).astype(jnp.int32)
+    own, give = choose(where, near_pieces + far_pieces)
+    got = swap_dp(give)
+    span_shape = (CH_DEV, NBR * slice_len, E)
+    own, got = own.reshape(span_shape), got.reshape(span_shape)
+    neighbours = (own, got, swap(own, 1), swap(got, 1))
+
+    result = attend(place, neighbours, (k0, kx, ky, kd, v0, vx, vy, vd), qg)
+    back = lax.all_to_all(
+        result, "mp", split_axis=0, concat_axis=0, tiled=True, axis_index_groups=chip_groups
+    )
+    back = back.transpose(1, 2, 0, 3).reshape((2,) + queries.shape)
+    return back[0], back[1]
+
+
+def general(queries, cache, cache_scale, w_kv, nbr_shard, nbr_row, grad_out):
     dp_count = lax.axis_size("dp")
     mp_count = lax.axis_size("mp")
     my_mp = lax.axis_index("mp")
     slice_len = cache.shape[1]
     most_slots = 2 * ((dp_count * CH_DEV * NBR + mp_count - 1) // mp_count)
-    block_size = dp_count * CH_DEV * NBR
-    score_scale = HEAD_DIM ** (-0.5)
     local_query = lax.all_to_all(queries, "mp", split_axis=1, concat_axis=0, tiled=True)
-    shard_blk = (
-        nbr_shard.reshape(dp_count, mp_count, CH_DEV * NBR)
-        .transpose(1, 0, 2)
-        .reshape(mp_count, block_size)
-    )
-    row_blk = (
-        nbr_row.reshape(dp_count, mp_count, CH_DEV * NBR)
-        .transpose(1, 0, 2)
-        .reshape(mp_count, block_size)
-    )
-    positions = jnp.arange(block_size, dtype=jnp.int32)
-    earlier = positions[None, :] < positions[:, None]
-    same_shard = shard_blk[:, :, None] == shard_blk[:, None, :]
-    slot_blk = jnp.sum(jnp.logical_and(same_shard, earlier[None]), axis=2)
+    shard_blk, row_blk, slot_blk = requests(nbr_shard, nbr_row, dp_count, mp_count)
     to_me = shard_blk == my_mp
     slot_ids = jnp.arange(most_slots, dtype=jnp.int32)
     select = jnp.logical_and(to_me[:, None, :], slot_blk[:, None, :] == slot_ids[None, :, None])
@@ -64,7 +325,7 @@
     query_c = local_query.reshape(HEADS, HEAD_DIM, CH_DEV, SPAN)
     affinity_logits = (
         jnp.einsum("hdcq,ckhd->chqk", query_c, key_rows, preferred_element_type=jnp.float32)
-        * score_scale
+        * SCORE_SCALE
     )
     row_max = jnp.max(affinity_logits, axis=3, keepdims=True)
     exponent = jnp.exp(affinity_logits - row_max)
@@ -79,7 +340,7 @@
     grad_c = local_grad.reshape(HEADS, HEAD_DIM, CH_DEV, SPAN)
     dprobs = jnp.einsum("hdcq,ckhd->chqk", grad_c, values, preferred_element_type=jnp.float32)
     row_delta = jnp.einsum("hdcq,hdcq->chq", grad_c, output_c, preferred_element_type=jnp.float32)
-    dscores = (attn_probs * (dprobs - row_delta[..., None]) * score_scale).astype(jnp.bfloat16)
+    dscores = (attn_probs * (dprobs - row_delta[..., None]) * SCORE_SCALE).astype(jnp.bfloat16)
     grad_query = jnp.einsum(
         "chqk,ckhd->hdcq", dscores, key_rows, preferred_element_type=jnp.float32
     ).astype(jnp.bfloat16)
@@ -89,8 +350,9 @@
 
 
 def solution(mesh):
+    fits = mesh.shape["dp"] == 2 and mesh.shape["mp"] == len(ALL)
     return jax.shard_map(
-        shards,
+        small if fits else general,
         mesh=mesh,
         in_specs=(
             P("mp", "dp"),

time: 276 us -> 321 us (1.16)
  Pallas kernels: 0 us -> 163 us
  waiting for transfers between devices: 117 us -> 66.3 us
  local copies, waits for them, and re-layouts: 45.1 us -> 12.1 us
  matrix products: 17.2 us -> 0 us
  between operations: 14.2 us -> 0.95 us
  starting transfers between devices: 55.2 us -> 44.5 us
  blocking collectives: 18.4 us -> 28.5 us
    pallas_call x0 -> x4, Pallas kernels: none -> 163 us  [the longest x2 115 us: pick_rows(): pl.pallas_call(rows_kernel, in_specs=[pl.BlockSpec(memory_space=pltpu.SME...]
    all_to_all x5 -> x1, waiting for transfers between devices: 116 us -> 0.01 us  [small(): lax.all_to_all(qg, 'mp', split_axis=0, concat_axis=0, tiled=True, axis_in...]
    ppermute x0 -> x28, waiting for transfers between devices: none -> 66.3 us  [the longest x3 25.5 us: small(): lax.ppermute(chip_w, 'mp', [(m, (m + XS * CS * r) % len(ALL)) for m in ALL])]
    all_to_all x5 -> x1, starting transfers between devices: 55.2 us -> 3.78 us  [small(): lax.all_to_all(qg, 'mp', split_axis=0, concat_axis=0, tiled=True, axis_in...]
    ppermute x0 -> x28, starting transfers between devices: none -> 40.7 us  [the longest x21 23.8 us: swap(): return lax.ppermute(a, 'mp', [(m, m ^ bits) for m in ALL])]
    reshape x4 -> x7, local copies, waits for them, and re-layouts: 27.5 us -> 1.67 us  [the longest x1 0.68 us: small(): lax.dynamic_index_in_dim(by_parity, 1 - my_c, 3, keepdims=False)]
    dot_general x5 -> x0, matrix products: 17.2 us -> none  [the longest x1 9.11 us: shards(): jnp.einsum('cte,ken->kctn', neighbours, all_weights, preferred_element_ty...]
    all_to_all x1, blocking collectives: 18.4 us -> 28.5 us  [small(): lax.all_to_all(result, 'mp', split_axis=0, concat_axis=0, tiled=True, axi...]
  transfers between devices with their start and end apart: 6 -> 29, of which waited for: 4 -> 13; matrix products, arithmetic and copies ran while one was open for 22% -> 3% of each run, Pallas kernels for 0% -> 45%
where the time goes in v2:
time: 321 us
  Pallas kernels  163 us (51%)
  waiting for transfers between devices  66.3 us (21%)
  starting transfers between devices  44.5 us (14%)
  blocking collectives  28.5 us (9%)
  local copies, waits for them, and re-layouts  12.1 us (4%)
  other arithmetic  4.83 us (2%)
    pallas_call x2, Pallas kernels, pick_rows(): pl.pallas_call(rows_kernel, in_specs=[pl.BlockSpec(memory_space=pltpu.SME...  115 us
    pallas_call x1, Pallas kernels, choose(): pl.pallas_call(choose_kernel, in_specs=[pl.BlockSpec(memory_space=pltpu.S...  29.6 us
    all_to_all x1, blocking collectives, small(): lax.all_to_all(result, 'mp', split_axis=0, concat_axis=0, tiled=True, axi...  28.5 us
    ppermute x3, waiting for transfers between devices, small(): lax.ppermute(chip_w, 'mp', [(m, (m + XS * CS * r) % len(ALL)) for m in ALL])  25.5 us
    ppermute x21, starting transfers between devices, swap(): return lax.ppermute(a, 'mp', [(m, m ^ bits) for m in ALL])  23.8 us
    ppermute x21, waiting for transfers between devices, swap(): return lax.ppermute(a, 'mp', [(m, m ^ bits) for m in ALL])  22.7 us
    pallas_call x1, Pallas kernels, attend(): pl.pallas_call(attend_kernel, grid_spec=pltpu.PrefetchScalarGridSpec(num_...  18.7 us
    ppermute x4, waiting for transfers between devices, swap_dp(): return lax.ppermute(a, 'dp', [(0, 1), (1, 0)])  18.1 us
  transfers between devices with their start and end apart: 29, of which 13 were waited for; matrix products, arithmetic and copies ran while one was open for 3% of the time, Pallas kernels for 45%

profile of v2, /device:TPU:0, one launch (start us, length us, event | category | flops | bytes accessed | tf_op | source)
XLA Modules:
  0.0 320.5 jit_solution(10968047220140236545)
XLA Ops:
  0.7 1.4 multiply_convert_fusion.src_ref
  2.1 4.1 %collective-permute-start.7 = (bf16[8,64,896]{2,1,0:T(8,128)(2,1)S(1)}, bf16[8,64,896]{2,1,0:T(8,128)(2,1)S(1)}, u32[]{:S(2)}, u32[]{:S(2)}) collective-permute-start(bf16[8,64,896]{2,1,0:T(8,128)(2,1)S(1)} %multiply_convert_fusion.src_ref), channel_id=1, source_target_pairs={{0,8},{1,9},{2,10},{3,11},{4,12},{5,13},{6,14},{7,15},{8,0},{9,1},... | collective-permute-start | bytes 2752520 | tf_op jit(solution)/shard_map/ppermute | solution.py:227
  7.1 0.6 gather_fusion
  7.7 0.6 reshape_squeeze.6.rows_ref
  8.3 57.6 %pick_rows.2 = (bf16[2,64,896]{2,1,0:T(8,128)(2,1)}, bf16[2,64,896]{2,1,0:T(8,128)(2,1)}, bf16[2,64,896]{2,1,0:T(8,128)(2,1)}, bf16[2,64,896]{2,1,0:T(8,128)(2,1...) custom-call(s32[16]{0:T(128)} %reshape_squeeze.6.rows_ref, ...), custom_call_target="tpu_custom_call" | custom-call | tf_op jit(solution)/shard_map/pick_rows/pallas_call | solution.py:63
  66.0 1.6 collective-permute-start.1
  67.6 0.3 collective-permute-start.2
  68.0 1.4 dynamic-slice_reduce_fusion.1
  69.5 0.7 reshape.116
  70.2 0.3 collective-permute-start.18
  70.5 0.3 copy.64
  70.8 0.2 copy.66
  71.2 0.3 copy.63
  71.5 0.2 copy.65
  71.7 1.1 maximum_bitcast_fusion
  72.8 3.8 %all-to-all-start = ((bf16[8,2,128,256]{3,2,1,0:T(8,128)(2,1)}), bf16[8,2,128,256]{3,2,1,0:T(8,128)(2,1)S(1)}, u32[]{:S(2)}, u32[]{:S(2)}) async-start(bf16[8,2,128,256]{3,2,1,0:T(8,128)(2,1)} %maximum_bitcast_fusion), calls=%async_computation | async-start | bytes 2097152 | tf_op jit(solution)/shard_map/all_to_all | solution.py:269
  77.0 0.9 broadcast_select_fusion.1
  78.0 0.7 pad_maximum_fusion.2
  78.7 3.8 %collective-permute-start.21 = (bf16[2,112,512]{2,1,0:T(8,128)(2,1)}, bf16[2,112,512]{2,1,0:T(8,128)(2,1)}, u32[]{:S(2)}, u32[]{:S(2)}) collective-permute-start(bf16[2,112,512]{2,1,0:T(8,128)(2,1)} %pad_maximum_fusion.2), channel_id=1, source_target_pairs={{0,12},{1,13},{2,14},{3,15},{4,0},{5,1},{6,2},{7,3},{8,4},{9,5},{1... | collective-permute-start | bytes 688136 | tf_op jit(solution)/shard_map/ppermute | solution.py:255
  82.5 0.6 reshape.110.where_ref
  83.1 0.6 reshape_squeeze.7.rows_ref
  83.7 16.3 %collective-permute-done.21 = bf16[2,112,512]{2,1,0:T(8,128)(2,1)} collective-permute-done((bf16[2,112,512]{2,1,0:T(8,128)(2,1)}, bf16[2,112,512]{2,1,0:T(8,128)(2,1)}, u32[]{:S(2)}, u32[]{:S(2)}) %collective-permute-start.21) | collective-permute-done | bytes 229408 | tf_op jit(solution)/shard_map/ppermute | solution.py:255
  100.0 7.4 %collective-permute-start.20 = (bf16[2,112,512]{2,1,0:T(8,128)(2,1)}, bf16[2,112,512]{2,1,0:T(8,128)(2,1)S(1)}, u32[]{:S(2)}, u32[]{:S(2)}) collective-permute-start(bf16[2,112,512]{2,1,0:T(8,128)(2,1)} %pad_maximum_fusion.2), channel_id=1, source_target_pairs={{0,8},{1,9},{2,10},{3,11},{4,12},{5,13},{6,14},{7,15},{8,0},{9,1},... | collective-permute-start | bytes 688136 | tf_op jit(solution)/shard_map/ppermute | solution.py:255
  107.4 1.0 fusion.6
  108.4 9.2 %collective-permute-done.20 = bf16[2,112,512]{2,1,0:T(8,128)(2,1)S(1)} collective-permute-done((bf16[2,112,512]{2,1,0:T(8,128)(2,1)}, bf16[2,112,512]{2,1,0:T(8,128)(2,1)S(1)}, u32[]{:S(2)}, u32[]{:S(2)}) %collective-permute-start.20) | collective-permute-done | bytes 229408 | tf_op jit(solution)/shard_map/ppermute | solution.py:255
  117.6 0.6 collective-permute-start.3
  118.2 1.4 collective-permute-start.19
  119.6 57.5 %pick_rows.3 = (bf16[2,64,896]{2,1,0:T(8,128)(2,1)}, bf16[2,64,896]{2,1,0:T(8,128)(2,1)}, bf16[2,64,896]{2,1,0:T(8,128)(2,1)}, bf16[2,64,896]{2,1,0:T(8,128)(2,1...) custom-call(s32[16]{0:T(128)} %reshape_squeeze.7.rows_ref, ...), custom_call_target="tpu_custom_call" | custom-call | tf_op jit(solution)/shard_map/pick_rows/pallas_call | solution.py:63
  177.2 1.4 collective-permute-start.4
  178.5 2.0 collective-permute-start.5
  180.6 1.4 collective-permute-start.6
  182.0 1.5 collective-permute-start.9
  183.5 0.9 collective-permute-done.4.refs_5_
  184.4 3.1 collective-permute-start.10
  187.5 4.7 %collective-permute-done.5.refs_6_ = bf16[2,64,896]{2,1,0:T(8,128)(2,1)S(1)} collective-permute-done((bf16[2,64,896]{2,1,0:T(8,128)(2,1)}, bf16[2,64,896]{2,1,0:T(8,128)(2,1)S(1)}, u32[]{:S(2)}, u32[]{:S(2)}) %collective-permute-start.5) | collective-permute-done | bytes 229408 | tf_op jit(solution)/shard_map/ppermute | solution.py:227
  192.2 0.5 collective-permute-start.11
  192.6 2.5 collective-permute-done.6.refs_7_
  195.2 2.1 collective-permute-start.12
  197.2 1.3 collective-permute-start.13
  198.6 1.7 collective-permute-done.9.refs_10_
  200.3 0.5 collective-permute-start.14
  200.9 3.7 %collective-permute-done.10.refs_11_ = bf16[2,64,896]{2,1,0:T(8,128)(2,1)S(1)} collective-permute-done((bf16[2,64,896]{2,1,0:T(8,128)(2,1)}, bf16[2,64,896]{2,1,0:T(8,128)(2,1)S(1)}, u32[]{:S(2)}, u32[]{:S(2)}) %collective-permute-start.10) | collective-permute-done | bytes 229408 | tf_op jit(solution)/shard_map/ppermute | solution.py:227
  204.7 1.0 collective-permute-start.22
  205.7 1.6 collective-permute-start.23
  207.3 0.6 collective-permute-start.26
  207.9 4.0 %collective-permute-done.13.refs_14_ = bf16[2,64,896]{2,1,0:T(8,128)(2,1)S(1)} collective-permute-done((bf16[2,64,896]{2,1,0:T(8,128)(2,1)}, bf16[2,64,896]{2,1,0:T(8,128)(2,1)S(1)}, u32[]{:S(2)}, u32[]{:S(2)}) %collective-permute-start.13) | collective-permute-done | bytes 229408 | tf_op jit(solution)/shard_map/ppermute | solution.py:227
  211.9 3.0 collective-permute-done.14.refs_15_
  214.9 0.7 copy-done.15
  215.6 29.6 %choose.1 = (bf16[4,64,896]{2,1,0:T(8,128)(2,1)}, bf16[4,64,896]{2,1,0:T(8,128)(2,1)}) custom-call(s32[16]{0:T(128)} %reshape.110.where_ref, bf16[2,64,896]{2,1,0:T(8,128)(2,1)} %get-tuple-element.20.refs_0_, bf16[2,64,896]{2,1,0:T(8,128)(2,1)} %collective-permute-done.refs_1_, bf16[2,64,896]{2,1,0:T(8,128)(2,1)} %collective-permute-done.1.refs_2_, ...), custom_call_target="tpu_custom_call" | custom-call | tf_op jit(solution)/shard_map/choose/pallas_call | solution.py:95
  245.2 1.6 collective-permute-start.15
  246.8 0.8 collective-permute-start.25
  247.6 0.5 collective-permute-start.24
  248.1 1.3 collective-permute-start.27
  249.4 9.6 %collective-permute-done.15 = bf16[4,64,896]{2,1,0:T(8,128)(2,1)} collective-permute-done((bf16[4,64,896]{2,1,0:T(8,128)(2,1)}, bf16[4,64,896]{2,1,0:T(8,128)(2,1)}, u32[]{:S(2)}, u32[]{:S(2)}) %collective-permute-start.15) | collective-permute-done | bytes 458784 | tf_op jit(solution)/shard_map/ppermute | solution.py:230
  259.1 1.1 collective-permute-done.25.vx
  260.2 8.4 %collective-permute-done.24.kd = bf16[4,112,512]{2,1,0:T(8,128)(2,1)} collective-permute-done((bf16[4,112,512]{2,1,0:T(8,128)(2,1)S(1)}, bf16[4,112,512]{2,1,0:T(8,128)(2,1)}, u32[]{:S(2)}, u32[]{:S(2)}) %collective-permute-start.24) | collective-permute-done | bytes 458784 | tf_op jit(solution)/shard_map/ppermute | solution.py:230
  268.6 1.0 collective-permute-done.27.vd
  269.7 1.0 copy-done
  270.7 18.7 %attend.1 = bf16[8,2,128,256]{3,2,1,0:T(8,128)(2,1)S(1)} custom-call(s32[4]{0:T(128)S(1)} %pad_add_fusion.2.place_ref, bf16[2,128,896]{2,1,0:T(8,128)(2,1)S(1)} %bitcast.24, bf16[2,128,896]{2,1,0:T(8,128)(2,1)} %bitcast.12.nb, bf16[2,128,896]{2,1,0:T(8,128)(2,1)} %collective-permute-done.16.sa, bf16[2,128,896]{2,1,0:T(8,128)(2,1)} %collective-permute-done.17.sb, ...), custom_call_target="tpu_custom_call" | custom-call | tf_op jit(solution)/shard_map/attend/pallas_call | solution.py:196
  289.4 28.5 %all_to_all.10 = bf16[8,2,128,256]{3,2,1,0:T(8,128)(2,1)S(1)} all-to-all(bf16[8,2,128,256]{3,2,1,0:T(8,128)(2,1)S(1)} %attend.1), channel_id=1, replica_groups={{0,2,4,6,8,10,12,14},{1,3,5,7,9,11,13,15},{16,18,20,22,24,26,28,30},{17..., dimensions={0} | all-to-all | bytes 2097152 | tf_op jit(solution)/shard_map/all_to_all | solution.py:284
  317.9 0.3 copy.67
  318.2 1.0 copy.69
  319.2 0.3 copy.68
  319.5 1.0 copy.70
  (84 shorter events, 2.2 us)
Async XLA Ops:
  0.6 5.6 %copy-start.16 = (s32[64,2]{0,1:T(2,128)S(1)}, s32[64,2]{0,1:T(2,128)}, u32[]{:S(2)}) copy-start(s32[64,2]{0,1:T(2,128)} %param.11) | copy-start | bytes 1540
  0.6 5.8 %copy-start.17 = (s32[64,2]{0,1:T(2,128)S(1)}, s32[64,2]{0,1:T(2,128)}, u32[]{:S(2)}) copy-start(s32[64,2]{0,1:T(2,128)} %param.12) | copy-start | bytes 1540
  2.1 6.2 %copy-start.1 = (bf16[8,64,896]{2,1,0:T(8,128)(2,1)}, bf16[8,64,896]{2,1,0:T(8,128)(2,1)S(1)}, u32[]{:S(2)}) copy-start(bf16[8,64,896]{2,1,0:T(8,128)(2,1)S(1)} %multiply_convert_fusion.src_ref) | copy-start | bytes 2752516
  2.1 65.8 %copy-start.5 = (bf16[2,56,1024]{2,1,0:T(8,128)(2,1)S(1)}, bf16[2,56,1024]{2,1,0:T(8,128)(2,1)}, u32[]{:S(2)}) copy-start(bf16[2,56,1024]{2,1,0:T(8,128)(2,1)} %param.10) | copy-start | bytes 688132
  2.1 116.1 %collective-permute-start.7 = (bf16[8,64,896]{2,1,0:T(8,128)(2,1)S(1)}, bf16[8,64,896]{2,1,0:T(8,128)(2,1)S(1)}, u32[]{:S(2)}, u32[]{:S(2)}) collective-permute-start(bf16[8,64,896]{2,1,0:T(8,128)(2,1)S(1)} %multiply_convert_fusion.src_ref), channel_id=1, source_target_pairs={{0,8},{1,9},{2,10},{3,11},{4,12},{5,13},{6,14},{7,15},{8,0},{9,1},... | collective-permute-start | bytes 2752520 | tf_op jit(solution)/shard_map/ppermute | solution.py:227
  8.3 62.2 %copy-start.3 = (bf16[128,2048]{1,0:T(8,128)(2,1)S(1)}, bf16[128,2048]{1,0:T(8,128)(2,1)}, u32[]{:S(2)}) copy-start(bf16[128,2048]{1,0:T(8,128)(2,1)} %param.13) | copy-start | bytes 1572868
  65.9 111.2 %collective-permute-start = (bf16[2,64,896]{2,1,0:T(8,128)(2,1)}, bf16[2,64,896]{2,1,0:T(8,128)(2,1)}, u32[]{:S(2)}, u32[]{:S(2)}) collective-permute-start(bf16[2,64,896]{2,1,0:T(8,128)(2,1)} %get-tuple-element.21), channel_id=1, source_target_pairs={{0,1},{1,0},{2,3},{3,2},{4,5},{5,4},{6,7},{7,6},{8,9},{9,8},{10,11... | collective-permute-start | bytes 688136 | tf_op jit(solution)/shard_map/ppermute | solution.py:227
  66.0 112.5 %collective-permute-start.1 = (bf16[2,64,896]{2,1,0:T(8,128)(2,1)}, bf16[2,64,896]{2,1,0:T(8,128)(2,1)}, u32[]{:S(2)}, u32[]{:S(2)}) collective-permute-start(bf16[2,64,896]{2,1,0:T(8,128)(2,1)} %get-tuple-element.22), channel_id=1, source_target_pairs={{0,2},{1,3},{2,0},{3,1},{4,6},{5,7},{6,4},{7,5},{8,10},{9,11},{10,... | collective-permute-start | bytes 688136 | tf_op jit(solution)/shard_map/ppermute | solution.py:227
  67.6 113.0 %collective-permute-start.2 = (bf16[2,64,896]{2,1,0:T(8,128)(2,1)}, bf16[2,64,896]{2,1,0:T(8,128)(2,1)}, u32[]{:S(2)}, u32[]{:S(2)}) collective-permute-start(bf16[2,64,896]{2,1,0:T(8,128)(2,1)} %get-tuple-element.23), channel_id=1, source_target_pairs={{0,3},{1,2},{2,1},{3,0},{4,7},{5,6},{6,5},{7,4},{8,11},{9,10},{10,... | collective-permute-start | bytes 688136 | tf_op jit(solution)/shard_map/ppermute | solution.py:227
  70.2 1.0 copy-start.4
  70.2 6.9 %collective-permute-start.18 = (bf16[2,56,512]{2,1,0:T(8,128)(2,1)}, bf16[2,56,512]{2,1,0:T(8,128)(2,1)}, u32[]{:S(2)}, u32[]{:S(2)}) collective-permute-start(bf16[2,56,512]{2,1,0:T(8,128)(2,1)} %reshape.116), channel_id=1, source_target_pairs={{0,1},{1,0},{2,3},{3,2},{4,5},{5,4},{6,7},{7,6},{8,9},{9,8},{10,11... | collective-permute-start | bytes 344072 | tf_op jit(solution)/shard_map/ppermute | solution.py:227
  72.8 196.9 %all-to-all-start = ((bf16[8,2,128,256]{3,2,1,0:T(8,128)(2,1)}), bf16[8,2,128,256]{3,2,1,0:T(8,128)(2,1)S(1)}, u32[]{:S(2)}, u32[]{:S(2)}) async-start(bf16[8,2,128,256]{3,2,1,0:T(8,128)(2,1)} %maximum_bitcast_fusion), calls=%async_computation | async-start | bytes 2097152 | tf_op jit(solution)/shard_map/all_to_all | solution.py:269
  78.7 21.3 %collective-permute-start.21 = (bf16[2,112,512]{2,1,0:T(8,128)(2,1)}, bf16[2,112,512]{2,1,0:T(8,128)(2,1)}, u32[]{:S(2)}, u32[]{:S(2)}) collective-permute-start(bf16[2,112,512]{2,1,0:T(8,128)(2,1)} %pad_maximum_fusion.2), channel_id=1, source_target_pairs={{0,12},{1,13},{2,14},{3,15},{4,0},{5,1},{6,2},{7,3},{8,4},{9,5},{1... | collective-permute-start | bytes 688136 | tf_op jit(solution)/shard_map/ppermute | solution.py:255
  100.0 17.6 %collective-permute-start.20 = (bf16[2,112,512]{2,1,0:T(8,128)(2,1)}, bf16[2,112,512]{2,1,0:T(8,128)(2,1)S(1)}, u32[]{:S(2)}, u32[]{:S(2)}) collective-permute-start(bf16[2,112,512]{2,1,0:T(8,128)(2,1)} %pad_maximum_fusion.2), channel_id=1, source_target_pairs={{0,8},{1,9},{2,10},{3,11},{4,12},{5,13},{6,14},{7,15},{8,0},{9,1},... | collective-permute-start | bytes 688136 | tf_op jit(solution)/shard_map/ppermute | solution.py:255
  117.6 64.4 %collective-permute-start.3 = (bf16[2,64,896]{2,1,0:T(8,128)(2,1)}, bf16[2,64,896]{2,1,0:T(8,128)(2,1)}, u32[]{:S(2)}, u32[]{:S(2)}) collective-permute-start(bf16[2,64,896]{2,1,0:T(8,128)(2,1)} %get-tuple-element.24), channel_id=1, source_target_pairs={{0,4},{1,5},{2,6},{3,7},{4,0},{5,1},{6,2},{7,3},{8,12},{9,13},{10,... | collective-permute-start | bytes 688136 | tf_op jit(solution)/shard_map/ppermute | solution.py:227
  118.2 1.4 copy-start.2
  118.2 63.8 %collective-permute-start.19 = (bf16[2,112,512]{2,1,0:T(8,128)(2,1)}, bf16[2,112,512]{2,1,0:T(8,128)(2,1)S(1)}, u32[]{:S(2)}, u32[]{:S(2)}) collective-permute-start(bf16[2,112,512]{2,1,0:T(8,128)(2,1)} %pad_maximum_fusion.2), channel_id=1, source_target_pairs={{0,4},{1,5},{2,6},{3,7},{4,8},{5,9},{6,10},{7,11},{8,12},{9,13},{1... | collective-permute-start | bytes 688136 | tf_op jit(solution)/shard_map/ppermute | solution.py:255
  177.2 7.2 %collective-permute-start.4 = (bf16[2,64,896]{2,1,0:T(8,128)(2,1)}, bf16[2,64,896]{2,1,0:T(8,128)(2,1)S(1)}, u32[]{:S(2)}, u32[]{:S(2)}) collective-permute-start(bf16[2,64,896]{2,1,0:T(8,128)(2,1)} %get-tuple-element.25), channel_id=1, source_target_pairs={{0,5},{1,4},{2,7},{3,6},{4,1},{5,0},{6,3},{7,2},{8,13},{9,12},{10,... | collective-permute-start | bytes 688136 | tf_op jit(solution)/shard_map/ppermute | solution.py:227
  178.5 13.6 %collective-permute-start.5 = (bf16[2,64,896]{2,1,0:T(8,128)(2,1)}, bf16[2,64,896]{2,1,0:T(8,128)(2,1)S(1)}, u32[]{:S(2)}, u32[]{:S(2)}) collective-permute-start(bf16[2,64,896]{2,1,0:T(8,128)(2,1)} %get-tuple-element.26), channel_id=1, source_target_pairs={{0,6},{1,7},{2,4},{3,5},{4,2},{5,3},{6,0},{7,1},{8,14},{9,15},{10,... | collective-permute-start | bytes 688136 | tf_op jit(solution)/shard_map/ppermute | solution.py:227
  180.6 14.6 %collective-permute-start.6 = (bf16[2,64,896]{2,1,0:T(8,128)(2,1)}, bf16[2,64,896]{2,1,0:T(8,128)(2,1)S(1)}, u32[]{:S(2)}, u32[]{:S(2)}) collective-permute-start(bf16[2,64,896]{2,1,0:T(8,128)(2,1)} %get-tuple-element.27), channel_id=1, source_target_pairs={{0,7},{1,6},{2,5},{3,4},{4,3},{5,2},{6,1},{7,0},{8,15},{9,14},{10,... | collective-permute-start | bytes 688136 | tf_op jit(solution)/shard_map/ppermute | solution.py:227
  182.0 15.2 %collective-permute-start.8 = (bf16[2,64,896]{2,1,0:T(8,128)(2,1)}, bf16[2,64,896]{2,1,0:T(8,128)(2,1)S(1)}, u32[]{:S(2)}, u32[]{:S(2)}) collective-permute-start(bf16[2,64,896]{2,1,0:T(8,128)(2,1)} %get-tuple-element.29), channel_id=1, source_target_pairs={{0,1},{1,0},{2,3},{3,2},{4,5},{5,4},{6,7},{7,6},{8,9},{9,8},{10,11... | collective-permute-start | bytes 688136 | tf_op jit(solution)/shard_map/ppermute | solution.py:227
  182.0 18.3 %collective-permute-start.9 = (bf16[2,64,896]{2,1,0:T(8,128)(2,1)}, bf16[2,64,896]{2,1,0:T(8,128)(2,1)S(1)}, u32[]{:S(2)}, u32[]{:S(2)}) collective-permute-start(bf16[2,64,896]{2,1,0:T(8,128)(2,1)} %get-tuple-element.30), channel_id=1, source_target_pairs={{0,2},{1,3},{2,0},{3,1},{4,6},{5,7},{6,4},{7,5},{8,10},{9,11},{10,... | collective-permute-start | bytes 688136 | tf_op jit(solution)/shard_map/ppermute | solution.py:227
  184.4 16.4 %copy-start.6 = (bf16[2,64,896]{2,1,0:T(8,128)(2,1)}, bf16[2,64,896]{2,1,0:T(8,128)(2,1)S(1)}, u32[]{:S(2)}) copy-start(bf16[2,64,896]{2,1,0:T(8,128)(2,1)S(1)} %collective-permute-done.4.refs_5_) | copy-start | bytes 688132
  184.4 20.3 %collective-permute-start.10 = (bf16[2,64,896]{2,1,0:T(8,128)(2,1)}, bf16[2,64,896]{2,1,0:T(8,128)(2,1)S(1)}, u32[]{:S(2)}, u32[]{:S(2)}) collective-permute-start(bf16[2,64,896]{2,1,0:T(8,128)(2,1)} %get-tuple-element.31), channel_id=1, source_target_pairs={{0,3},{1,2},{2,1},{3,0},{4,7},{5,6},{6,5},{7,4},{8,11},{9,10},{10,... | collective-permute-start | bytes 688136 | tf_op jit(solution)/shard_map/ppermute | solution.py:227
  192.2 8.6 %copy-start.7 = (bf16[2,64,896]{2,1,0:T(8,128)(2,1)}, bf16[2,64,896]{2,1,0:T(8,128)(2,1)S(1)}, u32[]{:S(2)}) copy-start(bf16[2,64,896]{2,1,0:T(8,128)(2,1)S(1)} %collective-permute-done.5.refs_6_) | copy-start | bytes 688132
  192.2 13.5 %collective-permute-start.11 = (bf16[2,64,896]{2,1,0:T(8,128)(2,1)}, bf16[2,64,896]{2,1,0:T(8,128)(2,1)S(1)}, u32[]{:S(2)}, u32[]{:S(2)}) collective-permute-start(bf16[2,64,896]{2,1,0:T(8,128)(2,1)} %get-tuple-element.32), channel_id=1, source_target_pairs={{0,4},{1,5},{2,6},{3,7},{4,0},{5,1},{6,2},{7,3},{8,12},{9,13},{10,... | collective-permute-start | bytes 688136 | tf_op jit(solution)/shard_map/ppermute | solution.py:227
  195.2 10.5 %copy-start.8 = (bf16[2,64,896]{2,1,0:T(8,128)(2,1)}, bf16[2,64,896]{2,1,0:T(8,128)(2,1)S(1)}, u32[]{:S(2)}) copy-start(bf16[2,64,896]{2,1,0:T(8,128)(2,1)S(1)} %collective-permute-done.6.refs_7_) | copy-start | bytes 688132
  195.2 12.2 %collective-permute-start.12 = (bf16[2,64,896]{2,1,0:T(8,128)(2,1)}, bf16[2,64,896]{2,1,0:T(8,128)(2,1)S(1)}, u32[]{:S(2)}, u32[]{:S(2)}) collective-permute-start(bf16[2,64,896]{2,1,0:T(8,128)(2,1)} %get-tuple-element.33), channel_id=1, source_target_pairs={{0,5},{1,4},{2,7},{3,6},{4,1},{5,0},{6,3},{7,2},{8,13},{9,12},{10,... | collective-permute-start | bytes 688136 | tf_op jit(solution)/shard_map/ppermute | solution.py:227
  197.2 8.5 %copy-start.9 = (bf16[2,64,896]{2,1,0:T(8,128)(2,1)}, bf16[2,64,896]{2,1,0:T(8,128)(2,1)S(1)}, u32[]{:S(2)}) copy-start(bf16[2,64,896]{2,1,0:T(8,128)(2,1)S(1)} %collective-permute-done.8.refs_9_) | copy-start | bytes 688132
  197.2 14.7 %collective-permute-start.13 = (bf16[2,64,896]{2,1,0:T(8,128)(2,1)}, bf16[2,64,896]{2,1,0:T(8,128)(2,1)S(1)}, u32[]{:S(2)}, u32[]{:S(2)}) collective-permute-start(bf16[2,64,896]{2,1,0:T(8,128)(2,1)} %get-tuple-element.34), channel_id=1, source_target_pairs={{0,6},{1,7},{2,4},{3,5},{4,2},{5,3},{6,0},{7,1},{8,14},{9,15},{10,... | collective-permute-start | bytes 688136 | tf_op jit(solution)/shard_map/ppermute | solution.py:227
  200.3 7.0 %copy-start.10 = (bf16[2,64,896]{2,1,0:T(8,128)(2,1)}, bf16[2,64,896]{2,1,0:T(8,128)(2,1)S(1)}, u32[]{:S(2)}) copy-start(bf16[2,64,896]{2,1,0:T(8,128)(2,1)S(1)} %collective-permute-done.9.refs_10_) | copy-start | bytes 688132
  200.3 14.6 %collective-permute-start.14 = (bf16[2,64,896]{2,1,0:T(8,128)(2,1)}, bf16[2,64,896]{2,1,0:T(8,128)(2,1)S(1)}, u32[]{:S(2)}, u32[]{:S(2)}) collective-permute-start(bf16[2,64,896]{2,1,0:T(8,128)(2,1)} %get-tuple-element.35), channel_id=1, source_target_pairs={{0,7},{1,6},{2,5},{3,4},{4,3},{5,2},{6,1},{7,0},{8,15},{9,14},{10,... | collective-permute-start | bytes 688136 | tf_op jit(solution)/shard_map/ppermute | solution.py:227
  204.7 2.6 copy-start.11
  204.7 42.9 %collective-permute-start.22 = (bf16[4,112,512]{2,1,0:T(8,128)(2,1)S(1)}, bf16[4,112,512]{2,1,0:T(8,128)(2,1)S(1)}, u32[]{:S(2)}, u32[]{:S(2)}) collective-permute-start(bf16[4,112,512]{2,1,0:T(8,128)(2,1)S(1)} %pad_maximum_fusion.k0), channel_id=1, source_target_pairs={{0,2},{1,3},{2,0},{3,1},{4,6},{5,7},{6,4},{7,5},{8,10},{9,11},{10,... | collective-permute-start | bytes 1376264 | tf_op jit(solution)/shard_map/ppermute | solution.py:227
  205.7 2.2 copy-start.12
  205.7 43.6 %collective-permute-start.23 = (bf16[4,112,512]{2,1,0:T(8,128)(2,1)S(1)}, bf16[4,112,512]{2,1,0:T(8,128)(2,1)S(1)}, u32[]{:S(2)}, u32[]{:S(2)}) collective-permute-start(bf16[4,112,512]{2,1,0:T(8,128)(2,1)S(1)} %pad_maximum_fusion.k0), channel_id=1, source_target_pairs={{0,16},{16,0},{1,17},{17,1},{2,18},{18,2},{3,19},{19,3},{4,20},{20... | collective-permute-start | bytes 1376264 | tf_op jit(solution)/shard_map/ppermute | solution.py:230
  207.3 4.6 %copy-start.13 = (bf16[2,64,896]{2,1,0:T(8,128)(2,1)}, bf16[2,64,896]{2,1,0:T(8,128)(2,1)S(1)}, u32[]{:S(2)}) copy-start(bf16[2,64,896]{2,1,0:T(8,128)(2,1)S(1)} %collective-permute-done.12.refs_13_) | copy-start | bytes 688132
  207.3 40.7 %collective-permute-start.26 = (bf16[4,112,512]{2,1,0:T(8,128)(2,1)S(1)}, bf16[4,112,512]{2,1,0:T(8,128)(2,1)S(1)}, u32[]{:S(2)}, u32[]{:S(2)}) collective-permute-start(bf16[4,112,512]{2,1,0:T(8,128)(2,1)S(1)} %pad_maximum_fusion.1.v0), channel_id=1, source_target_pairs={{0,16},{16,0},{1,17},{17,1},{2,18},{18,2},{3,19},{19,3},{4,20},{20... | collective-permute-start | bytes 1376264 | tf_op jit(solution)/shard_map/ppermute | solution.py:230
  211.9 3.0 copy-start.14
  214.9 0.7 copy-start.15
  245.2 13.8 %collective-permute-start.15 = (bf16[4,64,896]{2,1,0:T(8,128)(2,1)}, bf16[4,64,896]{2,1,0:T(8,128)(2,1)}, u32[]{:S(2)}, u32[]{:S(2)}) collective-permute-start(bf16[4,64,896]{2,1,0:T(8,128)(2,1)} %get-tuple-element.37), channel_id=1, source_target_pairs={{0,16},{16,0},{1,17},{17,1},{2,18},{18,2},{3,19},{19,3},{4,20},{20... | collective-permute-start | bytes 1376264 | tf_op jit(solution)/shard_map/ppermute | solution.py:230
  246.8 13.4 %collective-permute-start.25 = (bf16[4,112,512]{2,1,0:T(8,128)(2,1)S(1)}, bf16[4,112,512]{2,1,0:T(8,128)(2,1)}, u32[]{:S(2)}, u32[]{:S(2)}) collective-permute-start(bf16[4,112,512]{2,1,0:T(8,128)(2,1)S(1)} %pad_maximum_fusion.1.v0), channel_id=1, source_target_pairs={{0,2},{1,3},{2,0},{3,1},{4,6},{5,7},{6,4},{7,5},{8,10},{9,11},{10,... | collective-permute-start | bytes 1376264 | tf_op jit(solution)/shard_map/ppermute | solution.py:227
  247.6 21.1 %collective-permute-start.24 = (bf16[4,112,512]{2,1,0:T(8,128)(2,1)S(1)}, bf16[4,112,512]{2,1,0:T(8,128)(2,1)}, u32[]{:S(2)}, u32[]{:S(2)}) collective-permute-start(bf16[4,112,512]{2,1,0:T(8,128)(2,1)S(1)} %collective-permute-done.22.kx), channel_id=1, source_target_pairs={{0,16},{16,0},{1,17},{17,1},{2,18},{18,2},{3,19},{19,3},{4,20},{20... | collective-permute-start | bytes 1376264 | tf_op jit(solution)/shard_map/ppermute | solution.py:230
  248.1 21.6 %collective-permute-start.27 = (bf16[4,112,512]{2,1,0:T(8,128)(2,1)S(1)}, bf16[4,112,512]{2,1,0:T(8,128)(2,1)}, u32[]{:S(2)}, u32[]{:S(2)}) collective-permute-start(bf16[4,112,512]{2,1,0:T(8,128)(2,1)S(1)} %collective-permute-done.26.vy), channel_id=1, source_target_pairs={{0,2},{1,3},{2,0},{3,1},{4,6},{5,7},{6,4},{7,5},{8,10},{9,11},{10,... | collective-permute-start | bytes 1376264 | tf_op jit(solution)/shard_map/ppermute | solution.py:227
  249.3 20.3 %collective-permute-start.16 = (bf16[2,128,896]{2,1,0:T(8,128)(2,1)}, bf16[2,128,896]{2,1,0:T(8,128)(2,1)}, u32[]{:S(2)}, u32[]{:S(2)}) collective-permute-start(bf16[2,128,896]{2,1,0:T(8,128)(2,1)} %bitcast.23), channel_id=1, source_target_pairs={{0,1},{1,0},{2,3},{3,2},{4,5},{5,4},{6,7},{7,6},{8,9},{9,8},{10,11... | collective-permute-start | bytes 1376264 | tf_op jit(solution)/shard_map/ppermute | solution.py:227
  259.0 10.7 %collective-permute-start.17 = (bf16[2,128,896]{2,1,0:T(8,128)(2,1)}, bf16[2,128,896]{2,1,0:T(8,128)(2,1)}, u32[]{:S(2)}, u32[]{:S(2)}) collective-permute-start(bf16[2,128,896]{2,1,0:T(8,128)(2,1)} %bitcast.12.nb), channel_id=1, source_target_pairs={{0,1},{1,0},{2,3},{3,2},{4,5},{5,4},{6,7},{7,6},{8,9},{9,8},{10,11... | collective-permute-start | bytes 1376264 | tf_op jit(solution)/shard_map/ppermute | solution.py:227
  269.7 1.0 copy-start

commit v3 on v2

--- a/solution.py
+++ b/solution.py
@@ -42,20 +42,10 @@
 ALL = range(ZS * XS * CS)
 
 
-def rows_kernel(rows_ref, src_ref, *refs):
-    outs, sem = refs[:-1], refs[-1]
-    copies = []
+def rows_kernel(rows_ref, src_ref, *outs):
     for k in range(HALF):
-        for s in range(MOST):
-            copies.append(
-                pltpu.make_async_copy(
-                    src_ref.at[rows_ref[k * MOST + s]], outs[k].at[s], sem.at[k * MOST + s]
-                )
-            )
-    for copy in copies:
-        copy.start()
-    for copy in copies:
-        copy.wait()
+        for m in range(MOST):
+            outs[k][m] = src_ref[rows_ref[k * MOST + m]]
 
 
 def pick_rows(rows, source):
@@ -64,11 +54,11 @@
         rows_kernel,
         in_specs=[
             pl.BlockSpec(memory_space=pltpu.SMEM),
-            pl.BlockSpec(memory_space=pl.ANY),
+            pl.BlockSpec(memory_space=pltpu.VMEM),
         ],
-        out_specs=[pl.BlockSpec(memory_space=pl.ANY)] * HALF,
+        out_specs=[pl.BlockSpec(memory_space=pltpu.VMEM)] * HALF,
         out_shape=[piece] * HALF,
-        scratch_shapes=[pltpu.SemaphoreType.DMA((HALF * MOST,))],
+        compiler_params=pltpu.CompilerParams(vmem_limit_bytes=32 * 1024 * 1024),
         name="pick_rows",
     )(rows, source)
 
@@ -96,7 +86,7 @@
         choose_kernel,
         in_specs=[pl.BlockSpec(memory_space=pltpu.SMEM)]
         + [pl.BlockSpec(memory_space=pl.ANY)] * len(pieces),
-        out_specs=[pl.BlockSpec(memory_space=pl.ANY)] * 2,
+        out_specs=[pl.BlockSpec(memory_space=pltpu.VMEM)] * 2,
         out_shape=[half] * 2,
         scratch_shapes=[pltpu.SemaphoreType.DMA((2 * CH_DEV * NBR,))],
         name="choose",

time: 321 us -> 215 us (0.67)
  Pallas kernels: 163 us -> 23.7 us
  waiting for transfers between devices: 66.3 us -> 86.9 us
  local copies, waits for them, and re-layouts: 12.1 us -> 18.8 us
    pallas_call x2, Pallas kernels: 115 us -> 2.15 us  [pick_rows(): pl.pallas_call(rows_kernel, in_specs=[pl.BlockSpec(memory_space=pltpu.SME...]
    pallas_call x1, Pallas kernels: 29.6 us -> 2.93 us  [choose(): pl.pallas_call(choose_kernel, in_specs=[pl.BlockSpec(memory_space=pltpu.S...]
    ppermute x3, waiting for transfers between devices: 25.5 us -> 43.4 us  [small(): lax.ppermute(chip_w, 'mp', [(m, (m + XS * CS * r) % len(ALL)) for m in ALL])]
    unnamed x42 -> x48, local copies, waits for them, and re-layouts: 4.71 us -> 9.27 us
  transfers between devices with their start and end apart: 29 -> 29, of which waited for: 13 -> 14; matrix products, arithmetic and copies ran while one was open for 3% -> 8% of each run, Pallas kernels for 45% -> 2%
where the time goes in v3:
time: 215 us; the launch traced here: 214 us
  waiting for transfers between devices  86.9 us (40%)
  starting transfers between devices  47.5 us (22%)
  blocking collectives  29.3 us (14%)
  Pallas kernels  23.7 us (11%)
  local copies, waits for them, and re-layouts  18.8 us (9%)
  other arithmetic  6.84 us (3%)
    ppermute x3, waiting for transfers between devices, small(): lax.ppermute(chip_w, 'mp', [(m, (m + XS * CS * r) % len(ALL)) for m in ALL])  43.4 us
    all_to_all x1, blocking collectives, small(): lax.all_to_all(result, 'mp', split_axis=0, concat_axis=0, tiled=True, axi...  29.3 us
    ppermute x21, waiting for transfers between devices, swap(): return lax.ppermute(a, 'mp', [(m, m ^ bits) for m in ALL])  23.3 us
    ppermute x21, starting transfers between devices, swap(): return lax.ppermute(a, 'mp', [(m, m ^ bits) for m in ALL])  22.7 us
    ppermute x4, waiting for transfers between devices, swap_dp(): return lax.ppermute(a, 'dp', [(0, 1), (1, 0)])  20.1 us
    pallas_call x1, Pallas kernels, attend(): pl.pallas_call(attend_kernel, grid_spec=pltpu.PrefetchScalarGridSpec(num_...  18.7 us
    ppermute x3, starting transfers between devices, small(): lax.ppermute(chip_w, 'mp', [(m, (m + XS * CS * r) % len(ALL)) for m in ALL])  15.9 us
    unnamed x48, local copies, waits for them, and re-layouts  9.27 us
  transfers between devices with their start and end apart: 29, of which 14 were waited for; matrix products, arithmetic and copies ran while one was open for 8% of the time, Pallas kernels for 2%

profile of v3, /device:TPU:0, one launch (start us, length us, event | category | flops | bytes accessed | tf_op | source)
XLA Modules:
  0.0 214.1 jit_solution(6134118473465843601)
XLA Ops:
  0.7 1.4 multiply_convert_fusion.src_ref
  2.1 4.1 %collective-permute-start.7 = (bf16[8,64,896]{2,1,0:T(8,128)(2,1)S(1)}, bf16[8,64,896]{2,1,0:T(8,128)(2,1)S(1)}, u32[]{:S(2)}, u32[]{:S(2)}) collective-permute-start(bf16[8,64,896]{2,1,0:T(8,128)(2,1)S(1)} %multiply_convert_fusion.src_ref), channel_id=1, source_target_pairs={{0,8},{1,9},{2,10},{3,11},{4,12},{5,13},{6,14},{7,15},{8,0},{9,1},... | collective-permute-start | bytes 2752520 | tf_op jit(solution)/shard_map/ppermute | solution.py:217
  7.1 0.6 gather_fusion
  7.8 1.5 pick_rows.2
  9.2 0.7 copy-done.1
  9.9 0.7 copy-done.5
  10.6 1.5 collective-permute-start.1
  12.1 0.4 collective-permute-start.2
  12.5 1.1 reshape.114
  13.5 1.4 dynamic-slice_reduce_fusion.1
  15.0 0.7 reshape.116
  16.0 1.3 copy.64
  17.3 1.0 copy.66
  18.3 1.4 copy.63
  19.7 1.0 copy.65
  20.7 2.1 maximum_bitcast_fusion
  22.8 3.8 %all-to-all-start = ((bf16[8,2,128,256]{3,2,1,0:T(8,128)(2,1)}), bf16[8,2,128,256]{3,2,1,0:T(8,128)(2,1)S(1)}, u32[]{:S(2)}, u32[]{:S(2)}) async-start(bf16[8,2,128,256]{3,2,1,0:T(8,128)(2,1)} %maximum_bitcast_fusion), calls=%async_computation | async-start | bytes 2097152 | tf_op jit(solution)/shard_map/all_to_all | solution.py:259
  27.0 0.7 reshape.115
  27.7 1.0 broadcast_select_fusion.1
  28.7 0.6 copy-done.7
  29.3 0.7 pad_maximum_fusion.2
  30.0 3.8 %collective-permute-start.21 = (bf16[2,112,512]{2,1,0:T(8,128)(2,1)}, bf16[2,112,512]{2,1,0:T(8,128)(2,1)}, u32[]{:S(2)}, u32[]{:S(2)}) collective-permute-start(bf16[2,112,512]{2,1,0:T(8,128)(2,1)} %pad_maximum_fusion.2), channel_id=1, source_target_pairs={{0,12},{1,13},{2,14},{3,15},{4,0},{5,1},{6,2},{7,3},{8,4},{9,5},{1... | collective-permute-start | bytes 688136 | tf_op jit(solution)/shard_map/ppermute | solution.py:245
  33.9 0.6 reshape.110.where_ref
  34.6 0.9 fusion.1
  35.5 27.0 %collective-permute-done.21 = bf16[2,112,512]{2,1,0:T(8,128)(2,1)} collective-permute-done((bf16[2,112,512]{2,1,0:T(8,128)(2,1)}, bf16[2,112,512]{2,1,0:T(8,128)(2,1)}, u32[]{:S(2)}, u32[]{:S(2)}) %collective-permute-start.21) | collective-permute-done | bytes 229408 | tf_op jit(solution)/shard_map/ppermute | solution.py:245
  62.5 10.8 %collective-permute-start.20 = (bf16[2,112,512]{2,1,0:T(8,128)(2,1)}, bf16[2,112,512]{2,1,0:T(8,128)(2,1)S(1)}, u32[]{:S(2)}, u32[]{:S(2)}) collective-permute-start(bf16[2,112,512]{2,1,0:T(8,128)(2,1)} %pad_maximum_fusion.2), channel_id=1, source_target_pairs={{0,8},{1,9},{2,10},{3,11},{4,12},{5,13},{6,14},{7,15},{8,0},{9,1},... | collective-permute-start | bytes 688136 | tf_op jit(solution)/shard_map/ppermute | solution.py:245
  73.3 1.0 fusion.6
  74.3 9.2 %collective-permute-done.20 = bf16[2,112,512]{2,1,0:T(8,128)(2,1)S(1)} collective-permute-done((bf16[2,112,512]{2,1,0:T(8,128)(2,1)}, bf16[2,112,512]{2,1,0:T(8,128)(2,1)S(1)}, u32[]{:S(2)}, u32[]{:S(2)}) %collective-permute-start.20) | collective-permute-done | bytes 229408 | tf_op jit(solution)/shard_map/ppermute | solution.py:245
  83.5 0.8 collective-permute-start.3
  84.3 1.2 collective-permute-start.19
  85.5 0.7 pick_rows.3
  86.3 1.7 collective-permute-start.4
  88.0 2.0 collective-permute-start.5
  89.9 1.4 collective-permute-start.6
  91.3 7.2 %collective-permute-done.19 = bf16[2,112,512]{2,1,0:T(8,128)(2,1)S(1)} collective-permute-done((bf16[2,112,512]{2,1,0:T(8,128)(2,1)}, bf16[2,112,512]{2,1,0:T(8,128)(2,1)S(1)}, u32[]{:S(2)}, u32[]{:S(2)}) %collective-permute-start.19) | collective-permute-done | bytes 229408 | tf_op jit(solution)/shard_map/ppermute | solution.py:245
  98.6 1.4 collective-permute-start.9
  100.0 0.3 collective-permute-done.4.refs_5_
  100.4 1.5 collective-permute-start.10
  101.8 5.0 %collective-permute-done.5.refs_6_ = bf16[2,64,896]{2,1,0:T(8,128)(2,1)S(1)} collective-permute-done((bf16[2,64,896]{2,1,0:T(8,128)(2,1)S(1)}, bf16[2,64,896]{2,1,0:T(8,128)(2,1)S(1)}, u32[]{:S(2)}, u32[]{:S(2)}) %collective-permute-start.5) | collective-permute-done | bytes 229408 | tf_op jit(solution)/shard_map/ppermute | solution.py:217
  106.8 1.9 collective-permute-start.11
  108.7 1.5 collective-permute-done.6.refs_7_
  110.2 2.8 %collective-permute-start.12 = (bf16[2,64,896]{2,1,0:T(8,128)(2,1)S(1)}, bf16[2,64,896]{2,1,0:T(8,128)(2,1)S(1)}, u32[]{:S(2)}, u32[]{:S(2)}) collective-permute-start(bf16[2,64,896]{2,1,0:T(8,128)(2,1)S(1)} %get-tuple-element.33), channel_id=1, source_target_pairs={{0,5},{1,4},{2,7},{3,6},{4,1},{5,0},{6,3},{7,2},{8,13},{9,12},{10,... | collective-permute-start | bytes 688136 | tf_op jit(solution)/shard_map/ppermute | solution.py:217
  113.2 2.8 %collective-permute-done.9.refs_10_ = bf16[2,64,896]{2,1,0:T(8,128)(2,1)S(1)} collective-permute-done((bf16[2,64,896]{2,1,0:T(8,128)(2,1)S(1)}, bf16[2,64,896]{2,1,0:T(8,128)(2,1)S(1)}, u32[]{:S(2)}, u32[]{:S(2)}) %collective-permute-start.9) | collective-permute-done | bytes 229408 | tf_op jit(solution)/shard_map/ppermute | solution.py:217
  116.0 0.7 copy-done.13
  116.8 1.5 collective-permute-done.10.refs_11_
  118.3 1.9 collective-permute-start.22
  120.1 1.5 collective-permute-start.23
  121.6 0.5 collective-permute-start.26
  122.1 4.4 %collective-permute-done.13.refs_14_ = bf16[2,64,896]{2,1,0:T(8,128)(2,1)S(1)} collective-permute-done((bf16[2,64,896]{2,1,0:T(8,128)(2,1)S(1)}, bf16[2,64,896]{2,1,0:T(8,128)(2,1)S(1)}, u32[]{:S(2)}, u32[]{:S(2)}) %collective-permute-start.13) | collective-permute-done | bytes 229408 | tf_op jit(solution)/shard_map/ppermute | solution.py:217
  126.5 3.3 %collective-permute-done.14.refs_15_ = bf16[2,64,896]{2,1,0:T(8,128)(2,1)S(1)} collective-permute-done((bf16[2,64,896]{2,1,0:T(8,128)(2,1)S(1)}, bf16[2,64,896]{2,1,0:T(8,128)(2,1)S(1)}, u32[]{:S(2)}, u32[]{:S(2)}) %collective-permute-start.14) | collective-permute-done | bytes 229408 | tf_op jit(solution)/shard_map/ppermute | solution.py:217
  129.9 0.7 copy-done.18
  130.5 2.9 %choose.1 = (bf16[4,64,896]{2,1,0:T(8,128)(2,1)}, bf16[4,64,896]{2,1,0:T(8,128)(2,1)}) custom-call(s32[16]{0:T(128)} %reshape.110.where_ref, bf16[2,64,896]{2,1,0:T(8,128)(2,1)} %copy-done.1, bf16[2,64,896]{2,1,0:T(8,128)(2,1)} %collective-permute-done.refs_1_, bf16[2,64,896]{2,1,0:T(8,128)(2,1)} %collective-permute-done.1.refs_2_, ...), custom_call_target="tpu_custom_call" | custom-call | tf_op jit(solution)/shard_map/choose/pallas_call | solution.py:85
  133.5 1.6 collective-permute-start.15
  135.1 0.8 collective-permute-start.25
  135.8 4.5 %collective-permute-done.22.kx = bf16[4,112,512]{2,1,0:T(8,128)(2,1)S(1)} collective-permute-done((bf16[4,112,512]{2,1,0:T(8,128)(2,1)S(1)}, bf16[4,112,512]{2,1,0:T(8,128)(2,1)S(1)}, u32[]{:S(2)}, u32[]{:S(2)}) %collective-permute-start.22) | collective-permute-done | bytes 458784 | tf_op jit(solution)/shard_map/ppermute | solution.py:217
  140.4 1.5 collective-permute-start.24
  141.9 1.4 collective-permute-done.26.vy
  143.5 9.7 %collective-permute-done.15 = bf16[4,64,896]{2,1,0:T(8,128)(2,1)} collective-permute-done((bf16[4,64,896]{2,1,0:T(8,128)(2,1)}, bf16[4,64,896]{2,1,0:T(8,128)(2,1)}, u32[]{:S(2)}, u32[]{:S(2)}) %collective-permute-start.15) | collective-permute-done | bytes 458784 | tf_op jit(solution)/shard_map/ppermute | solution.py:220
  153.3 9.0 %collective-permute-done.24.kd = bf16[4,112,512]{2,1,0:T(8,128)(2,1)} collective-permute-done((bf16[4,112,512]{2,1,0:T(8,128)(2,1)S(1)}, bf16[4,112,512]{2,1,0:T(8,128)(2,1)}, u32[]{:S(2)}, u32[]{:S(2)}) %collective-permute-start.24) | collective-permute-done | bytes 458784 | tf_op jit(solution)/shard_map/ppermute | solution.py:220
  162.4 1.0 copy-done
  163.4 18.7 %attend.1 = bf16[8,2,128,256]{3,2,1,0:T(8,128)(2,1)S(1)} custom-call(s32[4]{0:T(128)S(1)} %pad_add_fusion.2.place_ref, bf16[2,128,896]{2,1,0:T(8,128)(2,1)S(1)} %bitcast.24, bf16[2,128,896]{2,1,0:T(8,128)(2,1)} %bitcast.12.nb, bf16[2,128,896]{2,1,0:T(8,128)(2,1)} %collective-permute-done.16.sa, bf16[2,128,896]{2,1,0:T(8,128)(2,1)} %collective-permute-done.17.sb, ...), custom_call_target="tpu_custom_call" | custom-call | tf_op jit(solution)/shard_map/attend/pallas_call | solution.py:186
  182.1 29.3 %all_to_all.10 = bf16[8,2,128,256]{3,2,1,0:T(8,128)(2,1)S(1)} all-to-all(bf16[8,2,128,256]{3,2,1,0:T(8,128)(2,1)S(1)} %attend.1), channel_id=1, replica_groups={{0,2,4,6,8,10,12,14},{1,3,5,7,9,11,13,15},{16,18,20,22,24,26,28,30},{17..., dimensions={0} | all-to-all | bytes 2097152 | tf_op jit(solution)/shard_map/all_to_all | solution.py:274
  211.8 1.0 copy.69
  213.1 1.0 copy.70
  (90 shorter events, 3.1 us)
Async XLA Ops:
  0.6 5.5 %copy-start.19 = (s32[64,2]{0,1:T(2,128)S(1)}, s32[64,2]{0,1:T(2,128)}, u32[]{:S(2)}) copy-start(s32[64,2]{0,1:T(2,128)} %param.11) | copy-start | bytes 1540
  0.6 5.8 %copy-start.20 = (s32[64,2]{0,1:T(2,128)S(1)}, s32[64,2]{0,1:T(2,128)}, u32[]{:S(2)}) copy-start(s32[64,2]{0,1:T(2,128)} %param.12) | copy-start | bytes 1540
  2.1 82.2 %collective-permute-start.7 = (bf16[8,64,896]{2,1,0:T(8,128)(2,1)S(1)}, bf16[8,64,896]{2,1,0:T(8,128)(2,1)S(1)}, u32[]{:S(2)}, u32[]{:S(2)}) collective-permute-start(bf16[8,64,896]{2,1,0:T(8,128)(2,1)S(1)} %multiply_convert_fusion.src_ref), channel_id=1, source_target_pairs={{0,8},{1,9},{2,10},{3,11},{4,12},{5,13},{6,14},{7,15},{8,0},{9,1},... | collective-permute-start | bytes 2752520 | tf_op jit(solution)/shard_map/ppermute | solution.py:217
  9.2 0.7 copy-start.1
  9.9 0.7 copy-start.5
  10.6 6.7 %copy-start.3 = (bf16[2,64,896]{2,1,0:T(8,128)(2,1)}, bf16[2,64,896]{2,1,0:T(8,128)(2,1)S(1)}, u32[]{:S(2)}) copy-start(bf16[2,64,896]{2,1,0:T(8,128)(2,1)S(1)} %get-tuple-element.25) | copy-start | bytes 688132
  10.6 75.7 %collective-permute-start = (bf16[2,64,896]{2,1,0:T(8,128)(2,1)}, bf16[2,64,896]{2,1,0:T(8,128)(2,1)}, u32[]{:S(2)}, u32[]{:S(2)}) collective-permute-start(bf16[2,64,896]{2,1,0:T(8,128)(2,1)} %get-tuple-element.21), channel_id=1, source_target_pairs={{0,1},{1,0},{2,3},{3,2},{4,5},{5,4},{6,7},{7,6},{8,9},{9,8},{10,11... | collective-permute-start | bytes 688136 | tf_op jit(solution)/shard_map/ppermute | solution.py:217
  10.6 77.4 %collective-permute-start.1 = (bf16[2,64,896]{2,1,0:T(8,128)(2,1)}, bf16[2,64,896]{2,1,0:T(8,128)(2,1)}, u32[]{:S(2)}, u32[]{:S(2)}) collective-permute-start(bf16[2,64,896]{2,1,0:T(8,128)(2,1)} %get-tuple-element.22), channel_id=1, source_target_pairs={{0,2},{1,3},{2,0},{3,1},{4,6},{5,7},{6,4},{7,5},{8,10},{9,11},{10,... | collective-permute-start | bytes 688136 | tf_op jit(solution)/shard_map/ppermute | solution.py:217
  12.1 77.9 %collective-permute-start.2 = (bf16[2,64,896]{2,1,0:T(8,128)(2,1)}, bf16[2,64,896]{2,1,0:T(8,128)(2,1)}, u32[]{:S(2)}, u32[]{:S(2)}) collective-permute-start(bf16[2,64,896]{2,1,0:T(8,128)(2,1)} %get-tuple-element.23), channel_id=1, source_target_pairs={{0,3},{1,2},{2,1},{3,0},{4,7},{5,6},{6,5},{7,4},{8,11},{9,10},{10,... | collective-permute-start | bytes 688136 | tf_op jit(solution)/shard_map/ppermute | solution.py:217
  15.7 12.0 %collective-permute-start.18 = (bf16[2,56,512]{2,1,0:T(8,128)(2,1)}, bf16[2,56,512]{2,1,0:T(8,128)(2,1)}, u32[]{:S(2)}, u32[]{:S(2)}) collective-permute-start(bf16[2,56,512]{2,1,0:T(8,128)(2,1)} %reshape.116), channel_id=1, source_target_pairs={{0,1},{1,0},{2,3},{3,2},{4,5},{5,4},{6,7},{7,6},{8,9},{9,8},{10,11... | collective-permute-start | bytes 344072 | tf_op jit(solution)/shard_map/ppermute | solution.py:217
  18.3 2.4 %copy-start.6 = (bf16[1,128,8,256]{3,1,0,2:T(8,128)(2,1)S(1)}, bf16[1,128,8,256]{3,1,0,2:T(8,128)(2,1)}, u32[]{:S(2)}) copy-start(bf16[1,128,8,256]{3,1,0,2:T(8,128)(2,1)} %copy.66) | copy-start | bytes 1572868
  22.8 139.6 %all-to-all-start = ((bf16[8,2,128,256]{3,2,1,0:T(8,128)(2,1)}), bf16[8,2,128,256]{3,2,1,0:T(8,128)(2,1)S(1)}, u32[]{:S(2)}, u32[]{:S(2)}) async-start(bf16[8,2,128,256]{3,2,1,0:T(8,128)(2,1)} %maximum_bitcast_fusion), calls=%async_computation | async-start | bytes 2097152 | tf_op jit(solution)/shard_map/all_to_all | solution.py:259
  28.7 0.6 copy-start.7
  30.0 32.4 %collective-permute-start.21 = (bf16[2,112,512]{2,1,0:T(8,128)(2,1)}, bf16[2,112,512]{2,1,0:T(8,128)(2,1)}, u32[]{:S(2)}, u32[]{:S(2)}) collective-permute-start(bf16[2,112,512]{2,1,0:T(8,128)(2,1)} %pad_maximum_fusion.2), channel_id=1, source_target_pairs={{0,12},{1,13},{2,14},{3,15},{4,0},{5,1},{6,2},{7,3},{8,4},{9,5},{1... | collective-permute-start | bytes 688136 | tf_op jit(solution)/shard_map/ppermute | solution.py:245
  34.6 51.7 %copy-start.4 = (bf16[2,64,896]{2,1,0:T(8,128)(2,1)S(1)}, bf16[2,64,896]{2,1,0:T(8,128)(2,1)}, u32[]{:S(2)}) copy-start(bf16[2,64,896]{2,1,0:T(8,128)(2,1)} %copy-done.3) | copy-start | bytes 688132
  62.5 21.0 %collective-permute-start.20 = (bf16[2,112,512]{2,1,0:T(8,128)(2,1)}, bf16[2,112,512]{2,1,0:T(8,128)(2,1)S(1)}, u32[]{:S(2)}, u32[]{:S(2)}) collective-permute-start(bf16[2,112,512]{2,1,0:T(8,128)(2,1)} %pad_maximum_fusion.2), channel_id=1, source_target_pairs={{0,8},{1,9},{2,10},{3,11},{4,12},{5,13},{6,14},{7,15},{8,0},{9,1},... | collective-permute-start | bytes 688136 | tf_op jit(solution)/shard_map/ppermute | solution.py:245
  83.5 7.9 %collective-permute-start.3 = (bf16[2,64,896]{2,1,0:T(8,128)(2,1)}, bf16[2,64,896]{2,1,0:T(8,128)(2,1)S(1)}, u32[]{:S(2)}, u32[]{:S(2)}) collective-permute-start(bf16[2,64,896]{2,1,0:T(8,128)(2,1)} %copy-done.5), channel_id=1, source_target_pairs={{0,4},{1,5},{2,6},{3,7},{4,0},{5,1},{6,2},{7,3},{8,12},{9,13},{10,... | collective-permute-start | bytes 688136 | tf_op jit(solution)/shard_map/ppermute | solution.py:217
  84.3 14.3 %collective-permute-start.19 = (bf16[2,112,512]{2,1,0:T(8,128)(2,1)}, bf16[2,112,512]{2,1,0:T(8,128)(2,1)S(1)}, u32[]{:S(2)}, u32[]{:S(2)}) collective-permute-start(bf16[2,112,512]{2,1,0:T(8,128)(2,1)} %pad_maximum_fusion.2), channel_id=1, source_target_pairs={{0,4},{1,5},{2,6},{3,7},{4,8},{5,9},{6,10},{7,11},{8,12},{9,13},{1... | collective-permute-start | bytes 688136 | tf_op jit(solution)/shard_map/ppermute | solution.py:245
  86.2 30.5 %copy-start.2 = (bf16[2,64,896]{2,1,0:T(8,128)(2,1)}, bf16[2,64,896]{2,1,0:T(8,128)(2,1)S(1)}, u32[]{:S(2)}) copy-start(bf16[2,64,896]{2,1,0:T(8,128)(2,1)S(1)} %get-tuple-element.28.refs_8_) | copy-start | bytes 688132
  86.3 14.1 %collective-permute-start.4 = (bf16[2,64,896]{2,1,0:T(8,128)(2,1)S(1)}, bf16[2,64,896]{2,1,0:T(8,128)(2,1)S(1)}, u32[]{:S(2)}, u32[]{:S(2)}) collective-permute-start(bf16[2,64,896]{2,1,0:T(8,128)(2,1)S(1)} %copy-done.4), channel_id=1, source_target_pairs={{0,5},{1,4},{2,7},{3,6},{4,1},{5,0},{6,3},{7,2},{8,13},{9,12},{10,... | collective-permute-start | bytes 688136 | tf_op jit(solution)/shard_map/ppermute | solution.py:217
  88.0 18.9 %collective-permute-start.5 = (bf16[2,64,896]{2,1,0:T(8,128)(2,1)S(1)}, bf16[2,64,896]{2,1,0:T(8,128)(2,1)S(1)}, u32[]{:S(2)}, u32[]{:S(2)}) collective-permute-start(bf16[2,64,896]{2,1,0:T(8,128)(2,1)S(1)} %get-tuple-element.26), channel_id=1, source_target_pairs={{0,6},{1,7},{2,4},{3,5},{4,2},{5,3},{6,0},{7,1},{8,14},{9,15},{10,... | collective-permute-start | bytes 688136 | tf_op jit(solution)/shard_map/ppermute | solution.py:217
  89.9 20.3 %collective-permute-start.6 = (bf16[2,64,896]{2,1,0:T(8,128)(2,1)S(1)}, bf16[2,64,896]{2,1,0:T(8,128)(2,1)S(1)}, u32[]{:S(2)}, u32[]{:S(2)}) collective-permute-start(bf16[2,64,896]{2,1,0:T(8,128)(2,1)S(1)} %get-tuple-element.27), channel_id=1, source_target_pairs={{0,7},{1,6},{2,5},{3,4},{4,3},{5,2},{6,1},{7,0},{8,15},{9,14},{10,... | collective-permute-start | bytes 688136 | tf_op jit(solution)/shard_map/ppermute | solution.py:217
  91.3 25.4 %copy-start.8 = (bf16[2,64,896]{2,1,0:T(8,128)(2,1)}, bf16[2,64,896]{2,1,0:T(8,128)(2,1)S(1)}, u32[]{:S(2)}) copy-start(bf16[2,64,896]{2,1,0:T(8,128)(2,1)S(1)} %collective-permute-done.3.refs_4_) | copy-start | bytes 688132
  91.3 21.7 %collective-permute-start.8 = (bf16[2,64,896]{2,1,0:T(8,128)(2,1)S(1)}, bf16[2,64,896]{2,1,0:T(8,128)(2,1)S(1)}, u32[]{:S(2)}, u32[]{:S(2)}) collective-permute-start(bf16[2,64,896]{2,1,0:T(8,128)(2,1)S(1)} %get-tuple-element.29), channel_id=1, source_target_pairs={{0,1},{1,0},{2,3},{3,2},{4,5},{5,4},{6,7},{7,6},{8,9},{9,8},{10,11... | collective-permute-start | bytes 688136 | tf_op jit(solution)/shard_map/ppermute | solution.py:217
  98.6 17.4 %collective-permute-start.9 = (bf16[2,64,896]{2,1,0:T(8,128)(2,1)S(1)}, bf16[2,64,896]{2,1,0:T(8,128)(2,1)S(1)}, u32[]{:S(2)}, u32[]{:S(2)}) collective-permute-start(bf16[2,64,896]{2,1,0:T(8,128)(2,1)S(1)} %get-tuple-element.30), channel_id=1, source_target_pairs={{0,2},{1,3},{2,0},{3,1},{4,6},{5,7},{6,4},{7,5},{8,10},{9,11},{10,... | collective-permute-start | bytes 688136 | tf_op jit(solution)/shard_map/ppermute | solution.py:217
  100.3 16.3 %copy-start.9 = (bf16[2,64,896]{2,1,0:T(8,128)(2,1)}, bf16[2,64,896]{2,1,0:T(8,128)(2,1)S(1)}, u32[]{:S(2)}) copy-start(bf16[2,64,896]{2,1,0:T(8,128)(2,1)S(1)} %collective-permute-done.4.refs_5_) | copy-start | bytes 688132
  100.4 17.9 %collective-permute-start.10 = (bf16[2,64,896]{2,1,0:T(8,128)(2,1)S(1)}, bf16[2,64,896]{2,1,0:T(8,128)(2,1)S(1)}, u32[]{:S(2)}, u32[]{:S(2)}) collective-permute-start(bf16[2,64,896]{2,1,0:T(8,128)(2,1)S(1)} %get-tuple-element.31), channel_id=1, source_target_pairs={{0,3},{1,2},{2,1},{3,0},{4,7},{5,6},{6,5},{7,4},{8,11},{9,10},{10,... | collective-permute-start | bytes 688136 | tf_op jit(solution)/shard_map/ppermute | solution.py:217
  106.8 9.1 %copy-start.10 = (bf16[2,64,896]{2,1,0:T(8,128)(2,1)}, bf16[2,64,896]{2,1,0:T(8,128)(2,1)S(1)}, u32[]{:S(2)}) copy-start(bf16[2,64,896]{2,1,0:T(8,128)(2,1)S(1)} %collective-permute-done.5.refs_6_) | copy-start | bytes 688132
  106.8 13.3 %collective-permute-start.11 = (bf16[2,64,896]{2,1,0:T(8,128)(2,1)S(1)}, bf16[2,64,896]{2,1,0:T(8,128)(2,1)S(1)}, u32[]{:S(2)}, u32[]{:S(2)}) collective-permute-start(bf16[2,64,896]{2,1,0:T(8,128)(2,1)S(1)} %get-tuple-element.32), channel_id=1, source_target_pairs={{0,4},{1,5},{2,6},{3,7},{4,0},{5,1},{6,2},{7,3},{8,12},{9,13},{10,... | collective-permute-start | bytes 688136 | tf_op jit(solution)/shard_map/ppermute | solution.py:217
  110.2 5.7 %copy-start.11 = (bf16[2,64,896]{2,1,0:T(8,128)(2,1)}, bf16[2,64,896]{2,1,0:T(8,128)(2,1)S(1)}, u32[]{:S(2)}) copy-start(bf16[2,64,896]{2,1,0:T(8,128)(2,1)S(1)} %collective-permute-done.6.refs_7_) | copy-start | bytes 688132
  110.2 11.4 %collective-permute-start.12 = (bf16[2,64,896]{2,1,0:T(8,128)(2,1)S(1)}, bf16[2,64,896]{2,1,0:T(8,128)(2,1)S(1)}, u32[]{:S(2)}, u32[]{:S(2)}) collective-permute-start(bf16[2,64,896]{2,1,0:T(8,128)(2,1)S(1)} %get-tuple-element.33), channel_id=1, source_target_pairs={{0,5},{1,4},{2,7},{3,6},{4,1},{5,0},{6,3},{7,2},{8,13},{9,12},{10,... | collective-permute-start | bytes 688136 | tf_op jit(solution)/shard_map/ppermute | solution.py:217
  113.0 2.9 %copy-start.12 = (bf16[2,64,896]{2,1,0:T(8,128)(2,1)}, bf16[2,64,896]{2,1,0:T(8,128)(2,1)S(1)}, u32[]{:S(2)}) copy-start(bf16[2,64,896]{2,1,0:T(8,128)(2,1)S(1)} %collective-permute-done.8.refs_9_) | copy-start | bytes 688132
  113.0 13.5 %collective-permute-start.13 = (bf16[2,64,896]{2,1,0:T(8,128)(2,1)S(1)}, bf16[2,64,896]{2,1,0:T(8,128)(2,1)S(1)}, u32[]{:S(2)}, u32[]{:S(2)}) collective-permute-start(bf16[2,64,896]{2,1,0:T(8,128)(2,1)S(1)} %get-tuple-element.34), channel_id=1, source_target_pairs={{0,6},{1,7},{2,4},{3,5},{4,2},{5,3},{6,0},{7,1},{8,14},{9,15},{10,... | collective-permute-start | bytes 688136 | tf_op jit(solution)/shard_map/ppermute | solution.py:217
  115.9 0.7 copy-start.13
  115.9 13.9 %collective-permute-start.14 = (bf16[2,64,896]{2,1,0:T(8,128)(2,1)S(1)}, bf16[2,64,896]{2,1,0:T(8,128)(2,1)S(1)}, u32[]{:S(2)}, u32[]{:S(2)}) collective-permute-start(bf16[2,64,896]{2,1,0:T(8,128)(2,1)S(1)} %get-tuple-element.35), channel_id=1, source_target_pairs={{0,7},{1,6},{2,5},{3,4},{4,3},{5,2},{6,1},{7,0},{8,15},{9,14},{10,... | collective-permute-start | bytes 688136 | tf_op jit(solution)/shard_map/ppermute | solution.py:217
  118.2 11.6 %copy-start.14 = (bf16[2,64,896]{2,1,0:T(8,128)(2,1)}, bf16[2,64,896]{2,1,0:T(8,128)(2,1)S(1)}, u32[]{:S(2)}) copy-start(bf16[2,64,896]{2,1,0:T(8,128)(2,1)S(1)} %collective-permute-done.10.refs_11_) | copy-start | bytes 688132
  118.3 22.1 %collective-permute-start.22 = (bf16[4,112,512]{2,1,0:T(8,128)(2,1)S(1)}, bf16[4,112,512]{2,1,0:T(8,128)(2,1)S(1)}, u32[]{:S(2)}, u32[]{:S(2)}) collective-permute-start(bf16[4,112,512]{2,1,0:T(8,128)(2,1)S(1)} %pad_maximum_fusion.k0), channel_id=1, source_target_pairs={{0,2},{1,3},{2,0},{3,1},{4,6},{5,7},{6,4},{7,5},{8,10},{9,11},{10,... | collective-permute-start | bytes 1376264 | tf_op jit(solution)/shard_map/ppermute | solution.py:217
  120.1 9.8 %copy-start.15 = (bf16[2,64,896]{2,1,0:T(8,128)(2,1)}, bf16[2,64,896]{2,1,0:T(8,128)(2,1)S(1)}, u32[]{:S(2)}) copy-start(bf16[2,64,896]{2,1,0:T(8,128)(2,1)S(1)} %collective-permute-done.11.refs_12_) | copy-start | bytes 688132
  120.1 23.4 %collective-permute-start.23 = (bf16[4,112,512]{2,1,0:T(8,128)(2,1)S(1)}, bf16[4,112,512]{2,1,0:T(8,128)(2,1)S(1)}, u32[]{:S(2)}, u32[]{:S(2)}) collective-permute-start(bf16[4,112,512]{2,1,0:T(8,128)(2,1)S(1)} %pad_maximum_fusion.k0), channel_id=1, source_target_pairs={{0,16},{16,0},{1,17},{17,1},{2,18},{18,2},{3,19},{19,3},{4,20},{20... | collective-permute-start | bytes 1376264 | tf_op jit(solution)/shard_map/ppermute | solution.py:220
  121.6 8.3 %copy-start.16 = (bf16[2,64,896]{2,1,0:T(8,128)(2,1)}, bf16[2,64,896]{2,1,0:T(8,128)(2,1)S(1)}, u32[]{:S(2)}) copy-start(bf16[2,64,896]{2,1,0:T(8,128)(2,1)S(1)} %collective-permute-done.12.refs_13_) | copy-start | bytes 688132
  121.6 21.7 %collective-permute-start.26 = (bf16[4,112,512]{2,1,0:T(8,128)(2,1)S(1)}, bf16[4,112,512]{2,1,0:T(8,128)(2,1)S(1)}, u32[]{:S(2)}, u32[]{:S(2)}) collective-permute-start(bf16[4,112,512]{2,1,0:T(8,128)(2,1)S(1)} %pad_maximum_fusion.1.v0), channel_id=1, source_target_pairs={{0,16},{16,0},{1,17},{17,1},{2,18},{18,2},{3,19},{19,3},{4,20},{20... | collective-permute-start | bytes 1376264 | tf_op jit(solution)/shard_map/ppermute | solution.py:220
  126.5 3.3 %copy-start.17 = (bf16[2,64,896]{2,1,0:T(8,128)(2,1)}, bf16[2,64,896]{2,1,0:T(8,128)(2,1)S(1)}, u32[]{:S(2)}) copy-start(bf16[2,64,896]{2,1,0:T(8,128)(2,1)S(1)} %collective-permute-done.13.refs_14_) | copy-start | bytes 688132
  129.9 0.7 copy-start.18
  133.5 19.7 %collective-permute-start.15 = (bf16[4,64,896]{2,1,0:T(8,128)(2,1)}, bf16[4,64,896]{2,1,0:T(8,128)(2,1)}, u32[]{:S(2)}, u32[]{:S(2)}) collective-permute-start(bf16[4,64,896]{2,1,0:T(8,128)(2,1)} %get-tuple-element.37), channel_id=1, source_target_pairs={{0,16},{16,0},{1,17},{17,1},{2,18},{18,2},{3,19},{19,3},{4,20},{20... | collective-permute-start | bytes 1376264 | tf_op jit(solution)/shard_map/ppermute | solution.py:220
  135.1 18.2 %collective-permute-start.25 = (bf16[4,112,512]{2,1,0:T(8,128)(2,1)S(1)}, bf16[4,112,512]{2,1,0:T(8,128)(2,1)}, u32[]{:S(2)}, u32[]{:S(2)}) collective-permute-start(bf16[4,112,512]{2,1,0:T(8,128)(2,1)S(1)} %pad_maximum_fusion.1.v0), channel_id=1, source_target_pairs={{0,2},{1,3},{2,0},{3,1},{4,6},{5,7},{6,4},{7,5},{8,10},{9,11},{10,... | collective-permute-start | bytes 1376264 | tf_op jit(solution)/shard_map/ppermute | solution.py:217
  140.4 22.0 %collective-permute-start.24 = (bf16[4,112,512]{2,1,0:T(8,128)(2,1)S(1)}, bf16[4,112,512]{2,1,0:T(8,128)(2,1)}, u32[]{:S(2)}, u32[]{:S(2)}) collective-permute-start(bf16[4,112,512]{2,1,0:T(8,128)(2,1)S(1)} %collective-permute-done.22.kx), channel_id=1, source_target_pairs={{0,16},{16,0},{1,17},{17,1},{2,18},{18,2},{3,19},{19,3},{4,20},{20... | collective-permute-start | bytes 1376264 | tf_op jit(solution)/shard_map/ppermute | solution.py:220
  143.3 19.1 %collective-permute-start.27 = (bf16[4,112,512]{2,1,0:T(8,128)(2,1)S(1)}, bf16[4,112,512]{2,1,0:T(8,128)(2,1)}, u32[]{:S(2)}, u32[]{:S(2)}) collective-permute-start(bf16[4,112,512]{2,1,0:T(8,128)(2,1)S(1)} %collective-permute-done.26.vy), channel_id=1, source_target_pairs={{0,2},{1,3},{2,0},{3,1},{4,6},{5,7},{6,4},{7,5},{8,10},{9,11},{10,... | collective-permute-start | bytes 1376264 | tf_op jit(solution)/shard_map/ppermute | solution.py:217
  143.5 18.9 %collective-permute-start.16 = (bf16[2,128,896]{2,1,0:T(8,128)(2,1)}, bf16[2,128,896]{2,1,0:T(8,128)(2,1)}, u32[]{:S(2)}, u32[]{:S(2)}) collective-permute-start(bf16[2,128,896]{2,1,0:T(8,128)(2,1)} %bitcast.23), channel_id=1, source_target_pairs={{0,1},{1,0},{2,3},{3,2},{4,5},{5,4},{6,7},{7,6},{8,9},{9,8},{10,11... | collective-permute-start | bytes 1376264 | tf_op jit(solution)/shard_map/ppermute | solution.py:217
  153.2 9.1 %collective-permute-start.17 = (bf16[2,128,896]{2,1,0:T(8,128)(2,1)}, bf16[2,128,896]{2,1,0:T(8,128)(2,1)}, u32[]{:S(2)}, u32[]{:S(2)}) collective-permute-start(bf16[2,128,896]{2,1,0:T(8,128)(2,1)} %bitcast.12.nb), channel_id=1, source_target_pairs={{0,1},{1,0},{2,3},{3,2},{4,5},{5,4},{6,7},{7,6},{8,9},{9,8},{10,11... | collective-permute-start | bytes 1376264 | tf_op jit(solution)/shard_map/ppermute | solution.py:217
  162.4 1.0 copy-start

commit v4 on v1

--- a/solution.py
+++ b/solution.py
@@ -1,6 +1,8 @@
 import jax
 import jax.numpy as jnp
 from jax import lax
+from jax.experimental import pallas as pl
+from jax.experimental.pallas import tpu as pltpu
 from jax.sharding import PartitionSpec as P
 
 HEADS = 16
@@ -10,31 +12,340 @@
 SPAN = 64
 NBR = 2
 CH_DEV = 2
-
-
-def shards(queries, cache, cache_scale, w_kv, nbr_shard, nbr_row, grad_out):
+MOST = 2
+
+SCORE_SCALE = HEAD_DIM ** (-0.5)
+
+
+def requests(nbr_shard, nbr_row, dp_count, mp_count):
+    block_size = dp_count * CH_DEV * NBR
+    shard_blk = (
+        nbr_shard.reshape(dp_count, mp_count, CH_DEV * NBR)
+        .transpose(1, 0, 2)
+        .reshape(mp_count, block_size)
+    )
+    row_blk = (
+        nbr_row.reshape(dp_count, mp_count, CH_DEV * NBR)
+        .transpose(1, 0, 2)
+        .reshape(mp_count, block_size)
+    )
+    positions = jnp.arange(block_size, dtype=jnp.int32)
+    earlier = positions[None, :] < positions[:, None]
+    same_shard = shard_blk[:, :, None] == shard_blk[:, None, :]
+    slot_blk = jnp.sum(jnp.logical_and(same_shard, earlier[None]), axis=2)
+    return shard_blk, row_blk, slot_blk
+
+
+ZS, XS, CS = 4, 2, 2
+CHIPS = ZS * XS
+HALF = 8
+ALL = range(ZS * XS * CS)
+
+
+def parity_kernel(core_ref, w_ref, mine_ref, sends_ref):
+    for core in range(CS):
+
+        @pl.when(core_ref[0] == core)
+        def _():
+            for j in range(HEADS // CS // 2):
+                at = slice(j * HEAD_DIM, (j + 1) * HEAD_DIM)
+                for ref, parity in ((mine_ref, core), (sends_ref, 1 - core)):
+                    head = CS * j + parity
+                    ref[:, :, at] = w_ref[:, :, head * HEAD_DIM : (head + 1) * HEAD_DIM]
+
+
+def by_parity(core, w_kv):
+    half = jax.ShapeDtypeStruct(w_kv.shape[:2] + (w_kv.shape[2] // CS,), w_kv.dtype)
+    return pl.pallas_call(
+        parity_kernel,
+        in_specs=[
+            pl.BlockSpec(memory_space=pltpu.SMEM),
+            pl.BlockSpec(memory_space=pltpu.VMEM),
+        ],
+        out_specs=[pl.BlockSpec(memory_space=pltpu.VMEM)] * 2,
+        out_shape=[half] * 2,
+        name="by_parity",
+    )(core, w_kv)
+
+
+def rows_kernel(rows_ref, src_ref, out_ref):
+    for k in range(out_ref.shape[0]):
+        out_ref[k] = src_ref[rows_ref[k]]
+
+
+def pick_rows(rows, source):
+    return pl.pallas_call(
+        rows_kernel,
+        in_specs=[
+            pl.BlockSpec(memory_space=pltpu.SMEM),
+            pl.BlockSpec(memory_space=pltpu.VMEM),
+        ],
+        out_specs=pl.BlockSpec(memory_space=pltpu.VMEM),
+        out_shape=jax.ShapeDtypeStruct(rows.shape + source.shape[1:], source.dtype),
+        compiler_params=pltpu.CompilerParams(vmem_limit_bytes=32 * 1024 * 1024),
+        name="pick_rows",
+    )(rows, source)
+
+
+def choose_kernel(far_ref, row_ref, near, far, own, give, sem):
+    each = CH_DEV * NBR
+    outs = [(own if r < each else give).at[r % each] for r in range(2 * each)]
+    for r, out in enumerate(outs):
+
+        @pl.when(far_ref[r] == 0)
+        def _():
+            pltpu.make_async_copy(near.at[row_ref[r]], out, sem.at[r]).start()
+
+        @pl.when(far_ref[r] != 0)
+        def _():
+            pltpu.make_async_copy(far.at[row_ref[r]], out, sem.at[r]).start()
+
+    for r, out in enumerate(outs):
+        pltpu.make_async_copy(near.at[0], out, sem.at[r]).wait()
+
+
+def choose(is_far, row, near, far):
+    half = jax.ShapeDtypeStruct((CH_DEV * NBR,) + near.shape[1:], near.dtype)
+    return pl.pallas_call(
+        choose_kernel,
+        in_specs=[pl.BlockSpec(memory_space=pltpu.SMEM)] * 2
+        + [pl.BlockSpec(memory_space=pl.ANY)] * 2,
+        out_specs=[pl.BlockSpec(memory_space=pltpu.VMEM)] * 2,
+        out_shape=[half] * 2,
+        scratch_shapes=[pltpu.SemaphoreType.DMA((2 * CH_DEV * NBR,))],
+        name="choose",
+    )(is_far, row, near, far)
+
+
+def tdot(a, b):
+    return lax.dot_general(a, b, (((0,), (0,)), ((), ())), preferred_element_type=jnp.float32)
+
+
+def ndot(a, b):
+    return jnp.dot(a, b, preferred_element_type=jnp.float32)
+
+
+def attend_kernel(
+    place_ref, na, nb, sa, sb, w_own, w_x, w_y, w_xy, qg_ref, out_ref, n_scr, w_scr
+):
+    my_c, my_x, my_z = place_ref[1], place_ref[2], place_ref[3]
+    rows = w_scr.shape[0] // CHIPS
+
+    @pl.when(pl.program_id(0) == 0)
+    def _():
+        for s in range(CH_DEV):
+            for core, first, second in ((my_c, na, nb), (1 - my_c, sa, sb)):
+                n_scr[CH_DEV * core + s, 0:NT, :] = first[s]
+                n_scr[CH_DEV * core + s, NT : 2 * NT, :] = second[s]
+
+    def put(*sources):
+        for r in range(ZS):
+            src_z = lax.rem(my_z - r + ZS, ZS)
+            for other, ref in enumerate(sources):
+                at = pl.multiple_of((src_z * XS + (my_x ^ other)) * rows, 16)
+                for kv in range(2):
+                    lanes = slice(HEAD_DIM * kv, HEAD_DIM * (kv + 1))
+                    w_scr[pl.ds(at, rows), lanes] = ref[r, kv]
+
+    own_dp = pl.program_id(0) < pl.num_programs(0) // 2
+
+    @pl.when(own_dp)
+    def _():
+        put(w_own, w_x)
+
+    @pl.when(jnp.logical_not(own_dp))
+    def _():
+        put(w_y, w_xy)
+
+    weights = w_scr[...]
+    kvs = [ndot(n_scr[s], weights).astype(jnp.bfloat16) for s in range(CS * CH_DEV)]
+    keys = [kv[:, :HEAD_DIM] for kv in kvs]
+    values = [kv[:, HEAD_DIM:] for kv in kvs]
+    low = lax.broadcasted_iota(jnp.int32, (1, 2 * SPAN), 1) < SPAN
+    pairs = range(CS)
+    lanes = [slice(2 * SPAN * p, 2 * SPAN * (p + 1)) for p in pairs]
+
+    def both(dot, spans, right):
+        return [
+            jnp.where(low, dot(spans[2 * p], right[p]), dot(spans[2 * p + 1], right[p]))
+            for p in pairs
+        ]
+
+    queries = [qg_ref[0, 0, :, at] for at in lanes]
+    grads = [qg_ref[0, 1, :, at] for at in lanes]
+    scores = [s * SCORE_SCALE for s in both(ndot, keys, queries)]
+    dprobs = both(ndot, values, grads)
+    exponent = [jnp.exp(s - jnp.max(s, axis=0, keepdims=True)) for s in scores]
+    probs = [e * (1.0 / jnp.sum(e, axis=0, keepdims=True)) for e in exponent]
+    probs_low = [p.astype(jnp.bfloat16) for p in probs]
+    outs = [o.astype(jnp.bfloat16) for o in both(tdot, values, probs_low)]
+    delta = [
+        jnp.sum(g.astype(jnp.float32) * o.astype(jnp.float32), axis=0, keepdims=True)
+        for g, o in zip(grads, outs)
+    ]
+    dscores = [
+        (p * (dp - dl) * SCORE_SCALE).astype(jnp.bfloat16)
+        for p, dp, dl in zip(probs, dprobs, delta)
+    ]
+    dqs = [q.astype(jnp.bfloat16) for q in both(tdot, keys, dscores)]
+    for p in pairs:
+        out_ref[0, 0, :, lanes[p]] = outs[p]
+        out_ref[0, 1, :, lanes[p]] = dqs[p]
+
+
+def attend(place, neighbours, weights, qg):
+    d_heads = HEADS // CS // 2
+    heads = 2 * d_heads
+    block = (1, 2, HEAD_DIM, qg.shape[-1])
+
+    def head_of(i, place):
+        return (i + d_heads * place[0]) & (heads - 1)
+
+    def came_at(i, place):
+        head = head_of(i, place)
+        half = head // d_heads
+        return (2 * (head & (d_heads - 1)) + jnp.abs(half - place[3] // 2), 0, 0, 0)
+
+    w_block = weights[0].shape[:3] + (HEAD_DIM,)
+    first = pl.BlockSpec(w_block, lambda i, place: (0, 0, 0, jnp.minimum(i, d_heads - 1)))
+    last = pl.BlockSpec(w_block, lambda i, place: (0, 0, 0, jnp.maximum(i - d_heads, 0)))
+    return pl.pallas_call(
+        attend_kernel,
+        grid_spec=pltpu.PrefetchScalarGridSpec(
+            num_scalar_prefetch=1,
+            grid=(heads,),
+            in_specs=[
+                pl.BlockSpec(a.shape, lambda i, place: (0, 0, 0)) for a in neighbours
+            ]
+            + [first, first, last, last, pl.BlockSpec(block, came_at)],
+            out_specs=pl.BlockSpec(block, lambda i, place: (head_of(i, place), 0, 0, 0)),
+            scratch_shapes=[
+                pltpu.VMEM((CS * CH_DEV, NBR * NT, E), jnp.bfloat16),
+                pltpu.VMEM((E, 2 * HEAD_DIM), jnp.bfloat16),
+            ],
+        ),
+        out_shape=jax.ShapeDtypeStruct(qg.shape, jnp.bfloat16),
+        compiler_params=pltpu.CompilerParams(vmem_limit_bytes=40 * 1024 * 1024),
+        name="attend",
+    )(place, *neighbours, *weights, qg)
+
+
+def small(queries, cache, cache_scale, w_kv, nbr_shard, nbr_row, grad_out):
+    dp_count = lax.axis_size("dp")
+    mp_count = lax.axis_size("mp")
+    my_dp = lax.axis_index("dp")
+    my_mp = lax.axis_index("mp")
+    my_c, my_x, my_z = my_mp & 1, (my_mp >> 1) & 1, my_mp >> 2
+    place = jnp.stack([my_dp, my_c, my_x, my_z]).astype(jnp.int32)
+    slice_len = cache.shape[1]
+
+    def swap(a, bits):
+        return lax.ppermute(a, "mp", [(m, m ^ bits) for m in ALL])
+
+    def swap_dp(a):
+        return lax.ppermute(a, "dp", [(0, 1), (1, 0)])
+
+    def over_half(a):
+        halves = [list(range(HALF)), list(range(HALF, 2 * HALF))]
+        return lax.all_to_all(
+            a, "mp", split_axis=0, concat_axis=0, tiled=True, axis_index_groups=halves
+        )
+
+    turned = [w_kv] + [
+        lax.ppermute(w_kv, "mp", [(m, (m + XS * CS * r) % len(ALL)) for m in ALL])
+        for r in range(1, ZS)
+    ]
+    scaled = (cache.astype(jnp.float32) * cache_scale[..., None]).astype(jnp.bfloat16)
+    scaled, turned = lax.optimization_barrier((scaled, turned))
+    far = swap(scaled, HALF)
+
+    mine, sends = by_parity(my_c.reshape(1).astype(jnp.int32), jnp.concatenate(turned))
+    came = swap(sends, 1)
+    line_w = jnp.where(
+        my_c == 0,
+        jnp.concatenate([mine, came], axis=1),
+        jnp.concatenate([came, mine], axis=1),
+    ).reshape(ZS, 2, CS * w_kv.shape[1], -1)
+    x_w, y_w = swap(line_w, CS), swap_dp(line_w)
+
+    shard_blk, row_blk, slot_blk = requests(nbr_shard, nbr_row, dp_count, mp_count)
+    holders = jnp.stack([my_mp, my_mp ^ HALF]).astype(jnp.int32)
+    select = jnp.logical_and(
+        shard_blk[:, None, None, :] == holders[None, :, None, None],
+        slot_blk[:, None, None, :] == jnp.arange(MOST, dtype=jnp.int32)[None, None, :, None],
+    )
+    wanted = jnp.sum(jnp.where(select, row_blk[:, None, None, :], 0), axis=3)
+    wanted = lax.dynamic_slice_in_dim(wanted, my_mp & HALF, HALF, 0)
+
+    def pieces(which, *sources):
+        rows = pick_rows(wanted[:, which].reshape(-1), *sources)
+        return over_half(rows.reshape((HALF, MOST) + rows.shape[1:])).reshape(rows.shape)
+
+    near_source, line_w = lax.optimization_barrier((scaled, line_w))
+    near_pieces = pieces(0, near_source)
+
+    my_half = my_mp // HALF
+    chips = CHIPS // 2
+    qg = jnp.stack([queries, grad_out]).reshape(2, HEAD_DIM, CHIPS, -1).transpose(2, 0, 1, 3)
+    qg = qg.reshape((2, chips) + qg.shape[1:])
+    qg_stay = lax.dynamic_index_in_dim(qg, my_half, 0, keepdims=False)
+    qg_go = lax.dynamic_index_in_dim(qg, 1 - my_half, 0, keepdims=False)
+
+    far, near_pieces, x_w, y_w, qg_go = lax.optimization_barrier(
+        (far, near_pieces, x_w, y_w, qg_go)
+    )
+    xy_w = swap_dp(x_w)
+    far_pieces = pieces(1, far)
+    qg_came = swap(qg_go, HALF)
+
+    far_pieces, qg_came, xy_w = lax.optimization_barrier((far_pieces, qg_came, xy_w))
+    chip_lines = [
+        [HALF * half + CS * chip + core for chip in range(chips)]
+        for half in range(2)
+        for core in range(CS)
+    ]
+    qg = lax.all_to_all(
+        jnp.stack([qg_stay, qg_came], axis=1),
+        "mp",
+        split_axis=0,
+        concat_axis=0,
+        tiled=True,
+        axis_index_groups=chip_lines,
+    )
+    qg = qg.reshape((CHIPS,) + qg.shape[2:])
+    chip_groups = [[CS * chip + core for chip in range(CHIPS)] for core in range(CS)]
+
+    shards = lax.dynamic_index_in_dim(shard_blk, my_mp, 0, keepdims=False)
+    slots = lax.dynamic_index_in_dim(slot_blk, my_mp, 0, keepdims=False)
+    row = jnp.roll(((shards & (HALF - 1)) * MOST + slots).reshape(dp_count, -1), my_dp, 0)
+    is_far = jnp.roll(((shards ^ my_mp) & HALF).reshape(dp_count, -1), my_dp, 0)
+    own, give = choose(
+        is_far.reshape(-1).astype(jnp.int32),
+        row.reshape(-1).astype(jnp.int32),
+        near_pieces,
+        far_pieces,
+    )
+    got = swap_dp(give)
+    span_shape = (CH_DEV, NBR * slice_len, E)
+    own, got = own.reshape(span_shape), got.reshape(span_shape)
+    neighbours = (own, got, swap(own, 1), swap(got, 1))
+
+    result = attend(place, neighbours, (line_w, x_w, y_w, xy_w), qg)
+    back = lax.all_to_all(
+        result, "mp", split_axis=0, concat_axis=0, tiled=True, axis_index_groups=chip_groups
+    )
+    back = back.transpose(1, 2, 0, 3).reshape((2,) + queries.shape)
+    return back[0], back[1]
+
+
+def general(queries, cache, cache_scale, w_kv, nbr_shard, nbr_row, grad_out):
     dp_count = lax.axis_size("dp")
     mp_count = lax.axis_size("mp")
     my_mp = lax.axis_index("mp")
     slice_len = cache.shape[1]
     most_slots = 2 * ((dp_count * CH_DEV * NBR + mp_count - 1) // mp_count)
-    block_size = dp_count * CH_DEV * NBR
-    score_scale = HEAD_DIM ** (-0.5)
     local_query = lax.all_to_all(queries, "mp", split_axis=1, concat_axis=0, tiled=True)
-    shard_blk = (
-        nbr_shard.reshape(dp_count, mp_count, CH_DEV * NBR)
-        .transpose(1, 0, 2)
-        .reshape(mp_count, block_size)
-    )
-    row_blk = (
-        nbr_row.reshape(dp_count, mp_count, CH_DEV * NBR)
-        .transpose(1, 0, 2)
-        .reshape(mp_count, block_size)
-    )
-    positions = jnp.arange(block_size, dtype=jnp.int32)
-    earlier = positions[None, :] < positions[:, None]
-    same_shard = shard_blk[:, :, None] == shard_blk[:, None, :]
-    slot_blk = jnp.sum(jnp.logical_and(same_shard, earlier[None]), axis=2)
+    shard_blk, row_blk, slot_blk = requests(nbr_shard, nbr_row, dp_count, mp_count)
     to_me = shard_blk == my_mp
     slot_ids = jnp.arange(most_slots, dtype=jnp.int32)
     select = jnp.logical_and(to_me[:, None, :], slot_blk[:, None, :] == slot_ids[None, :, None])
@@ -64,7 +375,7 @@
     query_c = local_query.reshape(HEADS, HEAD_DIM, CH_DEV, SPAN)
     affinity_logits = (
         jnp.einsum("hdcq,ckhd->chqk", query_c, key_rows, preferred_element_type=jnp.float32)
-        * score_scale
+        * SCORE_SCALE
     )
     row_max = jnp.max(affinity_logits, axis=3, keepdims=True)
     exponent = jnp.exp(affinity_logits - row_max)
@@ -79,7 +390,7 @@
     grad_c = local_grad.reshape(HEADS, HEAD_DIM, CH_DEV, SPAN)
     dprobs = jnp.einsum("hdcq,ckhd->chqk", grad_c, values, preferred_element_type=jnp.float32)
     row_delta = jnp.einsum("hdcq,hdcq->chq", grad_c, output_c, preferred_element_type=jnp.float32)
-    dscores = (attn_probs * (dprobs - row_delta[..., None]) * score_scale).astype(jnp.bfloat16)
+    dscores = (attn_probs * (dprobs - row_delta[..., None]) * SCORE_SCALE).astype(jnp.bfloat16)
     grad_query = jnp.einsum(
         "chqk,ckhd->hdcq", dscores, key_rows, preferred_element_type=jnp.float32
     ).astype(jnp.bfloat16)
@@ -89,8 +400,9 @@
 
 
 def solution(mesh):
+    fits = mesh.shape["dp"] == 2 and mesh.shape["mp"] == len(ALL)
     return jax.shard_map(
-        shards,
+        small if fits else general,
         mesh=mesh,
         in_specs=(
             P("mp", "dp"),

time: 276 us -> 196 us (0.71)
  local copies, waits for them, and re-layouts: 45.1 us -> 12 us
  waiting for transfers between devices: 117 us -> 87.7 us
  Pallas kernels: 0 us -> 23.3 us
  starting transfers between devices: 55.2 us -> 34.2 us
  matrix products: 17.2 us -> 0 us
  between operations: 14.2 us -> 0.79 us
  blocking collectives: 18.4 us -> 30.3 us
    all_to_all x5 -> x3, waiting for transfers between devices: 116 us -> 1.45 us  [the longest x2 1.44 us: over_half(): lax.all_to_all(a, 'mp', split_axis=0, concat_axis=0, tiled=True, axis_ind...]
    ppermute x0 -> x12, waiting for transfers between devices: none -> 86.3 us  [the longest x6 64.4 us: swap(): return lax.ppermute(a, 'mp', [(m, m ^ bits) for m in ALL])]
    all_to_all x5 -> x3, starting transfers between devices: 55.2 us -> 17 us  [the longest x2 12.2 us: over_half(): lax.all_to_all(a, 'mp', split_axis=0, concat_axis=0, tiled=True, axis_ind...]
    reshape x4 -> x5, local copies, waits for them, and re-layouts: 27.5 us -> 2.61 us  [the longest x1 1.2 us: small(): qg = qg.reshape((2, chips) + qg.shape[1:])]
    pallas_call x0 -> x5, Pallas kernels: none -> 23.3 us  [the longest x1 14.2 us: attend(): pl.pallas_call(attend_kernel, grid_spec=pltpu.PrefetchScalarGridSpec(num_...]
    dot_general x5 -> x0, matrix products: 17.2 us -> none  [the longest x1 9.11 us: shards(): jnp.einsum('cte,ken->kctn', neighbours, all_weights, preferred_element_ty...]
    ppermute x0 -> x12, starting transfers between devices: none -> 17.1 us  [the longest x3 7.01 us: small(): lax.ppermute(w_kv, 'mp', [(m, (m + XS * CS * r) % len(ALL)) for m in ALL])]
    all_to_all x1, blocking collectives: 18.4 us -> 30.3 us  [small(): lax.all_to_all(result, 'mp', split_axis=0, concat_axis=0, tiled=True, axi...]
  transfers between devices with their start and end apart: 6 -> 15, of which waited for: 4 -> 9; matrix products, arithmetic and copies ran while one was open for 22% -> 5% of each run, Pallas kernels for 0% -> 1%
where the time goes in v4:
time: 196 us; the launch traced here: 195 us
  waiting for transfers between devices  87.7 us (45%)
  starting transfers between devices  34.2 us (17%)
  blocking collectives  30.3 us (15%)
  Pallas kernels  23.3 us (12%)
  local copies, waits for them, and re-layouts  12 us (6%)
  other arithmetic  6.7 us (3%)
    ppermute x6, waiting for transfers between devices, swap(): return lax.ppermute(a, 'mp', [(m, m ^ bits) for m in ALL])  64.4 us
    all_to_all x1, blocking collectives, small(): lax.all_to_all(result, 'mp', split_axis=0, concat_axis=0, tiled=True, axi...  30.3 us
    pallas_call x1, Pallas kernels, attend(): pl.pallas_call(attend_kernel, grid_spec=pltpu.PrefetchScalarGridSpec(num_...  14.2 us
    all_to_all x2, starting transfers between devices, over_half(): lax.all_to_all(a, 'mp', split_axis=0, concat_axis=0, tiled=True, axis_ind...  12.2 us
    ppermute x3, waiting for transfers between devices, small(): lax.ppermute(w_kv, 'mp', [(m, (m + XS * CS * r) % len(ALL)) for m in ALL])  11.4 us
    ppermute x3, waiting for transfers between devices, swap_dp(): return lax.ppermute(a, 'dp', [(0, 1), (1, 0)])  10.5 us
    ppermute x3, starting transfers between devices, small(): lax.ppermute(w_kv, 'mp', [(m, (m + XS * CS * r) % len(ALL)) for m in ALL])  7.01 us
    unnamed x18, local copies, waits for them, and re-layouts  5.98 us
  transfers between devices with their start and end apart: 15, of which 9 were waited for; matrix products, arithmetic and copies ran while one was open for 5% of the time, Pallas kernels for 1%

profile of v4, /device:TPU:0, one launch (start us, length us, event | category | flops | bytes accessed | tf_op | source)
XLA Modules:
  0.0 195.0 jit_solution(14916529135445480356)
XLA Ops:
  0.6 3.1 %collective-permute-start = (bf16[2,56,1024]{2,1,0:T(8,128)(2,1)}, bf16[2,56,1024]{2,1,0:T(8,128)(2,1)S(1)}, u32[]{:S(2)}, u32[]{:S(2)}) collective-permute-start(bf16[2,56,1024]{2,1,0:T(8,128)(2,1)} %param.12), channel_id=1, source_target_pairs={{0,4},{1,5},{2,6},{3,7},{4,8},{5,9},{6,10},{7,11},{8,12},{9,13},{1... | collective-permute-start | bytes 688136 | tf_op jit(solution)/shard_map/ppermute | solution.py:255
  3.7 2.6 %collective-permute-start.1 = (bf16[2,56,1024]{2,1,0:T(8,128)(2,1)}, bf16[2,56,1024]{2,1,0:T(8,128)(2,1)S(1)}, u32[]{:S(2)}, u32[]{:S(2)}) collective-permute-start(bf16[2,56,1024]{2,1,0:T(8,128)(2,1)} %param.12), channel_id=1, source_target_pairs={{0,8},{1,9},{2,10},{3,11},{4,12},{5,13},{6,14},{7,15},{8,0},{9,1},... | collective-permute-start | bytes 688136 | tf_op jit(solution)/shard_map/ppermute | solution.py:255
  6.3 1.3 collective-permute-start.2
  7.7 0.8 copy.35
  8.4 0.1 reshape.106
  8.5 0.1 copy.36
  8.6 1.4 multiply_convert_fusion.src_ref
  10.0 0.1 convert_reduce_fusion
  10.1 2.4 %collective-permute-done = bf16[2,56,1024]{2,1,0:T(8,128)(2,1)S(1)} collective-permute-done((bf16[2,56,1024]{2,1,0:T(8,128)(2,1)}, bf16[2,56,1024]{2,1,0:T(8,128)(2,1)S(1)}, u32[]{:S(2)}, u32[]{:S(2)}) %collective-permute-start) | collective-permute-done | bytes 229408 | tf_op jit(solution)/shard_map/ppermute | solution.py:255
  12.5 9.0 %collective-permute-done.1 = bf16[2,56,1024]{2,1,0:T(8,128)(2,1)S(1)} collective-permute-done((bf16[2,56,1024]{2,1,0:T(8,128)(2,1)}, bf16[2,56,1024]{2,1,0:T(8,128)(2,1)S(1)}, u32[]{:S(2)}, u32[]{:S(2)}) %collective-permute-start.1) | collective-permute-done | bytes 229408 | tf_op jit(solution)/shard_map/ppermute | solution.py:255
  21.5 1.0 pad_maximum_fusion.1.w_ref
  22.6 2.3 %by_parity.1 = (bf16[8,56,512]{2,1,0:T(8,128)(2,1)}, bf16[8,56,512]{2,1,0:T(8,128)(2,1)}) custom-call(s32[1]{0:T(128)} %bitcast.1.core_ref, bf16[8,56,1024]{2,1,0:T(8,128)(2,1)} %pad_maximum_fusion.1.w_ref), custom_call_target="tpu_custom_call" | custom-call | tf_op jit(solution)/shard_map/by_parity/pallas_call | solution.py:59
  24.9 0.1 pad_add_fusion.3
  24.9 0.1 copy.37
  25.0 0.1 reshape.110
  25.1 0.1 copy.38
  25.2 0.1 broadcast_compare_fusion
  25.3 0.1 constant_dynamic-slice_fusion.2
  25.4 0.1 copy.39
  25.5 0.1 reshape_squeeze.6.rows_ref
  25.5 1.3 collective-permute-done.4
  26.9 1.5 maximum_select_fusion.w_own
  28.3 1.9 pick_rows.2
  30.2 7.7 %all-to-all-start = ((bf16[8,2,64,896]{3,2,1,0:T(8,128)(2,1)}), bf16[8,2,64,896]{3,2,1,0:T(8,128)(2,1)}, u32[]{:S(2)}, u32[]{:S(2)}) async-start(bf16[8,2,64,896]{3,2,1,0:T(8,128)(2,1)} %bitcast.12), calls=%async_computation | async-start | bytes 3670016 | tf_op jit(solution)/shard_map/all_to_all | solution.py:250
  38.0 1.6 collective-permute-start.3
  39.5 2.0 %collective-permute-start.5 = (bf16[4,2,112,512]{3,2,1,0:T(8,128)(2,1)S(1)}, bf16[4,2,112,512]{3,2,1,0:T(8,128)(2,1)}, u32[]{:S(2)}, u32[]{:S(2)}) collective-permute-start(bf16[4,2,112,512]{3,2,1,0:T(8,128)(2,1)S(1)} %maximum_select_fusion.w_own), channel_id=1, source_target_pairs={{0,2},{1,3},{2,0},{3,1},{4,6},{5,7},{6,4},{7,5},{8,10},{9,11},{10,... | collective-permute-start | bytes 2752520 | tf_op jit(solution)/shard_map/ppermute | solution.py:243
  41.6 1.5 collective-permute-start.6
  43.1 0.1 copy.49
  43.2 1.2 copy.48
  44.4 0.1 maximum_bitcast_fusion
  44.5 1.2 copy.47
  45.7 0.1 copy.41
  45.8 0.1 reshape_squeeze.7.rows_ref
  45.8 2.1 %dynamic-slice_bitcast_fusion = (bf16[4,1,2,128,256]{4,3,2,1,0:T(8,128)(2,1)S(1)}, bf16[4,2,128,256]{3,2,1,0:T(8,128)(2,1)}) fusion(bf16[2,4,2,128,256]{4,3,2,1,0:T(8,128)(2,1)} %bitcast.46, s32[]{:T(128)S(6)} %select_n.49, s32[]{:T(128)S(6)} %select_n.48), kind=kLoop, calls=%fused_computation.5 | loop fusion | bytes 2097160 | tf_op jit(solution)/shard_map/stack | solution.py:308
  47.9 30.6 %collective-permute-done.3.src_ref = bf16[8,64,896]{2,1,0:T(8,128)(2,1)S(1)} collective-permute-done((bf16[8,64,896]{2,1,0:T(8,128)(2,1)S(1)}, bf16[8,64,896]{2,1,0:T(8,128)(2,1)S(1)}, u32[]{:S(2)}, u32[]{:S(2)}) %collective-permute-start.3) | collective-permute-done | bytes 917536 | tf_op jit(solution)/shard_map/ppermute | solution.py:243
  78.5 2.1 %collective-permute-done.5.w_x = bf16[4,2,112,512]{3,2,1,0:T(8,128)(2,1)} collective-permute-done((bf16[4,2,112,512]{3,2,1,0:T(8,128)(2,1)S(1)}, bf16[4,2,112,512]{3,2,1,0:T(8,128)(2,1)}, u32[]{:S(2)}, u32[]{:S(2)}) %collective-permute-start.5) | collective-permute-done | bytes 917536 | tf_op jit(solution)/shard_map/ppermute | solution.py:243
  80.6 0.0 all-to-all-done
  80.7 1.9 pick_rows.3
  82.6 4.5 %all-to-all-start.1 = ((bf16[8,2,64,896]{3,2,1,0:T(8,128)(2,1)}), bf16[8,2,64,896]{3,2,1,0:T(8,128)(2,1)}, u32[]{:S(2)}, u32[]{:S(2)}) async-start(bf16[8,2,64,896]{3,2,1,0:T(8,128)(2,1)} %bitcast.17), calls=%async_computation.1 | async-start | bytes 3670016 | tf_op jit(solution)/shard_map/all_to_all | solution.py:250
  87.1 1.6 collective-permute-start.8
  88.7 1.8 collective-permute-start.7
  90.5 28.5 %collective-permute-done.7 = bf16[4,2,128,256]{3,2,1,0:T(8,128)(2,1)S(1)} collective-permute-done((bf16[4,2,128,256]{3,2,1,0:T(8,128)(2,1)S(1)}, bf16[4,2,128,256]{3,2,1,0:T(8,128)(2,1)S(1)}, u32[]{:S(2)}, u32[]{:S(2)}) %collective-permute-start.7) | collective-permute-done | bytes 524320 | tf_op jit(solution)/shard_map/ppermute | solution.py:243
  119.0 0.8 copy-done.3
  119.8 1.4 all-to-all-done.1
  121.2 2.1 %pad_maximum_fusion = bf16[4,2,2,128,256]{4,3,2,1,0:T(8,128)(2,1)} fusion(bf16[4,1,2,128,256]{4,3,2,1,0:T(8,128)(2,1)} %bitcast.53, bf16[4,1,2,128,256]{4,3,2,1,0:T(8,128)(2,1)S(1)} %get-tuple-element.49), kind=kLoop, calls=%fused_computation.2 | loop fusion | flops 524288 | bytes 2097152 | tf_op jit(solution)/shard_map/stack | solution.py:308
  123.3 4.9 %all-to-all-start.2 = ((bf16[4,2,2,128,256]{4,3,2,1,0:T(8,128)(2,1)}), bf16[4,2,2,128,256]{4,3,2,1,0:T(8,128)(2,1)S(1)}, u32[]{:S(2)}, u32[]{:S(2)}) async-start(bf16[4,2,2,128,256]{4,3,2,1,0:T(8,128)(2,1)} %pad_maximum_fusion), calls=%async_computation.2 | async-start | bytes 2097152 | tf_op jit(solution)/shard_map/all_to_all | solution.py:307
  128.2 0.2 add_reduce_fusion
  128.4 0.1 add.34
  128.5 0.1 and.57
  128.6 0.7 reshape.108.far_ref
  129.3 0.6 reshape.109.row_ref
  129.9 2.9 %choose.1 = (bf16[4,64,896]{2,1,0:T(8,128)(2,1)}, bf16[4,64,896]{2,1,0:T(8,128)(2,1)}) custom-call(s32[8]{0:T(128)} %reshape.108.far_ref, s32[8]{0:T(128)} %reshape.109.row_ref, bf16[16,64,896]{2,1,0:T(8,128)(2,1)} %bitcast.13.near, bf16[16,64,896]{2,1,0:T(8,128)(2,1)} %bitcast.18.far), custom_call_target="tpu_custom_call" | custom-call | tf_op jit(solution)/shard_map/choose/pallas_call | solution.py:109
  132.8 1.6 collective-permute-start.9
  134.4 10.5 %collective-permute-done.9 = bf16[4,64,896]{2,1,0:T(8,128)(2,1)S(1)} collective-permute-done((bf16[4,64,896]{2,1,0:T(8,128)(2,1)}, bf16[4,64,896]{2,1,0:T(8,128)(2,1)S(1)}, u32[]{:S(2)}, u32[]{:S(2)}) %collective-permute-start.9) | collective-permute-done | bytes 458784 | tf_op jit(solution)/shard_map/ppermute | solution.py:246
  144.9 0.1 pad_add_fusion.2.place_ref
  144.9 1.9 collective-permute-done.11.sb
  146.8 1.0 copy-done
  147.8 14.2 %attend.1 = bf16[8,2,128,256]{3,2,1,0:T(8,128)(2,1)S(1)} custom-call(s32[4]{0:T(128)S(1)} %pad_add_fusion.2.place_ref, bf16[2,128,896]{2,1,0:T(8,128)(2,1)S(1)} %bitcast.42, bf16[2,128,896]{2,1,0:T(8,128)(2,1)S(1)} %bitcast.44, bf16[2,128,896]{2,1,0:T(8,128)(2,1)} %collective-permute-done.10.sa, bf16[2,128,896]{2,1,0:T(8,128)(2,1)} %collective-permute-done.11.sb, ...), custom_call_target="tpu_custom_call" | custom-call | tf_op jit(solution)/shard_map/attend/pallas_call | solution.py:212
  162.1 30.3 %all_to_all.20 = bf16[8,2,128,256]{3,2,1,0:T(8,128)(2,1)S(1)} all-to-all(bf16[8,2,128,256]{3,2,1,0:T(8,128)(2,1)S(1)} %attend.1), channel_id=1, replica_groups={{0,2,4,6,8,10,12,14},{1,3,5,7,9,11,13,15},{16,18,20,22,24,26,28,30},{17..., dimensions={0} | all-to-all | bytes 2097152 | tf_op jit(solution)/shard_map/all_to_all | solution.py:334
  192.4 0.1 fusion
  192.5 0.3 copy.43
  192.7 1.0 copy.45
  193.8 0.3 copy.44
  194.0 1.0 copy.46
  (24 shorter events, 0.1 us)
Async XLA Ops:
  0.6 20.9 %copy-start.4 = (bf16[2,56,1024]{2,1,0:T(8,128)(2,1)S(1)}, bf16[2,56,1024]{2,1,0:T(8,128)(2,1)}, u32[]{:S(2)}) copy-start(bf16[2,56,1024]{2,1,0:T(8,128)(2,1)} %param.12) | copy-start | bytes 688132
  0.6 11.9 %collective-permute-start = (bf16[2,56,1024]{2,1,0:T(8,128)(2,1)}, bf16[2,56,1024]{2,1,0:T(8,128)(2,1)S(1)}, u32[]{:S(2)}, u32[]{:S(2)}) collective-permute-start(bf16[2,56,1024]{2,1,0:T(8,128)(2,1)} %param.12), channel_id=1, source_target_pairs={{0,4},{1,5},{2,6},{3,7},{4,8},{5,9},{6,10},{7,11},{8,12},{9,13},{1... | collective-permute-start | bytes 688136 | tf_op jit(solution)/shard_map/ppermute | solution.py:255
  3.7 17.8 %collective-permute-start.1 = (bf16[2,56,1024]{2,1,0:T(8,128)(2,1)}, bf16[2,56,1024]{2,1,0:T(8,128)(2,1)S(1)}, u32[]{:S(2)}, u32[]{:S(2)}) collective-permute-start(bf16[2,56,1024]{2,1,0:T(8,128)(2,1)} %param.12), channel_id=1, source_target_pairs={{0,8},{1,9},{2,10},{3,11},{4,12},{5,13},{6,14},{7,15},{8,0},{9,1},... | collective-permute-start | bytes 688136 | tf_op jit(solution)/shard_map/ppermute | solution.py:255
  6.3 15.2 %collective-permute-start.2 = (bf16[2,56,1024]{2,1,0:T(8,128)(2,1)}, bf16[2,56,1024]{2,1,0:T(8,128)(2,1)S(1)}, u32[]{:S(2)}, u32[]{:S(2)}) collective-permute-start(bf16[2,56,1024]{2,1,0:T(8,128)(2,1)} %param.12), channel_id=1, source_target_pairs={{0,12},{1,13},{2,14},{3,15},{4,0},{5,1},{6,2},{7,3},{8,4},{9,5},{1... | collective-permute-start | bytes 688136 | tf_op jit(solution)/shard_map/ppermute | solution.py:255
  10.0 14.9 %copy-start.5 = (s32[64,2]{0,1:T(2,128)S(1)}, s32[64,2]{0,1:T(2,128)}, u32[]{:S(2)}) copy-start(s32[64,2]{0,1:T(2,128)} %param.14) | copy-start | bytes 1540
  24.8 2.0 %collective-permute-start.4 = (bf16[8,56,512]{2,1,0:T(8,128)(2,1)}, bf16[8,56,512]{2,1,0:T(8,128)(2,1)S(1)}, u32[]{:S(2)}, u32[]{:S(2)}) collective-permute-start(bf16[8,56,512]{2,1,0:T(8,128)(2,1)} %get-tuple-element.28), channel_id=1, source_target_pairs={{0,1},{1,0},{2,3},{3,2},{4,5},{5,4},{6,7},{7,6},{8,9},{9,8},{10,11... | collective-permute-start | bytes 1376264 | tf_op jit(solution)/shard_map/ppermute | solution.py:243
  30.2 12.8 %copy-start.1 = (bf16[128,2048]{1,0:T(8,128)(2,1)S(1)}, bf16[128,2048]{1,0:T(8,128)(2,1)}, u32[]{:S(2)}) copy-start(bf16[128,2048]{1,0:T(8,128)(2,1)} %param.15) | copy-start | bytes 1572868
  30.2 50.4 %all-to-all-start = ((bf16[8,2,64,896]{3,2,1,0:T(8,128)(2,1)}), bf16[8,2,64,896]{3,2,1,0:T(8,128)(2,1)}, u32[]{:S(2)}, u32[]{:S(2)}) async-start(bf16[8,2,64,896]{3,2,1,0:T(8,128)(2,1)} %bitcast.12), calls=%async_computation | async-start | bytes 3670016 | tf_op jit(solution)/shard_map/all_to_all | solution.py:250
  38.0 40.5 %collective-permute-start.3 = (bf16[8,64,896]{2,1,0:T(8,128)(2,1)S(1)}, bf16[8,64,896]{2,1,0:T(8,128)(2,1)S(1)}, u32[]{:S(2)}, u32[]{:S(2)}) collective-permute-start(bf16[8,64,896]{2,1,0:T(8,128)(2,1)S(1)} %multiply_convert_fusion.src_ref), channel_id=1, source_target_pairs={{0,8},{1,9},{2,10},{3,11},{4,12},{5,13},{6,14},{7,15},{8,0},{9,1},... | collective-permute-start | bytes 2752520 | tf_op jit(solution)/shard_map/ppermute | solution.py:243
  39.5 41.1 %collective-permute-start.5 = (bf16[4,2,112,512]{3,2,1,0:T(8,128)(2,1)S(1)}, bf16[4,2,112,512]{3,2,1,0:T(8,128)(2,1)}, u32[]{:S(2)}, u32[]{:S(2)}) collective-permute-start(bf16[4,2,112,512]{3,2,1,0:T(8,128)(2,1)S(1)} %maximum_select_fusion.w_own), channel_id=1, source_target_pairs={{0,2},{1,3},{2,0},{3,1},{4,6},{5,7},{6,4},{7,5},{8,10},{9,11},{10,... | collective-permute-start | bytes 2752520 | tf_op jit(solution)/shard_map/ppermute | solution.py:243
  41.6 39.1 %collective-permute-start.6 = (bf16[4,2,112,512]{3,2,1,0:T(8,128)(2,1)S(1)}, bf16[4,2,112,512]{3,2,1,0:T(8,128)(2,1)}, u32[]{:S(2)}, u32[]{:S(2)}) collective-permute-start(bf16[4,2,112,512]{3,2,1,0:T(8,128)(2,1)S(1)} %maximum_select_fusion.w_own), channel_id=1, source_target_pairs={{0,16},{16,0},{1,17},{17,1},{2,18},{18,2},{3,19},{19,3},{4,20},{20... | collective-permute-start | bytes 2752520 | tf_op jit(solution)/shard_map/ppermute | solution.py:246
  82.6 6.1 %copy-start.2 = (bf16[4,2,128,256]{3,2,1,0:T(8,128)(2,1)S(1)}, bf16[4,2,128,256]{3,2,1,0:T(8,128)(2,1)}, u32[]{:S(2)}) copy-start(bf16[4,2,128,256]{3,2,1,0:T(8,128)(2,1)} %get-tuple-element.32) | copy-start | bytes 1572868
  82.6 38.6 %all-to-all-start.1 = ((bf16[8,2,64,896]{3,2,1,0:T(8,128)(2,1)}), bf16[8,2,64,896]{3,2,1,0:T(8,128)(2,1)}, u32[]{:S(2)}, u32[]{:S(2)}) async-start(bf16[8,2,64,896]{3,2,1,0:T(8,128)(2,1)} %bitcast.17), calls=%async_computation.1 | async-start | bytes 3670016 | tf_op jit(solution)/shard_map/all_to_all | solution.py:250
  87.1 32.7 %collective-permute-start.8 = (bf16[4,2,112,512]{3,2,1,0:T(8,128)(2,1)}, bf16[4,2,112,512]{3,2,1,0:T(8,128)(2,1)S(1)}, u32[]{:S(2)}, u32[]{:S(2)}) collective-permute-start(bf16[4,2,112,512]{3,2,1,0:T(8,128)(2,1)} %collective-permute-done.5.w_x), channel_id=1, source_target_pairs={{0,16},{16,0},{1,17},{17,1},{2,18},{18,2},{3,19},{19,3},{4,20},{20... | collective-permute-start | bytes 2752520 | tf_op jit(solution)/shard_map/ppermute | solution.py:246
  88.7 30.3 %collective-permute-start.7 = (bf16[4,2,128,256]{3,2,1,0:T(8,128)(2,1)S(1)}, bf16[4,2,128,256]{3,2,1,0:T(8,128)(2,1)S(1)}, u32[]{:S(2)}, u32[]{:S(2)}) collective-permute-start(bf16[4,2,128,256]{3,2,1,0:T(8,128)(2,1)S(1)} %copy-done.2), channel_id=1, source_target_pairs={{0,8},{1,9},{2,10},{3,11},{4,12},{5,13},{6,14},{7,15},{8,0},{9,1},... | collective-permute-start | bytes 1572872 | tf_op jit(solution)/shard_map/ppermute | solution.py:243
  119.0 0.8 copy-start.3
  123.3 23.5 %all-to-all-start.2 = ((bf16[4,2,2,128,256]{4,3,2,1,0:T(8,128)(2,1)}), bf16[4,2,2,128,256]{4,3,2,1,0:T(8,128)(2,1)S(1)}, u32[]{:S(2)}, u32[]{:S(2)}) async-start(bf16[4,2,2,128,256]{4,3,2,1,0:T(8,128)(2,1)} %pad_maximum_fusion), calls=%async_computation.2 | async-start | bytes 2097152 | tf_op jit(solution)/shard_map/all_to_all | solution.py:307
  132.8 12.1 %collective-permute-start.9 = (bf16[4,64,896]{2,1,0:T(8,128)(2,1)}, bf16[4,64,896]{2,1,0:T(8,128)(2,1)S(1)}, u32[]{:S(2)}, u32[]{:S(2)}) collective-permute-start(bf16[4,64,896]{2,1,0:T(8,128)(2,1)} %get-tuple-element.36), channel_id=1, source_target_pairs={{0,16},{16,0},{1,17},{17,1},{2,18},{18,2},{3,19},{19,3},{4,20},{20... | collective-permute-start | bytes 1376264 | tf_op jit(solution)/shard_map/ppermute | solution.py:246
  134.4 10.6 %collective-permute-start.10 = (bf16[2,128,896]{2,1,0:T(8,128)(2,1)}, bf16[2,128,896]{2,1,0:T(8,128)(2,1)}, u32[]{:S(2)}, u32[]{:S(2)}) collective-permute-start(bf16[2,128,896]{2,1,0:T(8,128)(2,1)} %bitcast.41), channel_id=1, source_target_pairs={{0,1},{1,0},{2,3},{3,2},{4,5},{5,4},{6,7},{7,6},{8,9},{9,8},{10,11... | collective-permute-start | bytes 1376264 | tf_op jit(solution)/shard_map/ppermute | solution.py:243
  144.8 1.9 collective-permute-start.11
  146.8 1.0 copy-start

commit v5 on v4

--- a/solution.py
+++ b/solution.py
@@ -39,6 +39,7 @@
 ZS, XS, CS = 4, 2, 2
 CHIPS = ZS * XS
 HALF = 8
+PER_STEP = 2
 ALL = range(ZS * XS * CS)
 
 
@@ -129,7 +130,7 @@
     place_ref, na, nb, sa, sb, w_own, w_x, w_y, w_xy, qg_ref, out_ref, n_scr, w_scr
 ):
     my_c, my_x, my_z = place_ref[1], place_ref[2], place_ref[3]
-    rows = w_scr.shape[0] // CHIPS
+    rows, width = w_scr.shape[0] // CHIPS, w_scr.shape[1] // 2
 
     @pl.when(pl.program_id(0) == 0)
     def _():
@@ -144,7 +145,7 @@
             for other, ref in enumerate(sources):
                 at = pl.multiple_of((src_z * XS + (my_x ^ other)) * rows, 16)
                 for kv in range(2):
-                    lanes = slice(HEAD_DIM * kv, HEAD_DIM * (kv + 1))
+                    lanes = slice(width * kv, width * (kv + 1))
                     w_scr[pl.ds(at, rows), lanes] = ref[r, kv]
 
     own_dp = pl.program_id(0) < pl.num_programs(0) // 2
@@ -159,20 +160,22 @@
 
     weights = w_scr[...]
     kvs = [ndot(n_scr[s], weights).astype(jnp.bfloat16) for s in range(CS * CH_DEV)]
-    keys = [kv[:, :HEAD_DIM] for kv in kvs]
-    values = [kv[:, HEAD_DIM:] for kv in kvs]
     low = lax.broadcasted_iota(jnp.int32, (1, 2 * SPAN), 1) < SPAN
-    pairs = range(CS)
-    lanes = [slice(2 * SPAN * p, 2 * SPAN * (p + 1)) for p in pairs]
+    units = [(h, p) for h in range(PER_STEP) for p in range(CS)]
+    lanes = [slice(2 * SPAN * p, 2 * SPAN * (p + 1)) for p in range(CS)]
+
+    def spans_of(kv):
+        at = [slice(width * kv + HEAD_DIM * h, width * kv + HEAD_DIM * (h + 1)) for h, _ in units]
+        return [
+            (kvs[CH_DEV * p][:, a], kvs[CH_DEV * p + 1][:, a]) for (_, p), a in zip(units, at)
+        ]
 
     def both(dot, spans, right):
-        return [
-            jnp.where(low, dot(spans[2 * p], right[p]), dot(spans[2 * p + 1], right[p]))
-            for p in pairs
-        ]
-
-    queries = [qg_ref[0, 0, :, at] for at in lanes]
-    grads = [qg_ref[0, 1, :, at] for at in lanes]
+        return [jnp.where(low, dot(a, r), dot(b, r)) for (a, b), r in zip(spans, right)]
+
+    keys, values = spans_of(0), spans_of(1)
+    queries = [qg_ref[h, 0, 0, :, lanes[p]] for h, p in units]
+    grads = [qg_ref[h, 0, 1, :, lanes[p]] for h, p in units]
     scores = [s * SCORE_SCALE for s in both(ndot, keys, queries)]
     dprobs = both(ndot, values, grads)
     exponent = [jnp.exp(s - jnp.max(s, axis=0, keepdims=True)) for s in scores]
@@ -188,43 +191,44 @@
         for p, dp, dl in zip(probs, dprobs, delta)
     ]
     dqs = [q.astype(jnp.bfloat16) for q in both(tdot, keys, dscores)]
-    for p in pairs:
-        out_ref[0, 0, :, lanes[p]] = outs[p]
-        out_ref[0, 1, :, lanes[p]] = dqs[p]
+    for i, (h, p) in enumerate(units):
+        out_ref[h, 0, :, lanes[p]] = outs[i]
+        out_ref[h, 1, :, lanes[p]] = dqs[i]
 
 
 def attend(place, neighbours, weights, qg):
-    d_heads = HEADS // CS // 2
-    heads = 2 * d_heads
-    block = (1, 2, HEAD_DIM, qg.shape[-1])
-
-    def head_of(i, place):
-        return (i + d_heads * place[0]) & (heads - 1)
+    steps = HEADS // CS // PER_STEP
+    d_steps = steps // 2
+    block = (PER_STEP,) + qg.shape[2:]
+
+    def pair_of(i, place):
+        return (i + d_steps * place[0]) & (steps - 1)
 
     def came_at(i, place):
-        head = head_of(i, place)
-        half = head // d_heads
-        return (2 * (head & (d_heads - 1)) + jnp.abs(half - place[3] // 2), 0, 0, 0)
-
-    w_block = weights[0].shape[:3] + (HEAD_DIM,)
-    first = pl.BlockSpec(w_block, lambda i, place: (0, 0, 0, jnp.minimum(i, d_heads - 1)))
-    last = pl.BlockSpec(w_block, lambda i, place: (0, 0, 0, jnp.maximum(i - d_heads, 0)))
+        pair = pair_of(i, place)
+        return (pair & (d_steps - 1), jnp.abs(pair // d_steps - place[3] // 2), 0, 0, 0)
+
+    w_block = weights[0].shape[:3] + (PER_STEP * HEAD_DIM,)
+    first = pl.BlockSpec(w_block, lambda i, place: (0, 0, 0, jnp.minimum(i, d_steps - 1)))
+    last = pl.BlockSpec(w_block, lambda i, place: (0, 0, 0, jnp.maximum(i - d_steps, 0)))
+    head_block = pl.BlockSpec(block, lambda i, place: (pair_of(i, place), 0, 0, 0))
     return pl.pallas_call(
         attend_kernel,
         grid_spec=pltpu.PrefetchScalarGridSpec(
             num_scalar_prefetch=1,
-            grid=(heads,),
+            grid=(steps,),
             in_specs=[
                 pl.BlockSpec(a.shape, lambda i, place: (0, 0, 0)) for a in neighbours
             ]
-            + [first, first, last, last, pl.BlockSpec(block, came_at)],
-            out_specs=pl.BlockSpec(block, lambda i, place: (head_of(i, place), 0, 0, 0)),
+            + [first, first, last, last]
+            + [pl.BlockSpec(block[:1] + (1,) + block[1:], came_at)],
+            out_specs=head_block,
             scratch_shapes=[
                 pltpu.VMEM((CS * CH_DEV, NBR * NT, E), jnp.bfloat16),
-                pltpu.VMEM((E, 2 * HEAD_DIM), jnp.bfloat16),
+                pltpu.VMEM((E, 2 * PER_STEP * HEAD_DIM), jnp.bfloat16),
             ],
         ),
-        out_shape=jax.ShapeDtypeStruct(qg.shape, jnp.bfloat16),
+        out_shape=jax.ShapeDtypeStruct((CHIPS,) + block[1:], jnp.bfloat16),
         compiler_params=pltpu.CompilerParams(vmem_limit_bytes=40 * 1024 * 1024),
         name="attend",
     )(place, *neighbours, *weights, qg)
@@ -256,7 +260,16 @@
         for r in range(1, ZS)
     ]
     scaled = (cache.astype(jnp.float32) * cache_scale[..., None]).astype(jnp.bfloat16)
-    scaled, turned = lax.optimization_barrier((scaled, turned))
+    shard_blk, row_blk, slot_blk = requests(nbr_shard, nbr_row, dp_count, mp_count)
+    holders = jnp.stack([my_mp, my_mp ^ HALF]).astype(jnp.int32)
+    select = jnp.logical_and(
+        shard_blk[:, None, None, :] == holders[None, :, None, None],
+        slot_blk[:, None, None, :] == jnp.arange(MOST, dtype=jnp.int32)[None, None, :, None],
+    )
+    wanted = jnp.sum(jnp.where(select, row_blk[:, None, None, :], 0), axis=3)
+    wanted = lax.dynamic_slice_in_dim(wanted, my_mp & HALF, HALF, 0)
+    near_rows = pick_rows(wanted[:, 0].reshape(-1), scaled)
+    scaled, turned, near_rows = lax.optimization_barrier((scaled, turned, near_rows))
     far = swap(scaled, HALF)
 
     mine, sends = by_parity(my_c.reshape(1).astype(jnp.int32), jnp.concatenate(turned))
@@ -268,21 +281,18 @@
     ).reshape(ZS, 2, CS * w_kv.shape[1], -1)
     x_w, y_w = swap(line_w, CS), swap_dp(line_w)
 
-    shard_blk, row_blk, slot_blk = requests(nbr_shard, nbr_row, dp_count, mp_count)
-    holders = jnp.stack([my_mp, my_mp ^ HALF]).astype(jnp.int32)
-    select = jnp.logical_and(
-        shard_blk[:, None, None, :] == holders[None, :, None, None],
-        slot_blk[:, None, None, :] == jnp.arange(MOST, dtype=jnp.int32)[None, None, :, None],
-    )
-    wanted = jnp.sum(jnp.where(select, row_blk[:, None, None, :], 0), axis=3)
-    wanted = lax.dynamic_slice_in_dim(wanted, my_mp & HALF, HALF, 0)
-
-    def pieces(which, *sources):
-        rows = pick_rows(wanted[:, which].reshape(-1), *sources)
+
+    shards = lax.dynamic_index_in_dim(shard_blk, my_mp, 0, keepdims=False)
+    slots = lax.dynamic_index_in_dim(slot_blk, my_mp, 0, keepdims=False)
+    row = jnp.roll(((shards & (HALF - 1)) * MOST + slots).reshape(dp_count, -1), my_dp, 0)
+    is_far = jnp.roll(((shards ^ my_mp) & HALF).reshape(dp_count, -1), my_dp, 0)
+    row = row.reshape(-1).astype(jnp.int32)
+    is_far = is_far.reshape(-1).astype(jnp.int32)
+
+    def spread(rows):
         return over_half(rows.reshape((HALF, MOST) + rows.shape[1:])).reshape(rows.shape)
 
-    near_source, line_w = lax.optimization_barrier((scaled, line_w))
-    near_pieces = pieces(0, near_source)
+    near_pieces = spread(near_rows)
 
     my_half = my_mp // HALF
     chips = CHIPS // 2
@@ -291,11 +301,11 @@
     qg_stay = lax.dynamic_index_in_dim(qg, my_half, 0, keepdims=False)
     qg_go = lax.dynamic_index_in_dim(qg, 1 - my_half, 0, keepdims=False)
 
-    far, near_pieces, x_w, y_w, qg_go = lax.optimization_barrier(
-        (far, near_pieces, x_w, y_w, qg_go)
+    far, near_pieces, x_w, y_w, qg_go, row, is_far = lax.optimization_barrier(
+        (far, near_pieces, x_w, y_w, qg_go, row, is_far)
     )
     xy_w = swap_dp(x_w)
-    far_pieces = pieces(1, far)
+    far_pieces = spread(pick_rows(wanted[:, 1].reshape(-1), far))
     qg_came = swap(qg_go, HALF)
 
     far_pieces, qg_came, xy_w = lax.optimization_barrier((far_pieces, qg_came, xy_w))
@@ -312,16 +322,11 @@
         tiled=True,
         axis_index_groups=chip_lines,
     )
-    qg = qg.reshape((CHIPS,) + qg.shape[2:])
     chip_groups = [[CS * chip + core for chip in range(CHIPS)] for core in range(CS)]
 
-    shards = lax.dynamic_index_in_dim(shard_blk, my_mp, 0, keepdims=False)
-    slots = lax.dynamic_index_in_dim(slot_blk, my_mp, 0, keepdims=False)
-    row = jnp.roll(((shards & (HALF - 1)) * MOST + slots).reshape(dp_count, -1), my_dp, 0)
-    is_far = jnp.roll(((shards ^ my_mp) & HALF).reshape(dp_count, -1), my_dp, 0)
     own, give = choose(
-        is_far.reshape(-1).astype(jnp.int32),
-        row.reshape(-1).astype(jnp.int32),
+        is_far,
+        row,
         near_pieces,
         far_pieces,
     )

time: 196 us -> 186 us (0.949)
  waiting for transfers between devices: 87.7 us -> 79.6 us
  Pallas kernels: 23.3 us -> 19.9 us
    ppermute x6, waiting for transfers between devices: 64.4 us -> 59.5 us  [swap(): return lax.ppermute(a, 'mp', [(m, m ^ bits) for m in ALL])]
    pallas_call x1, Pallas kernels: 14.2 us -> 10.8 us  [attend(): pl.pallas_call(attend_kernel, grid_spec=pltpu.PrefetchScalarGridSpec(num_...]
    ppermute x3, waiting for transfers between devices: 11.4 us -> 8.17 us  [small(): lax.ppermute(w_kv, 'mp', [(m, (m + XS * CS * r) % len(ALL)) for m in ALL])]
  transfers between devices with their start and end apart: 15 -> 15, of which waited for: 9 -> 7; matrix products, arithmetic and copies ran while one was open for 5% -> 7% of each run, Pallas kernels for 1% -> 4%
where the time goes in v5:
time: 186 us; the launch traced here: 185 us
  waiting for transfers between devices  79.6 us (43%)
  starting transfers between devices  33.9 us (18%)
  blocking collectives  30.7 us (17%)
  Pallas kernels  19.9 us (11%)
  local copies, waits for them, and re-layouts  13.5 us (7%)
  other arithmetic  6.95 us (4%)
    ppermute x6, waiting for transfers between devices, swap(): return lax.ppermute(a, 'mp', [(m, m ^ bits) for m in ALL])  59.5 us
    all_to_all x1, blocking collectives, small(): lax.all_to_all(result, 'mp', split_axis=0, concat_axis=0, tiled=True, axi...  30.7 us
    all_to_all x2, starting transfers between devices, over_half(): lax.all_to_all(a, 'mp', split_axis=0, concat_axis=0, tiled=True, axis_ind...  12.2 us
    pallas_call x1, Pallas kernels, attend(): pl.pallas_call(attend_kernel, grid_spec=pltpu.PrefetchScalarGridSpec(num_...  10.8 us
    ppermute x3, waiting for transfers between devices, swap_dp(): return lax.ppermute(a, 'dp', [(0, 1), (1, 0)])  10.5 us
    ppermute x3, waiting for transfers between devices, small(): lax.ppermute(w_kv, 'mp', [(m, (m + XS * CS * r) % len(ALL)) for m in ALL])  8.17 us
    unnamed x18, local copies, waits for them, and re-layouts  7.41 us
    ppermute x3, starting transfers between devices, small(): lax.ppermute(w_kv, 'mp', [(m, (m + XS * CS * r) % len(ALL)) for m in ALL])  7.01 us
  transfers between devices with their start and end apart: 15, of which 7 were waited for; matrix products, arithmetic and copies ran while one was open for 7% of the time, Pallas kernels for 4%

profile of v5, /device:TPU:0, one launch (start us, length us, event | category | flops | bytes accessed | tf_op | source)
XLA Modules:
  0.0 185.2 jit_solution(9365221635635291216)
XLA Ops:
  0.6 3.1 %collective-permute-start = (bf16[2,56,1024]{2,1,0:T(8,128)(2,1)}, bf16[2,56,1024]{2,1,0:T(8,128)(2,1)S(1)}, u32[]{:S(2)}, u32[]{:S(2)}) collective-permute-start(bf16[2,56,1024]{2,1,0:T(8,128)(2,1)} %param.12), channel_id=1, source_target_pairs={{0,4},{1,5},{2,6},{3,7},{4,8},{5,9},{6,10},{7,11},{8,12},{9,13},{1... | collective-permute-start | bytes 688136 | tf_op jit(solution)/shard_map/ppermute | solution.py:259
  3.7 2.6 %collective-permute-start.1 = (bf16[2,56,1024]{2,1,0:T(8,128)(2,1)}, bf16[2,56,1024]{2,1,0:T(8,128)(2,1)S(1)}, u32[]{:S(2)}, u32[]{:S(2)}) collective-permute-start(bf16[2,56,1024]{2,1,0:T(8,128)(2,1)} %param.12), channel_id=1, source_target_pairs={{0,8},{1,9},{2,10},{3,11},{4,12},{5,13},{6,14},{7,15},{8,0},{9,1},... | collective-permute-start | bytes 688136 | tf_op jit(solution)/shard_map/ppermute | solution.py:259
  6.3 1.3 collective-permute-start.2
  7.7 0.8 copy.35
  8.4 0.1 reshape.102
  8.5 0.1 copy.36
  8.6 0.8 copy.33
  9.4 0.1 reshape.101
  9.4 0.1 copy.34
  9.5 0.1 convert_reduce_fusion
  9.6 0.1 pad_add_fusion.3
  9.7 0.1 iota_compare_fusion
  9.8 0.1 constant_dynamic-slice_fusion.3
  9.9 0.1 copy.37
  10.0 0.1 reshape_squeeze.6.rows_ref
  10.0 1.4 multiply_convert_fusion.src_ref
  11.4 1.9 %pick_rows.2 = bf16[16,64,896]{2,1,0:T(8,128)(2,1)} custom-call(s32[16]{0:T(128)S(1)} %reshape_squeeze.6.rows_ref, bf16[8,64,896]{2,1,0:T(8,128)(2,1)S(1)} %multiply_convert_fusion.src_ref), custom_call_target="tpu_custom_call" | custom-call | tf_op jit(solution)/shard_map/pick_rows/pallas_call | solution.py:78
  13.3 8.2 %collective-permute-done.1 = bf16[2,56,1024]{2,1,0:T(8,128)(2,1)S(1)} collective-permute-done((bf16[2,56,1024]{2,1,0:T(8,128)(2,1)}, bf16[2,56,1024]{2,1,0:T(8,128)(2,1)S(1)}, u32[]{:S(2)}, u32[]{:S(2)}) %collective-permute-start.1) | collective-permute-done | bytes 229408 | tf_op jit(solution)/shard_map/ppermute | solution.py:259
  21.5 0.0 collective-permute-done.2
  21.5 7.7 %all-to-all-start = ((bf16[8,2,64,896]{3,2,1,0:T(8,128)(2,1)}), bf16[8,2,64,896]{3,2,1,0:T(8,128)(2,1)}, u32[]{:S(2)}, u32[]{:S(2)}) async-start(bf16[8,2,64,896]{3,2,1,0:T(8,128)(2,1)} %bitcast.10), calls=%async_computation | async-start | bytes 3670016 | tf_op jit(solution)/shard_map/all_to_all | solution.py:254
  29.2 1.1 pad_maximum_fusion.1.w_ref
  30.3 2.3 %by_parity.1 = (bf16[8,56,512]{2,1,0:T(8,128)(2,1)}, bf16[8,56,512]{2,1,0:T(8,128)(2,1)}) custom-call(s32[1]{0:T(128)} %bitcast.1.core_ref, bf16[8,56,1024]{2,1,0:T(8,128)(2,1)} %pad_maximum_fusion.1.w_ref), custom_call_target="tpu_custom_call" | custom-call | tf_op jit(solution)/shard_map/by_parity/pallas_call | solution.py:60
  32.6 0.5 collective-permute-start.4
  33.1 1.6 collective-permute-start.3
  34.7 0.1 collective-permute-done.4
  34.8 0.8 copy-done.4
  35.5 1.7 maximum_select_fusion.w_own
  37.2 2.0 %collective-permute-start.5 = (bf16[4,2,112,512]{3,2,1,0:T(8,128)(2,1)S(1)}, bf16[4,2,112,512]{3,2,1,0:T(8,128)(2,1)}, u32[]{:S(2)}, u32[]{:S(2)}) collective-permute-start(bf16[4,2,112,512]{3,2,1,0:T(8,128)(2,1)S(1)} %maximum_select_fusion.w_own), channel_id=1, source_target_pairs={{0,2},{1,3},{2,0},{3,1},{4,6},{5,7},{6,4},{7,5},{8,10},{9,11},{10,... | collective-permute-start | bytes 2752520 | tf_op jit(solution)/shard_map/ppermute | solution.py:247
  39.2 1.5 collective-permute-start.6
  40.7 0.1 copy.45
  40.8 1.2 copy.44
  42.0 0.1 maximum_bitcast_fusion
  42.1 1.2 copy.38
  43.3 0.2 and_reduce_fusion
  43.5 0.1 and.65
  43.6 0.1 add.36
  43.7 0.6 reshape.106.row_ref
  44.4 0.7 reshape.107.far_ref
  45.0 0.1 copy.39
  45.1 0.1 reshape_squeeze.7.rows_ref
  45.2 2.1 %dynamic-slice_bitcast_fusion = (bf16[4,1,2,128,256]{4,3,2,1,0:T(8,128)(2,1)S(1)}, bf16[4,2,128,256]{3,2,1,0:T(8,128)(2,1)}) fusion(bf16[2,4,2,128,256]{4,3,2,1,0:T(8,128)(2,1)} %bitcast.44, s32[]{:T(128)S(6)} %select_n.49, s32[]{:T(128)S(6)} %select_n.47), kind=kLoop, calls=%fused_computation.5 | loop fusion | bytes 2097160 | tf_op jit(solution)/shard_map/stack | solution.py:318
  47.3 28.7 %collective-permute-done.3.src_ref = bf16[8,64,896]{2,1,0:T(8,128)(2,1)S(1)} collective-permute-done((bf16[8,64,896]{2,1,0:T(8,128)(2,1)S(1)}, bf16[8,64,896]{2,1,0:T(8,128)(2,1)S(1)}, u32[]{:S(2)}, u32[]{:S(2)}) %collective-permute-start.3) | collective-permute-done | bytes 917536 | tf_op jit(solution)/shard_map/ppermute | solution.py:247
  76.0 1.9 %pick_rows.3 = bf16[16,64,896]{2,1,0:T(8,128)(2,1)} custom-call(s32[16]{0:T(128)S(1)} %reshape_squeeze.7.rows_ref, bf16[8,64,896]{2,1,0:T(8,128)(2,1)S(1)} %collective-permute-done.3.src_ref), custom_call_target="tpu_custom_call" | custom-call | tf_op jit(solution)/shard_map/pick_rows/pallas_call | solution.py:78
  78.0 4.5 %all-to-all-start.1 = ((bf16[8,2,64,896]{3,2,1,0:T(8,128)(2,1)}), bf16[8,2,64,896]{3,2,1,0:T(8,128)(2,1)}, u32[]{:S(2)}, u32[]{:S(2)}) async-start(bf16[8,2,64,896]{3,2,1,0:T(8,128)(2,1)} %bitcast.17), calls=%async_computation.1 | async-start | bytes 3670016 | tf_op jit(solution)/shard_map/all_to_all | solution.py:254
  82.4 1.6 collective-permute-start.8
  84.0 1.5 collective-permute-start.7
  85.5 28.9 %collective-permute-done.7 = bf16[4,2,128,256]{3,2,1,0:T(8,128)(2,1)S(1)} collective-permute-done((bf16[4,2,128,256]{3,2,1,0:T(8,128)(2,1)S(1)}, bf16[4,2,128,256]{3,2,1,0:T(8,128)(2,1)S(1)}, u32[]{:S(2)}, u32[]{:S(2)}) %collective-permute-start.7) | collective-permute-done | bytes 524320 | tf_op jit(solution)/shard_map/ppermute | solution.py:247
  114.3 0.8 copy-done.3
  115.1 1.4 all-to-all-done.1
  116.5 2.1 %pad_maximum_fusion = bf16[4,2,2,128,256]{4,3,2,1,0:T(8,128)(2,1)} fusion(bf16[4,1,2,128,256]{4,3,2,1,0:T(8,128)(2,1)} %bitcast.51, bf16[4,1,2,128,256]{4,3,2,1,0:T(8,128)(2,1)S(1)} %get-tuple-element.51), kind=kLoop, calls=%fused_computation.2 | loop fusion | flops 524288 | bytes 2097152 | tf_op jit(solution)/shard_map/stack | solution.py:318
  118.6 4.5 %all-to-all-start.2 = ((bf16[4,2,2,128,256]{4,3,2,1,0:T(8,128)(2,1)}), bf16[4,2,2,128,256]{4,3,2,1,0:T(8,128)(2,1)S(1)}, u32[]{:S(2)}, u32[]{:S(2)}) async-start(bf16[4,2,2,128,256]{4,3,2,1,0:T(8,128)(2,1)} %pad_maximum_fusion), calls=%async_computation.2 | async-start | bytes 2097152 | tf_op jit(solution)/shard_map/all_to_all | solution.py:317
  123.2 2.9 %choose.1 = (bf16[4,64,896]{2,1,0:T(8,128)(2,1)}, bf16[4,64,896]{2,1,0:T(8,128)(2,1)}) custom-call(s32[8]{0:T(128)} %reshape.107.far_ref, s32[8]{0:T(128)} %reshape.106.row_ref, bf16[16,64,896]{2,1,0:T(8,128)(2,1)} %bitcast.11.near, bf16[16,64,896]{2,1,0:T(8,128)(2,1)} %bitcast.18.far), custom_call_target="tpu_custom_call" | custom-call | tf_op jit(solution)/shard_map/choose/pallas_call | solution.py:110
  126.1 1.6 collective-permute-start.9
  127.7 10.5 %collective-permute-done.9 = bf16[4,64,896]{2,1,0:T(8,128)(2,1)S(1)} collective-permute-done((bf16[4,64,896]{2,1,0:T(8,128)(2,1)}, bf16[4,64,896]{2,1,0:T(8,128)(2,1)S(1)}, u32[]{:S(2)}, u32[]{:S(2)}) %collective-permute-start.9) | collective-permute-done | bytes 458784 | tf_op jit(solution)/shard_map/ppermute | solution.py:250
  138.1 0.1 pad_add_fusion.2.place_ref
  138.2 1.9 %collective-permute-done.11.sb = bf16[2,128,896]{2,1,0:T(8,128)(2,1)} collective-permute-done((bf16[2,128,896]{2,1,0:T(8,128)(2,1)S(1)}, bf16[2,128,896]{2,1,0:T(8,128)(2,1)}, u32[]{:S(2)}, u32[]{:S(2)}) %collective-permute-start.11) | collective-permute-done | bytes 458784 | tf_op jit(solution)/shard_map/ppermute | solution.py:247
  140.1 1.0 copy-done
  141.1 10.8 %attend.1 = bf16[8,2,128,256]{3,2,1,0:T(8,128)(2,1)S(1)} custom-call(s32[4]{0:T(128)S(1)} %pad_add_fusion.2.place_ref, bf16[2,128,896]{2,1,0:T(8,128)(2,1)S(1)} %bitcast.40, bf16[2,128,896]{2,1,0:T(8,128)(2,1)S(1)} %bitcast.42, bf16[2,128,896]{2,1,0:T(8,128)(2,1)} %collective-permute-done.10.sa, bf16[2,128,896]{2,1,0:T(8,128)(2,1)} %collective-permute-done.11.sb, ...), custom_call_target="tpu_custom_call" | custom-call | tf_op jit(solution)/shard_map/attend/pallas_call | solution.py:215
  151.9 30.7 %all_to_all.20 = bf16[8,2,128,256]{3,2,1,0:T(8,128)(2,1)S(1)} all-to-all(bf16[8,2,128,256]{3,2,1,0:T(8,128)(2,1)S(1)} %attend.1), channel_id=1, replica_groups={{0,2,4,6,8,10,12,14},{1,3,5,7,9,11,13,15},{16,18,20,22,24,26,28,30},{17..., dimensions={0} | all-to-all | bytes 2097152 | tf_op jit(solution)/shard_map/all_to_all | solution.py:339
  182.6 0.1 fusion
  182.7 0.3 copy.40
  182.9 1.0 copy.42
  184.0 0.3 copy.41
  184.2 1.0 copy.43
  (23 shorter events, 0.1 us)
Async XLA Ops:
  0.6 12.7 %collective-permute-start = (bf16[2,56,1024]{2,1,0:T(8,128)(2,1)}, bf16[2,56,1024]{2,1,0:T(8,128)(2,1)S(1)}, u32[]{:S(2)}, u32[]{:S(2)}) collective-permute-start(bf16[2,56,1024]{2,1,0:T(8,128)(2,1)} %param.12), channel_id=1, source_target_pairs={{0,4},{1,5},{2,6},{3,7},{4,8},{5,9},{6,10},{7,11},{8,12},{9,13},{1... | collective-permute-start | bytes 688136 | tf_op jit(solution)/shard_map/ppermute | solution.py:259
  3.7 17.8 %collective-permute-start.1 = (bf16[2,56,1024]{2,1,0:T(8,128)(2,1)}, bf16[2,56,1024]{2,1,0:T(8,128)(2,1)S(1)}, u32[]{:S(2)}, u32[]{:S(2)}) collective-permute-start(bf16[2,56,1024]{2,1,0:T(8,128)(2,1)} %param.12), channel_id=1, source_target_pairs={{0,8},{1,9},{2,10},{3,11},{4,12},{5,13},{6,14},{7,15},{8,0},{9,1},... | collective-permute-start | bytes 688136 | tf_op jit(solution)/shard_map/ppermute | solution.py:259
  6.3 15.2 %collective-permute-start.2 = (bf16[2,56,1024]{2,1,0:T(8,128)(2,1)}, bf16[2,56,1024]{2,1,0:T(8,128)(2,1)S(1)}, u32[]{:S(2)}, u32[]{:S(2)}) collective-permute-start(bf16[2,56,1024]{2,1,0:T(8,128)(2,1)} %param.12), channel_id=1, source_target_pairs={{0,12},{1,13},{2,14},{3,15},{4,0},{5,1},{6,2},{7,3},{8,4},{9,5},{1... | collective-permute-start | bytes 688136 | tf_op jit(solution)/shard_map/ppermute | solution.py:259
  21.5 7.7 %copy-start.5 = (bf16[2,56,1024]{2,1,0:T(8,128)(2,1)S(1)}, bf16[2,56,1024]{2,1,0:T(8,128)(2,1)}, u32[]{:S(2)}) copy-start(bf16[2,56,1024]{2,1,0:T(8,128)(2,1)} %param.12) | copy-start | bytes 688132
  21.5 54.5 %all-to-all-start = ((bf16[8,2,64,896]{3,2,1,0:T(8,128)(2,1)}), bf16[8,2,64,896]{3,2,1,0:T(8,128)(2,1)}, u32[]{:S(2)}, u32[]{:S(2)}) async-start(bf16[8,2,64,896]{3,2,1,0:T(8,128)(2,1)} %bitcast.10), calls=%async_computation | async-start | bytes 3670016 | tf_op jit(solution)/shard_map/all_to_all | solution.py:254
  30.3 10.4 %copy-start.1 = (bf16[128,2048]{1,0:T(8,128)(2,1)S(1)}, bf16[128,2048]{1,0:T(8,128)(2,1)}, u32[]{:S(2)}) copy-start(bf16[128,2048]{1,0:T(8,128)(2,1)} %param.15) | copy-start | bytes 1572868
  32.6 2.2 %collective-permute-start.4 = (bf16[8,56,512]{2,1,0:T(8,128)(2,1)}, bf16[8,56,512]{2,1,0:T(8,128)(2,1)S(1)}, u32[]{:S(2)}, u32[]{:S(2)}) collective-permute-start(bf16[8,56,512]{2,1,0:T(8,128)(2,1)} %get-tuple-element.30), channel_id=1, source_target_pairs={{0,1},{1,0},{2,3},{3,2},{4,5},{5,4},{6,7},{7,6},{8,9},{9,8},{10,11... | collective-permute-start | bytes 1376264 | tf_op jit(solution)/shard_map/ppermute | solution.py:247
  33.1 42.9 %collective-permute-start.3 = (bf16[8,64,896]{2,1,0:T(8,128)(2,1)S(1)}, bf16[8,64,896]{2,1,0:T(8,128)(2,1)S(1)}, u32[]{:S(2)}, u32[]{:S(2)}) collective-permute-start(bf16[8,64,896]{2,1,0:T(8,128)(2,1)S(1)} %multiply_convert_fusion.src_ref), channel_id=1, source_target_pairs={{0,8},{1,9},{2,10},{3,11},{4,12},{5,13},{6,14},{7,15},{8,0},{9,1},... | collective-permute-start | bytes 2752520 | tf_op jit(solution)/shard_map/ppermute | solution.py:247
  34.8 0.8 copy-start.4
  37.2 38.8 %collective-permute-start.5 = (bf16[4,2,112,512]{3,2,1,0:T(8,128)(2,1)S(1)}, bf16[4,2,112,512]{3,2,1,0:T(8,128)(2,1)}, u32[]{:S(2)}, u32[]{:S(2)}) collective-permute-start(bf16[4,2,112,512]{3,2,1,0:T(8,128)(2,1)S(1)} %maximum_select_fusion.w_own), channel_id=1, source_target_pairs={{0,2},{1,3},{2,0},{3,1},{4,6},{5,7},{6,4},{7,5},{8,10},{9,11},{10,... | collective-permute-start | bytes 2752520 | tf_op jit(solution)/shard_map/ppermute | solution.py:247
  39.2 36.8 %collective-permute-start.6 = (bf16[4,2,112,512]{3,2,1,0:T(8,128)(2,1)S(1)}, bf16[4,2,112,512]{3,2,1,0:T(8,128)(2,1)}, u32[]{:S(2)}, u32[]{:S(2)}) collective-permute-start(bf16[4,2,112,512]{3,2,1,0:T(8,128)(2,1)S(1)} %maximum_select_fusion.w_own), channel_id=1, source_target_pairs={{0,16},{16,0},{1,17},{17,1},{2,18},{18,2},{3,19},{19,3},{4,20},{20... | collective-permute-start | bytes 2752520 | tf_op jit(solution)/shard_map/ppermute | solution.py:250
  78.0 6.0 %copy-start.2 = (bf16[4,2,128,256]{3,2,1,0:T(8,128)(2,1)S(1)}, bf16[4,2,128,256]{3,2,1,0:T(8,128)(2,1)}, u32[]{:S(2)}) copy-start(bf16[4,2,128,256]{3,2,1,0:T(8,128)(2,1)} %get-tuple-element.35) | copy-start | bytes 1572868
  78.0 38.6 %all-to-all-start.1 = ((bf16[8,2,64,896]{3,2,1,0:T(8,128)(2,1)}), bf16[8,2,64,896]{3,2,1,0:T(8,128)(2,1)}, u32[]{:S(2)}, u32[]{:S(2)}) async-start(bf16[8,2,64,896]{3,2,1,0:T(8,128)(2,1)} %bitcast.17), calls=%async_computation.1 | async-start | bytes 3670016 | tf_op jit(solution)/shard_map/all_to_all | solution.py:254
  82.4 32.7 %collective-permute-start.8 = (bf16[4,2,112,512]{3,2,1,0:T(8,128)(2,1)}, bf16[4,2,112,512]{3,2,1,0:T(8,128)(2,1)S(1)}, u32[]{:S(2)}, u32[]{:S(2)}) collective-permute-start(bf16[4,2,112,512]{3,2,1,0:T(8,128)(2,1)} %collective-permute-done.5.w_x), channel_id=1, source_target_pairs={{0,16},{16,0},{1,17},{17,1},{2,18},{18,2},{3,19},{19,3},{4,20},{20... | collective-permute-start | bytes 2752520 | tf_op jit(solution)/shard_map/ppermute | solution.py:250
  84.0 30.3 %collective-permute-start.7 = (bf16[4,2,128,256]{3,2,1,0:T(8,128)(2,1)S(1)}, bf16[4,2,128,256]{3,2,1,0:T(8,128)(2,1)S(1)}, u32[]{:S(2)}, u32[]{:S(2)}) collective-permute-start(bf16[4,2,128,256]{3,2,1,0:T(8,128)(2,1)S(1)} %copy-done.2), channel_id=1, source_target_pairs={{0,8},{1,9},{2,10},{3,11},{4,12},{5,13},{6,14},{7,15},{8,0},{9,1},... | collective-permute-start | bytes 1572872 | tf_op jit(solution)/shard_map/ppermute | solution.py:247
  114.3 0.8 copy-start.3
  118.6 21.4 %all-to-all-start.2 = ((bf16[4,2,2,128,256]{4,3,2,1,0:T(8,128)(2,1)}), bf16[4,2,2,128,256]{4,3,2,1,0:T(8,128)(2,1)S(1)}, u32[]{:S(2)}, u32[]{:S(2)}) async-start(bf16[4,2,2,128,256]{4,3,2,1,0:T(8,128)(2,1)} %pad_maximum_fusion), calls=%async_computation.2 | async-start | bytes 2097152 | tf_op jit(solution)/shard_map/all_to_all | solution.py:317
  126.1 12.0 %collective-permute-start.9 = (bf16[4,64,896]{2,1,0:T(8,128)(2,1)}, bf16[4,64,896]{2,1,0:T(8,128)(2,1)S(1)}, u32[]{:S(2)}, u32[]{:S(2)}) collective-permute-start(bf16[4,64,896]{2,1,0:T(8,128)(2,1)} %get-tuple-element.39), channel_id=1, source_target_pairs={{0,16},{16,0},{1,17},{17,1},{2,18},{18,2},{3,19},{19,3},{4,20},{20... | collective-permute-start | bytes 1376264 | tf_op jit(solution)/shard_map/ppermute | solution.py:250
  127.7 10.5 %collective-permute-start.10 = (bf16[2,128,896]{2,1,0:T(8,128)(2,1)}, bf16[2,128,896]{2,1,0:T(8,128)(2,1)}, u32[]{:S(2)}, u32[]{:S(2)}) collective-permute-start(bf16[2,128,896]{2,1,0:T(8,128)(2,1)} %bitcast.39), channel_id=1, source_target_pairs={{0,1},{1,0},{2,3},{3,2},{4,5},{5,4},{6,7},{7,6},{8,9},{9,8},{10,11... | collective-permute-start | bytes 1376264 | tf_op jit(solution)/shard_map/ppermute | solution.py:247
  138.1 1.9 %collective-permute-start.11 = (bf16[2,128,896]{2,1,0:T(8,128)(2,1)S(1)}, bf16[2,128,896]{2,1,0:T(8,128)(2,1)}, u32[]{:S(2)}, u32[]{:S(2)}) collective-permute-start(bf16[2,128,896]{2,1,0:T(8,128)(2,1)S(1)} %bitcast.41), channel_id=1, source_target_pairs={{0,1},{1,0},{2,3},{3,2},{4,5},{5,4},{6,7},{7,6},{8,9},{9,8},{10,11... | collective-permute-start | bytes 1376264 | tf_op jit(solution)/shard_map/ppermute | solution.py:247
  140.1 1.0 copy-start

commit v6 on v5

--- a/solution.py
+++ b/solution.py
@@ -39,7 +39,7 @@
 ZS, XS, CS = 4, 2, 2
 CHIPS = ZS * XS
 HALF = 8
-PER_STEP = 2
+PER_STEP = 4
 ALL = range(ZS * XS * CS)
 
 
@@ -268,19 +268,31 @@
     )
     wanted = jnp.sum(jnp.where(select, row_blk[:, None, None, :], 0), axis=3)
     wanted = lax.dynamic_slice_in_dim(wanted, my_mp & HALF, HALF, 0)
+    my_half = my_mp // HALF
+    chips = CHIPS // 2
+    qg = jnp.stack([queries, grad_out]).reshape(2, HEAD_DIM, CHIPS, -1).transpose(2, 0, 1, 3)
+    qg = qg.reshape((2, chips) + qg.shape[1:])
+    qg_stay = lax.dynamic_index_in_dim(qg, my_half, 0, keepdims=False)
+    qg_go = lax.dynamic_index_in_dim(qg, 1 - my_half, 0, keepdims=False)
     near_rows = pick_rows(wanted[:, 0].reshape(-1), scaled)
-    scaled, turned, near_rows = lax.optimization_barrier((scaled, turned, near_rows))
+    scaled, turned, near_rows, qg_go, qg_stay = lax.optimization_barrier(
+        (scaled, turned, near_rows, qg_go, qg_stay)
+    )
     far = swap(scaled, HALF)
 
-    mine, sends = by_parity(my_c.reshape(1).astype(jnp.int32), jnp.concatenate(turned))
-    came = swap(sends, 1)
-    line_w = jnp.where(
-        my_c == 0,
-        jnp.concatenate([mine, came], axis=1),
-        jnp.concatenate([came, mine], axis=1),
-    ).reshape(ZS, 2, CS * w_kv.shape[1], -1)
-    x_w, y_w = swap(line_w, CS), swap_dp(line_w)
-
+    core = my_c.reshape(1).astype(jnp.int32)
+
+    def parity_rows(line):
+        mine, sends = by_parity(core, line)
+        came = swap(sends, 1)
+        return jnp.where(
+            my_c == 0,
+            jnp.concatenate([mine, came], axis=1),
+            jnp.concatenate([came, mine], axis=1),
+        ).reshape(ZS, 2, CS * w_kv.shape[1], -1)
+
+    line = jnp.concatenate(turned)
+    x_line, y_line = swap(line, CS), swap_dp(line)
 
     shards = lax.dynamic_index_in_dim(shard_blk, my_mp, 0, keepdims=False)
     slots = lax.dynamic_index_in_dim(slot_blk, my_mp, 0, keepdims=False)
@@ -294,26 +306,34 @@
 
     near_pieces = spread(near_rows)
 
-    my_half = my_mp // HALF
-    chips = CHIPS // 2
-    qg = jnp.stack([queries, grad_out]).reshape(2, HEAD_DIM, CHIPS, -1).transpose(2, 0, 1, 3)
-    qg = qg.reshape((2, chips) + qg.shape[1:])
-    qg_stay = lax.dynamic_index_in_dim(qg, my_half, 0, keepdims=False)
-    qg_go = lax.dynamic_index_in_dim(qg, 1 - my_half, 0, keepdims=False)
-
-    far, near_pieces, x_w, y_w, qg_go, row, is_far = lax.optimization_barrier(
-        (far, near_pieces, x_w, y_w, qg_go, row, is_far)
-    )
-    xy_w = swap_dp(x_w)
+    line_w = parity_rows(line)
+    far, near_pieces, x_line, y_line, line_w, row, is_far = lax.optimization_barrier(
+        (far, near_pieces, x_line, y_line, line_w, row, is_far)
+    )
+    xy_line = swap_dp(x_line)
+    x_w, y_w = parity_rows(x_line), parity_rows(y_line)
     far_pieces = spread(pick_rows(wanted[:, 1].reshape(-1), far))
     qg_came = swap(qg_go, HALF)
 
-    far_pieces, qg_came, xy_w = lax.optimization_barrier((far_pieces, qg_came, xy_w))
+    far_pieces, qg_came, xy_line, x_w, y_w = lax.optimization_barrier(
+        (far_pieces, qg_came, xy_line, x_w, y_w)
+    )
+    xy_w = parity_rows(xy_line)
     chip_lines = [
         [HALF * half + CS * chip + core for chip in range(chips)]
         for half in range(2)
         for core in range(CS)
     ]
+    chip_groups = [[CS * chip + core for chip in range(CHIPS)] for core in range(CS)]
+
+    own, give = choose(
+        is_far,
+        row,
+        near_pieces,
+        far_pieces,
+    )
+    give, qg_came = lax.optimization_barrier((give, qg_came))
+    got = swap_dp(give)
     qg = lax.all_to_all(
         jnp.stack([qg_stay, qg_came], axis=1),
         "mp",
@@ -322,15 +342,6 @@
         tiled=True,
         axis_index_groups=chip_lines,
     )
-    chip_groups = [[CS * chip + core for chip in range(CHIPS)] for core in range(CS)]
-
-    own, give = choose(
-        is_far,
-        row,
-        near_pieces,
-        far_pieces,
-    )
-    got = swap_dp(give)
     span_shape = (CH_DEV, NBR * slice_len, E)
     own, got = own.reshape(span_shape), got.reshape(span_shape)
     neighbours = (own, got, swap(own, 1), swap(got, 1))

time: 186 us -> 183 us (0.984)
  waiting for transfers between devices: 79.6 us -> 61.4 us
  local copies, waits for them, and re-layouts: 13.5 us -> 19.2 us
  Pallas kernels: 19.9 us -> 25.5 us
  other arithmetic: 6.95 us -> 10.5 us
    ppermute x6 -> x9, waiting for transfers between devices: 59.5 us -> 45.8 us  [swap(): return lax.ppermute(a, 'mp', [(m, m ^ bits) for m in ALL])]
    pallas_call x1 -> x4, Pallas kernels: 2.32 us -> 9.23 us  [by_parity(): pl.pallas_call(parity_kernel, in_specs=[pl.BlockSpec(memory_space=pltpu.S...]
    unnamed x18 -> x33, local copies, waits for them, and re-layouts: 7.41 us -> 13.6 us
    select_n x1 -> x4, other arithmetic: 1.7 us -> 7.42 us  [parity_rows(): jnp.where(my_c == 0, jnp.concatenate([mine, came], axis=1), jnp.concatena...]
    ppermute x3, waiting for transfers between devices: 10.5 us -> 7.79 us  [swap_dp(): return lax.ppermute(a, 'dp', [(0, 1), (1, 0)])]
    ppermute x3, waiting for transfers between devices: 8.17 us -> 5.73 us  [small(): lax.ppermute(w_kv, 'mp', [(m, (m + XS * CS * r) % len(ALL)) for m in ALL])]
    another operation x1 -> x0, local copies, waits for them, and re-layouts: 2.08 us -> none  [small(): jnp.stack([qg_stay, qg_came], axis=1)]
    ppermute x6 -> x9, starting transfers between devices: 5.52 us -> 6.49 us  [swap(): return lax.ppermute(a, 'mp', [(m, m ^ bits) for m in ALL])]
  transfers between devices with their start and end apart: 15 -> 18, of which waited for: 7 -> 7; matrix products, arithmetic and copies ran while one was open for 7% -> 11% of each run, Pallas kernels for 4% -> 6%
where the time goes in v6:
time: 183 us; the launch traced here: 182 us
  waiting for transfers between devices  61.4 us (34%)
  starting transfers between devices  34.2 us (19%)
  blocking collectives  30.8 us (17%)
  Pallas kernels  25.5 us (14%)
  local copies, waits for them, and re-layouts  19.2 us (10%)
  other arithmetic  10.5 us (6%)
    ppermute x9, waiting for transfers between devices, swap(): return lax.ppermute(a, 'mp', [(m, m ^ bits) for m in ALL])  45.8 us
    all_to_all x1, blocking collectives, small(): lax.all_to_all(result, 'mp', split_axis=0, concat_axis=0, tiled=True, axi...  30.8 us
    unnamed x33, local copies, waits for them, and re-layouts  13.6 us
    all_to_all x2, starting transfers between devices, over_half(): lax.all_to_all(a, 'mp', split_axis=0, concat_axis=0, tiled=True, axis_ind...  11.8 us
    pallas_call x1, Pallas kernels, attend(): pl.pallas_call(attend_kernel, grid_spec=pltpu.PrefetchScalarGridSpec(num_...  9.41 us
    pallas_call x4, Pallas kernels, by_parity(): pl.pallas_call(parity_kernel, in_specs=[pl.BlockSpec(memory_space=pltpu.S...  9.23 us
    ppermute x3, waiting for transfers between devices, swap_dp(): return lax.ppermute(a, 'dp', [(0, 1), (1, 0)])  7.79 us
    select_n x4, other arithmetic, parity_rows(): jnp.where(my_c == 0, jnp.concatenate([mine, came], axis=1), jnp.concatena...  7.42 us
  transfers between devices with their start and end apart: 18, of which 7 were waited for; matrix products, arithmetic and copies ran while one was open for 11% of the time, Pallas kernels for 6%

profile of v6, /device:TPU:0, one launch (start us, length us, event | category | flops | bytes accessed | tf_op | source)
XLA Modules:
  0.0 182.4 jit_solution(8077569393960028646)
XLA Ops:
  0.6 3.1 %collective-permute-start = (bf16[2,56,1024]{2,1,0:T(8,128)(2,1)}, bf16[2,56,1024]{2,1,0:T(8,128)(2,1)S(1)}, u32[]{:S(2)}, u32[]{:S(2)}) collective-permute-start(bf16[2,56,1024]{2,1,0:T(8,128)(2,1)} %param.12), channel_id=1, source_target_pairs={{0,4},{1,5},{2,6},{3,7},{4,8},{5,9},{6,10},{7,11},{8,12},{9,13},{1... | collective-permute-start | bytes 688136 | tf_op jit(solution)/shard_map/ppermute | solution.py:259
  3.7 2.6 %collective-permute-start.1 = (bf16[2,56,1024]{2,1,0:T(8,128)(2,1)}, bf16[2,56,1024]{2,1,0:T(8,128)(2,1)S(1)}, u32[]{:S(2)}, u32[]{:S(2)}) collective-permute-start(bf16[2,56,1024]{2,1,0:T(8,128)(2,1)} %param.12), channel_id=1, source_target_pairs={{0,8},{1,9},{2,10},{3,11},{4,12},{5,13},{6,14},{7,15},{8,0},{9,1},... | collective-permute-start | bytes 688136 | tf_op jit(solution)/shard_map/ppermute | solution.py:259
  6.3 1.3 collective-permute-start.2
  7.7 0.8 copy.35
  8.5 0.1 copy.36
  8.6 0.8 copy.33
  9.4 0.1 copy.34
  9.5 0.1 convert_reduce_fusion
  10.1 1.2 copy.45
  11.2 1.2 copy.44
  12.4 0.2 multiply_convert_fusion.src_ref
  12.6 0.1 maximum_bitcast_fusion
  12.7 0.2 copy.38
  13.0 2.0 %pick_rows.2 = bf16[16,64,896]{2,1,0:T(8,128)(2,1)} custom-call(s32[16]{0:T(128)S(1)} %reshape_squeeze.6.rows_ref, bf16[8,64,896]{2,1,0:T(8,128)(2,1)S(1)} %multiply_convert_fusion.src_ref), custom_call_target="tpu_custom_call" | custom-call | tf_op jit(solution)/shard_map/pick_rows/pallas_call | solution.py:78
  14.9 0.9 dynamic-slice_bitcast_fusion
  15.8 5.7 %collective-permute-done.1 = bf16[2,56,1024]{2,1,0:T(8,128)(2,1)S(1)} collective-permute-done((bf16[2,56,1024]{2,1,0:T(8,128)(2,1)}, bf16[2,56,1024]{2,1,0:T(8,128)(2,1)S(1)}, u32[]{:S(2)}, u32[]{:S(2)}) %collective-permute-start.1) | collective-permute-done | bytes 229408 | tf_op jit(solution)/shard_map/ppermute | solution.py:259
  21.6 0.7 copy-done.9
  22.2 0.1 copy-done.10
  22.3 7.5 %all-to-all-start = ((bf16[8,2,64,896]{3,2,1,0:T(8,128)(2,1)}), bf16[8,2,64,896]{3,2,1,0:T(8,128)(2,1)}, u32[]{:S(2)}, u32[]{:S(2)}) async-start(bf16[8,2,64,896]{3,2,1,0:T(8,128)(2,1)} %bitcast.14), calls=%async_computation | async-start | bytes 3670016 | tf_op jit(solution)/shard_map/all_to_all | solution.py:254
  29.8 1.7 collective-permute-start.3
  31.5 0.7 constant_dynamic-update-slice_fusion.3
  32.2 0.7 constant_dynamic-update-slice_fusion.2
  32.9 1.6 constant_dynamic-update-slice_fusion.1
  34.5 1.6 constant_dynamic-update-slice_fusion.w_ref
  36.1 2.0 %collective-permute-start.4 = (bf16[8,56,1024]{2,1,0:T(8,128)(2,1)}, bf16[8,56,1024]{2,1,0:T(8,128)(2,1)}, u32[]{:S(2)}, u32[]{:S(2)}) collective-permute-start(bf16[8,56,1024]{2,1,0:T(8,128)(2,1)} %constant_dynamic-update-slice_fusion.w_ref), channel_id=1, source_target_pairs={{0,2},{1,3},{2,0},{3,1},{4,6},{5,7},{6,4},{7,5},{8,10},{9,11},{10,... | collective-permute-start | bytes 2752520 | tf_op jit(solution)/shard_map/ppermute | solution.py:247
  38.2 1.5 collective-permute-start.5
  39.7 2.3 %by_parity.4 = (bf16[8,56,512]{2,1,0:T(8,128)(2,1)}, bf16[8,56,512]{2,1,0:T(8,128)(2,1)}) custom-call(s32[1]{0:T(128)} %bitcast.1.core_ref, bf16[8,56,1024]{2,1,0:T(8,128)(2,1)} %constant_dynamic-update-slice_fusion.w_ref), custom_call_target="tpu_custom_call" | custom-call | tf_op jit(solution)/shard_map/by_parity/pallas_call | solution.py:60
  42.0 0.2 and_reduce_fusion
  42.4 0.7 reshape.120.row_ref
  43.1 0.6 reshape.121.far_ref
  43.8 0.2 collective-permute-done.6
  44.0 0.8 copy-done.5
  44.8 1.7 maximum_select_fusion.w_own
  46.6 23.8 %collective-permute-done.3.src_ref = bf16[8,64,896]{2,1,0:T(8,128)(2,1)S(1)} collective-permute-done((bf16[8,64,896]{2,1,0:T(8,128)(2,1)S(1)}, bf16[8,64,896]{2,1,0:T(8,128)(2,1)S(1)}, u32[]{:S(2)}, u32[]{:S(2)}) %collective-permute-start.3) | collective-permute-done | bytes 917536 | tf_op jit(solution)/shard_map/ppermute | solution.py:247
  70.3 2.1 %collective-permute-done.4.w_ref = bf16[8,56,1024]{2,1,0:T(8,128)(2,1)} collective-permute-done((bf16[8,56,1024]{2,1,0:T(8,128)(2,1)}, bf16[8,56,1024]{2,1,0:T(8,128)(2,1)}, u32[]{:S(2)}, u32[]{:S(2)}) %collective-permute-start.4) | collective-permute-done | bytes 917536 | tf_op jit(solution)/shard_map/ppermute | solution.py:247
  72.5 2.0 %pick_rows.3 = bf16[16,64,896]{2,1,0:T(8,128)(2,1)} custom-call(s32[16]{0:T(128)S(1)} %reshape_squeeze.7.rows_ref, bf16[8,64,896]{2,1,0:T(8,128)(2,1)S(1)} %collective-permute-done.3.src_ref), custom_call_target="tpu_custom_call" | custom-call | tf_op jit(solution)/shard_map/pick_rows/pallas_call | solution.py:78
  74.5 4.3 %all-to-all-start.1 = ((bf16[8,2,64,896]{3,2,1,0:T(8,128)(2,1)}), bf16[8,2,64,896]{3,2,1,0:T(8,128)(2,1)}, u32[]{:S(2)}, u32[]{:S(2)}) async-start(bf16[8,2,64,896]{3,2,1,0:T(8,128)(2,1)} %bitcast.18), calls=%async_computation.1 | async-start | bytes 3670016 | tf_op jit(solution)/shard_map/all_to_all | solution.py:254
  78.9 1.6 collective-permute-start.8
  80.4 2.4 %by_parity.5 = (bf16[8,56,512]{2,1,0:T(8,128)(2,1)}, bf16[8,56,512]{2,1,0:T(8,128)(2,1)}) custom-call(s32[1]{0:T(128)} %bitcast.1.core_ref, bf16[8,56,1024]{2,1,0:T(8,128)(2,1)} %collective-permute-done.4.w_ref), custom_call_target="tpu_custom_call" | custom-call | tf_op jit(solution)/shard_map/by_parity/pallas_call | solution.py:60
  82.8 2.3 %by_parity.6 = (bf16[8,56,512]{2,1,0:T(8,128)(2,1)}, bf16[8,56,512]{2,1,0:T(8,128)(2,1)}) custom-call(s32[1]{0:T(128)} %bitcast.1.core_ref, bf16[8,56,1024]{2,1,0:T(8,128)(2,1)} %collective-permute-done.5.w_ref), custom_call_target="tpu_custom_call" | custom-call | tf_op jit(solution)/shard_map/by_parity/pallas_call | solution.py:60
  85.1 0.5 collective-permute-start.10
  85.6 1.8 collective-permute-start.7
  87.4 0.8 copy-done.7
  88.2 1.7 maximum_select_fusion.1.w_x
  90.0 1.3 maximum_select_fusion.2.w_y
  91.3 19.6 %collective-permute-done.7 = bf16[4,2,128,256]{3,2,1,0:T(8,128)(2,1)} collective-permute-done((bf16[4,2,128,256]{3,2,1,0:T(8,128)(2,1)}, bf16[4,2,128,256]{3,2,1,0:T(8,128)(2,1)}, u32[]{:S(2)}, u32[]{:S(2)}) %collective-permute-start.7) | collective-permute-done | bytes 524320 | tf_op jit(solution)/shard_map/ppermute | solution.py:247
  110.9 2.0 %all-to-all-done.1 = bf16[8,2,64,896]{3,2,1,0:T(8,128)(2,1)} async-done(((bf16[8,2,64,896]{3,2,1,0:T(8,128)(2,1)}), bf16[8,2,64,896]{3,2,1,0:T(8,128)(2,1)}, u32[]{:S(2)}, u32[]{:S(2)}) %all-to-all-start.1) | async-done | bytes 1835040 | tf_op jit(solution)/shard_map/all_to_all | solution.py:254
  113.0 2.9 %choose.1 = (bf16[4,64,896]{2,1,0:T(8,128)(2,1)}, bf16[4,64,896]{2,1,0:T(8,128)(2,1)}) custom-call(s32[8]{0:T(128)} %reshape.121.far_ref, s32[8]{0:T(128)} %reshape.120.row_ref, bf16[16,64,896]{2,1,0:T(8,128)(2,1)} %bitcast.15.near, bf16[16,64,896]{2,1,0:T(8,128)(2,1)} %bitcast.19.far), custom_call_target="tpu_custom_call" | custom-call | tf_op jit(solution)/shard_map/choose/pallas_call | solution.py:110
  115.9 2.2 %pad_maximum_fusion = bf16[4,2,2,128,256]{4,3,2,1,0:T(8,128)(2,1)} fusion(bf16[4,1,2,128,256]{4,3,2,1,0:T(8,128)(2,1)} %bitcast.29, bf16[4,1,2,128,256]{4,3,2,1,0:T(8,128)(2,1)S(1)} %bitcast.54), kind=kLoop, calls=%fused_computation.2 | loop fusion | flops 524288 | bytes 2097152 | tf_op jit(solution)/shard_map/stack | solution.py:338
  118.1 4.3 %all-to-all-start.2 = ((bf16[4,2,2,128,256]{4,3,2,1,0:T(8,128)(2,1)}), bf16[4,2,2,128,256]{4,3,2,1,0:T(8,128)(2,1)S(1)}, u32[]{:S(2)}, u32[]{:S(2)}) async-start(bf16[4,2,2,128,256]{4,3,2,1,0:T(8,128)(2,1)} %pad_maximum_fusion), calls=%async_computation.2 | async-start | bytes 2097152 | tf_op jit(solution)/shard_map/all_to_all | solution.py:337
  122.4 1.5 collective-permute-start.11
  123.9 2.3 %by_parity.7 = (bf16[8,56,512]{2,1,0:T(8,128)(2,1)}, bf16[8,56,512]{2,1,0:T(8,128)(2,1)}) custom-call(s32[1]{0:T(128)} %bitcast.1.core_ref, bf16[8,56,1024]{2,1,0:T(8,128)(2,1)} %copy-done.4), custom_call_target="tpu_custom_call" | custom-call | tf_op jit(solution)/shard_map/by_parity/pallas_call | solution.py:60
  126.2 0.5 collective-permute-start.12
  126.7 7.8 %collective-permute-done.11 = bf16[4,64,896]{2,1,0:T(8,128)(2,1)} collective-permute-done((bf16[4,64,896]{2,1,0:T(8,128)(2,1)}, bf16[4,64,896]{2,1,0:T(8,128)(2,1)}, u32[]{:S(2)}, u32[]{:S(2)}) %collective-permute-start.11) | collective-permute-done | bytes 458784 | tf_op jit(solution)/shard_map/ppermute | solution.py:250
  134.5 2.6 %maximum_select_fusion.3.w_xy = bf16[4,2,112,512]{3,2,1,0:T(8,128)(2,1)} fusion(bf16[4,2,56,512]{3,2,1,0:T(8,128)(2,1)} %bitcast.27, bf16[4,2,56,512]{3,2,1,0:T(8,128)(2,1)} %bitcast.59, pred[]{:T(512)S(6)} %eq.69), kind=kLoop, calls=%fused_computation.6 | loop fusion | flops 4128768 | bytes 1835009 | tf_op jit(solution)/shard_map/jit(_where)/select_n | solution.py:288
  137.2 1.2 copy-done
  138.4 1.2 copy-done.1
  139.6 9.4 %attend.1 = bf16[8,2,128,256]{3,2,1,0:T(8,128)(2,1)S(1)} custom-call(s32[4]{0:T(128)S(1)} %pad_add_fusion.2.place_ref, bf16[2,128,896]{2,1,0:T(8,128)(2,1)S(1)} %bitcast.47, bf16[2,128,896]{2,1,0:T(8,128)(2,1)} %bitcast.25.nb, bf16[2,128,896]{2,1,0:T(8,128)(2,1)} %collective-permute-done.12.sa, bf16[2,128,896]{2,1,0:T(8,128)(2,1)} %collective-permute-done.13.sb, ...), custom_call_target="tpu_custom_call" | custom-call | tf_op jit(solution)/shard_map/attend/pallas_call | solution.py:215
  149.0 30.8 %all_to_all.20 = bf16[8,2,128,256]{3,2,1,0:T(8,128)(2,1)S(1)} all-to-all(bf16[8,2,128,256]{3,2,1,0:T(8,128)(2,1)S(1)} %attend.1), channel_id=1, replica_groups={{0,2,4,6,8,10,12,14},{1,3,5,7,9,11,13,15},{16,18,20,22,24,26,28,30},{17..., dimensions={0} | all-to-all | bytes 2097152 | tf_op jit(solution)/shard_map/all_to_all | solution.py:350
  179.7 0.1 fusion
  179.8 0.3 copy.40
  180.1 1.0 copy.42
  181.1 0.3 copy.41
  181.4 1.0 copy.43
  (50 shorter events, 1.1 us)
Async XLA Ops:
  0.6 11.8 %copy-start.3 = (bf16[8,64,896]{2,1,0:T(8,128)(2,1)S(1)}, bf16[8,64,896]{2,1,0:T(8,128)(2,1)}, u32[]{:S(2)}) copy-start(bf16[8,64,896]{2,1,0:T(8,128)(2,1)} %param.10) | copy-start | bytes 2752516
  0.6 11.8 %copy-start.11 = (f32[8,64]{1,0:T(8,128)S(1)}, f32[8,64]{1,0:T(8,128)}, u32[]{:S(2)}) copy-start(f32[8,64]{1,0:T(8,128)} %param.11) | copy-start | bytes 6148
  0.6 15.2 %collective-permute-start = (bf16[2,56,1024]{2,1,0:T(8,128)(2,1)}, bf16[2,56,1024]{2,1,0:T(8,128)(2,1)S(1)}, u32[]{:S(2)}, u32[]{:S(2)}) collective-permute-start(bf16[2,56,1024]{2,1,0:T(8,128)(2,1)} %param.12), channel_id=1, source_target_pairs={{0,4},{1,5},{2,6},{3,7},{4,8},{5,9},{6,10},{7,11},{8,12},{9,13},{1... | collective-permute-start | bytes 688136 | tf_op jit(solution)/shard_map/ppermute | solution.py:259
  3.7 17.8 %collective-permute-start.1 = (bf16[2,56,1024]{2,1,0:T(8,128)(2,1)}, bf16[2,56,1024]{2,1,0:T(8,128)(2,1)S(1)}, u32[]{:S(2)}, u32[]{:S(2)}) collective-permute-start(bf16[2,56,1024]{2,1,0:T(8,128)(2,1)} %param.12), channel_id=1, source_target_pairs={{0,8},{1,9},{2,10},{3,11},{4,12},{5,13},{6,14},{7,15},{8,0},{9,1},... | collective-permute-start | bytes 688136 | tf_op jit(solution)/shard_map/ppermute | solution.py:259
  6.3 15.2 %collective-permute-start.2 = (bf16[2,56,1024]{2,1,0:T(8,128)(2,1)}, bf16[2,56,1024]{2,1,0:T(8,128)(2,1)S(1)}, u32[]{:S(2)}, u32[]{:S(2)}) collective-permute-start(bf16[2,56,1024]{2,1,0:T(8,128)(2,1)} %param.12), channel_id=1, source_target_pairs={{0,12},{1,13},{2,14},{3,15},{4,0},{5,1},{6,2},{7,3},{8,4},{9,5},{1... | collective-permute-start | bytes 688136 | tf_op jit(solution)/shard_map/ppermute | solution.py:259
  21.5 0.7 copy-start.9
  21.5 0.8 copy-start.10
  21.5 9.9 %copy-start.8 = (bf16[2,56,1024]{2,1,0:T(8,128)(2,1)S(1)}, bf16[2,56,1024]{2,1,0:T(8,128)(2,1)}, u32[]{:S(2)}) copy-start(bf16[2,56,1024]{2,1,0:T(8,128)(2,1)} %param.12) | copy-start | bytes 688132
  22.3 50.2 %all-to-all-start = ((bf16[8,2,64,896]{3,2,1,0:T(8,128)(2,1)}), bf16[8,2,64,896]{3,2,1,0:T(8,128)(2,1)}, u32[]{:S(2)}, u32[]{:S(2)}) async-start(bf16[8,2,64,896]{3,2,1,0:T(8,128)(2,1)} %bitcast.14), calls=%async_computation | async-start | bytes 3670016 | tf_op jit(solution)/shard_map/all_to_all | solution.py:254
  29.8 40.5 %collective-permute-start.3 = (bf16[8,64,896]{2,1,0:T(8,128)(2,1)S(1)}, bf16[8,64,896]{2,1,0:T(8,128)(2,1)S(1)}, u32[]{:S(2)}, u32[]{:S(2)}) collective-permute-start(bf16[8,64,896]{2,1,0:T(8,128)(2,1)S(1)} %multiply_convert_fusion.src_ref), channel_id=1, source_target_pairs={{0,8},{1,9},{2,10},{3,11},{4,12},{5,13},{6,14},{7,15},{8,0},{9,1},... | collective-permute-start | bytes 2752520 | tf_op jit(solution)/shard_map/ppermute | solution.py:247
  36.1 36.3 %collective-permute-start.4 = (bf16[8,56,1024]{2,1,0:T(8,128)(2,1)}, bf16[8,56,1024]{2,1,0:T(8,128)(2,1)}, u32[]{:S(2)}, u32[]{:S(2)}) collective-permute-start(bf16[8,56,1024]{2,1,0:T(8,128)(2,1)} %constant_dynamic-update-slice_fusion.w_ref), channel_id=1, source_target_pairs={{0,2},{1,3},{2,0},{3,1},{4,6},{5,7},{6,4},{7,5},{8,10},{9,11},{10,... | collective-permute-start | bytes 2752520 | tf_op jit(solution)/shard_map/ppermute | solution.py:247
  38.2 34.3 %collective-permute-start.5 = (bf16[8,56,1024]{2,1,0:T(8,128)(2,1)}, bf16[8,56,1024]{2,1,0:T(8,128)(2,1)}, u32[]{:S(2)}, u32[]{:S(2)}) collective-permute-start(bf16[8,56,1024]{2,1,0:T(8,128)(2,1)} %constant_dynamic-update-slice_fusion.w_ref), channel_id=1, source_target_pairs={{0,16},{16,0},{1,17},{17,1},{2,18},{18,2},{3,19},{19,3},{4,20},{20... | collective-permute-start | bytes 2752520 | tf_op jit(solution)/shard_map/ppermute | solution.py:250
  42.0 2.0 %collective-permute-start.6 = (bf16[8,56,512]{2,1,0:T(8,128)(2,1)}, bf16[8,56,512]{2,1,0:T(8,128)(2,1)S(1)}, u32[]{:S(2)}, u32[]{:S(2)}) collective-permute-start(bf16[8,56,512]{2,1,0:T(8,128)(2,1)} %get-tuple-element.42), channel_id=1, source_target_pairs={{0,1},{1,0},{2,3},{3,2},{4,5},{5,4},{6,7},{7,6},{8,9},{9,8},{10,11... | collective-permute-start | bytes 1376264 | tf_op jit(solution)/shard_map/ppermute | solution.py:247
  44.0 0.8 copy-start.5
  74.5 38.4 %all-to-all-start.1 = ((bf16[8,2,64,896]{3,2,1,0:T(8,128)(2,1)}), bf16[8,2,64,896]{3,2,1,0:T(8,128)(2,1)}, u32[]{:S(2)}, u32[]{:S(2)}) async-start(bf16[8,2,64,896]{3,2,1,0:T(8,128)(2,1)} %bitcast.18), calls=%async_computation.1 | async-start | bytes 3670016 | tf_op jit(solution)/shard_map/all_to_all | solution.py:254
  78.9 32.1 %collective-permute-start.8 = (bf16[8,56,1024]{2,1,0:T(8,128)(2,1)}, bf16[8,56,1024]{2,1,0:T(8,128)(2,1)S(1)}, u32[]{:S(2)}, u32[]{:S(2)}) collective-permute-start(bf16[8,56,1024]{2,1,0:T(8,128)(2,1)} %collective-permute-done.4.w_ref), channel_id=1, source_target_pairs={{0,16},{16,0},{1,17},{17,1},{2,18},{18,2},{3,19},{19,3},{4,20},{20... | collective-permute-start | bytes 2752520 | tf_op jit(solution)/shard_map/ppermute | solution.py:250
  82.8 4.6 %collective-permute-start.9 = (bf16[8,56,512]{2,1,0:T(8,128)(2,1)}, bf16[8,56,512]{2,1,0:T(8,128)(2,1)S(1)}, u32[]{:S(2)}, u32[]{:S(2)}) collective-permute-start(bf16[8,56,512]{2,1,0:T(8,128)(2,1)} %get-tuple-element.50), channel_id=1, source_target_pairs={{0,1},{1,0},{2,3},{3,2},{4,5},{5,4},{6,7},{7,6},{8,9},{9,8},{10,11... | collective-permute-start | bytes 1376264 | tf_op jit(solution)/shard_map/ppermute | solution.py:247
  85.1 4.8 %copy-start.6 = (bf16[8,56,512]{2,1,0:T(8,128)(2,1)S(1)}, bf16[8,56,512]{2,1,0:T(8,128)(2,1)}, u32[]{:S(2)}) copy-start(bf16[8,56,512]{2,1,0:T(8,128)(2,1)} %get-tuple-element.52) | copy-start | bytes 1376260
  85.1 4.8 %collective-permute-start.10 = (bf16[8,56,512]{2,1,0:T(8,128)(2,1)}, bf16[8,56,512]{2,1,0:T(8,128)(2,1)S(1)}, u32[]{:S(2)}, u32[]{:S(2)}) collective-permute-start(bf16[8,56,512]{2,1,0:T(8,128)(2,1)} %get-tuple-element.53), channel_id=1, source_target_pairs={{0,1},{1,0},{2,3},{3,2},{4,5},{5,4},{6,7},{7,6},{8,9},{9,8},{10,11... | collective-permute-start | bytes 1376264 | tf_op jit(solution)/shard_map/ppermute | solution.py:247
  85.6 25.3 %collective-permute-start.7 = (bf16[4,2,128,256]{3,2,1,0:T(8,128)(2,1)}, bf16[4,2,128,256]{3,2,1,0:T(8,128)(2,1)}, u32[]{:S(2)}, u32[]{:S(2)}) collective-permute-start(bf16[4,2,128,256]{3,2,1,0:T(8,128)(2,1)} %get-tuple-element.47), channel_id=1, source_target_pairs={{0,8},{1,9},{2,10},{3,11},{4,12},{5,13},{6,14},{7,15},{8,0},{9,1},... | collective-permute-start | bytes 1572872 | tf_op jit(solution)/shard_map/ppermute | solution.py:247
  87.4 0.8 copy-start.7
  110.9 5.0 %copy-start.4 = (bf16[8,56,1024]{2,1,0:T(8,128)(2,1)}, bf16[8,56,1024]{2,1,0:T(8,128)(2,1)S(1)}, u32[]{:S(2)}) copy-start(bf16[8,56,1024]{2,1,0:T(8,128)(2,1)S(1)} %collective-permute-done.8.w_ref) | copy-start | bytes 2752516
  118.1 8.1 %copy-start.2 = (bf16[4,64,896]{2,1,0:T(8,128)(2,1)S(1)}, bf16[4,64,896]{2,1,0:T(8,128)(2,1)}, u32[]{:S(2)}) copy-start(bf16[4,64,896]{2,1,0:T(8,128)(2,1)} %get-tuple-element.55) | copy-start | bytes 1376260
  118.1 19.1 %all-to-all-start.2 = ((bf16[4,2,2,128,256]{4,3,2,1,0:T(8,128)(2,1)}), bf16[4,2,2,128,256]{4,3,2,1,0:T(8,128)(2,1)S(1)}, u32[]{:S(2)}, u32[]{:S(2)}) async-start(bf16[4,2,2,128,256]{4,3,2,1,0:T(8,128)(2,1)} %pad_maximum_fusion), calls=%async_computation.2 | async-start | bytes 2097152 | tf_op jit(solution)/shard_map/all_to_all | solution.py:337
  122.4 12.1 %collective-permute-start.11 = (bf16[4,64,896]{2,1,0:T(8,128)(2,1)}, bf16[4,64,896]{2,1,0:T(8,128)(2,1)}, u32[]{:S(2)}, u32[]{:S(2)}) collective-permute-start(bf16[4,64,896]{2,1,0:T(8,128)(2,1)} %get-tuple-element.58), channel_id=1, source_target_pairs={{0,16},{16,0},{1,17},{17,1},{2,18},{18,2},{3,19},{19,3},{4,20},{20... | collective-permute-start | bytes 1376264 | tf_op jit(solution)/shard_map/ppermute | solution.py:250
  126.2 8.4 %collective-permute-start.14 = (bf16[8,56,512]{2,1,0:T(8,128)(2,1)}, bf16[8,56,512]{2,1,0:T(8,128)(2,1)}, u32[]{:S(2)}, u32[]{:S(2)}) collective-permute-start(bf16[8,56,512]{2,1,0:T(8,128)(2,1)} %get-tuple-element.64), channel_id=1, source_target_pairs={{0,1},{1,0},{2,3},{3,2},{4,5},{5,4},{6,7},{7,6},{8,9},{9,8},{10,11... | collective-permute-start | bytes 1376264 | tf_op jit(solution)/shard_map/ppermute | solution.py:247
  126.2 11.0 %collective-permute-start.12 = (bf16[2,128,896]{2,1,0:T(8,128)(2,1)S(1)}, bf16[2,128,896]{2,1,0:T(8,128)(2,1)}, u32[]{:S(2)}, u32[]{:S(2)}) collective-permute-start(bf16[2,128,896]{2,1,0:T(8,128)(2,1)S(1)} %bitcast.46), channel_id=1, source_target_pairs={{0,1},{1,0},{2,3},{3,2},{4,5},{5,4},{6,7},{7,6},{8,9},{9,8},{10,11... | collective-permute-start | bytes 1376264 | tf_op jit(solution)/shard_map/ppermute | solution.py:247
  134.4 2.7 %collective-permute-start.13 = (bf16[2,128,896]{2,1,0:T(8,128)(2,1)}, bf16[2,128,896]{2,1,0:T(8,128)(2,1)}, u32[]{:S(2)}, u32[]{:S(2)}) collective-permute-start(bf16[2,128,896]{2,1,0:T(8,128)(2,1)} %bitcast.25.nb), channel_id=1, source_target_pairs={{0,1},{1,0},{2,3},{3,2},{4,5},{5,4},{6,7},{7,6},{8,9},{9,8},{10,11... | collective-permute-start | bytes 1376264 | tf_op jit(solution)/shard_map/ppermute | solution.py:247
  137.2 1.2 copy-start
  138.4 1.2 copy-start.1

commit v7 on v6

--- a/solution.py
+++ b/solution.py
@@ -127,7 +127,7 @@
 
 
 def attend_kernel(
-    place_ref, na, nb, sa, sb, w_own, w_x, w_y, w_xy, qg_ref, out_ref, n_scr, w_scr
+    place_ref, na, nb, sa, sb, w_own, w_x, w_y, mine, came, qg_ref, out_ref, n_scr, w_scr
 ):
     my_c, my_x, my_z = place_ref[1], place_ref[2], place_ref[3]
     rows, width = w_scr.shape[0] // CHIPS, w_scr.shape[1] // 2
@@ -139,24 +139,34 @@
                 n_scr[CH_DEV * core + s, 0:NT, :] = first[s]
                 n_scr[CH_DEV * core + s, NT : 2 * NT, :] = second[s]
 
-    def put(*sources):
+    def spot(r, other):
+        src_z = lax.rem(my_z - r + ZS, ZS)
+        return pl.ds(pl.multiple_of((src_z * XS + (my_x ^ other)) * rows, 16), rows)
+
+    def put(ref, other):
         for r in range(ZS):
-            src_z = lax.rem(my_z - r + ZS, ZS)
-            for other, ref in enumerate(sources):
-                at = pl.multiple_of((src_z * XS + (my_x ^ other)) * rows, 16)
-                for kv in range(2):
-                    lanes = slice(width * kv, width * (kv + 1))
-                    w_scr[pl.ds(at, rows), lanes] = ref[r, kv]
+            for kv in range(2):
+                w_scr[spot(r, other), width * kv : width * (kv + 1)] = ref[r, kv]
+
+    def put_parts(other):
+        for r in range(ZS):
+            for kv in range(2):
+                m, c = (a[2 * r + kv].astype(jnp.float32) for a in (mine, came))
+                both_rows = [jnp.where(my_c == 0, m, c), jnp.where(my_c == 0, c, m)]
+                block = jnp.concatenate(both_rows, axis=0).astype(jnp.bfloat16)
+                w_scr[spot(r, other), width * kv : width * (kv + 1)] = block
 
     own_dp = pl.program_id(0) < pl.num_programs(0) // 2
 
     @pl.when(own_dp)
     def _():
-        put(w_own, w_x)
+        put(w_own, 0)
+        put(w_x, 1)
 
     @pl.when(jnp.logical_not(own_dp))
     def _():
-        put(w_y, w_xy)
+        put(w_y, 0)
+        put_parts(1)
 
     weights = w_scr[...]
     kvs = [ndot(n_scr[s], weights).astype(jnp.bfloat16) for s in range(CS * CH_DEV)]
@@ -220,7 +230,8 @@
             in_specs=[
                 pl.BlockSpec(a.shape, lambda i, place: (0, 0, 0)) for a in neighbours
             ]
-            + [first, first, last, last]
+            + [first, first, last]
+            + [pl.BlockSpec(a.shape, lambda i, place: (0, 0, 0)) for a in weights[3:]]
             + [pl.BlockSpec(block[:1] + (1,) + block[1:], came_at)],
             out_specs=head_block,
             scratch_shapes=[
@@ -318,7 +329,8 @@
     far_pieces, qg_came, xy_line, x_w, y_w = lax.optimization_barrier(
         (far_pieces, qg_came, xy_line, x_w, y_w)
     )
-    xy_w = parity_rows(xy_line)
+    xy_mine, xy_sends = by_parity(core, xy_line)
+    xy_came = swap(xy_sends, 1)
     chip_lines = [
         [HALF * half + CS * chip + core for chip in range(chips)]
         for half in range(2)
@@ -346,7 +358,7 @@
     own, got = own.reshape(span_shape), got.reshape(span_shape)
     neighbours = (own, got, swap(own, 1), swap(got, 1))
 
-    result = attend(place, neighbours, (line_w, x_w, y_w, xy_w), qg)
+    result = attend(place, neighbours, (line_w, x_w, y_w, xy_mine, xy_came), qg)
     back = lax.all_to_all(
         result, "mp", split_axis=0, concat_axis=0, tiled=True, axis_index_groups=chip_groups
     )

time: 183 us -> 182 us (level)
  waiting for transfers between devices: 61.4 us -> 64.2 us
  other arithmetic: 10.5 us -> 7.83 us
    ppermute x9, waiting for transfers between devices: 45.8 us -> 48.6 us  [swap(): return lax.ppermute(a, 'mp', [(m, m ^ bits) for m in ALL])]
    select_n x4 -> x3, other arithmetic: 7.42 us -> 4.75 us  [parity_rows(): jnp.where(my_c == 0, jnp.concatenate([mine, came], axis=1), jnp.concatena...]
    unnamed x33 -> x31, local copies, waits for them, and re-layouts: 13.6 us -> 12.8 us
  transfers between devices with their start and end apart: 18 -> 18, of which waited for: 7 -> 8; matrix products, arithmetic and copies ran while one was open for 11% -> 10% of each run, Pallas kernels for 6% -> 6%
where the time goes in v7:
time: 182 us; the launch traced here: 181 us
  waiting for transfers between devices  64.2 us (35%)
  starting transfers between devices  34.1 us (19%)
  blocking collectives  30.4 us (17%)
  Pallas kernels  25.8 us (14%)
  local copies, waits for them, and re-layouts  18.2 us (10%)
  other arithmetic  7.83 us (4%)
    ppermute x9, waiting for transfers between devices, swap(): return lax.ppermute(a, 'mp', [(m, m ^ bits) for m in ALL])  48.6 us
    all_to_all x1, blocking collectives, small(): lax.all_to_all(result, 'mp', split_axis=0, concat_axis=0, tiled=True, axi...  30.4 us
    unnamed x31, local copies, waits for them, and re-layouts  12.8 us
    all_to_all x2, starting transfers between devices, over_half(): lax.all_to_all(a, 'mp', split_axis=0, concat_axis=0, tiled=True, axis_ind...  11.8 us
    pallas_call x1, Pallas kernels, attend(): pl.pallas_call(attend_kernel, grid_spec=pltpu.PrefetchScalarGridSpec(num_...  9.67 us
    pallas_call x4, Pallas kernels, by_parity(): pl.pallas_call(parity_kernel, in_specs=[pl.BlockSpec(memory_space=pltpu.S...  9.27 us
    ppermute x3, waiting for transfers between devices, swap_dp(): return lax.ppermute(a, 'dp', [(0, 1), (1, 0)])  7.76 us
    ppermute x3, starting transfers between devices, small(): lax.ppermute(w_kv, 'mp', [(m, (m + XS * CS * r) % len(ALL)) for m in ALL])  7.01 us
  transfers between devices with their start and end apart: 18, of which 8 were waited for; matrix products, arithmetic and copies ran while one was open for 10% of the time, Pallas kernels for 6%

profile of v7, /device:TPU:0, one launch (start us, length us, event | category | flops | bytes accessed | tf_op | source)
XLA Modules:
  0.0 181.4 jit_solution(17516688838536417512)
XLA Ops:
  0.6 3.1 %collective-permute-start = (bf16[2,56,1024]{2,1,0:T(8,128)(2,1)}, bf16[2,56,1024]{2,1,0:T(8,128)(2,1)S(1)}, u32[]{:S(2)}, u32[]{:S(2)}) collective-permute-start(bf16[2,56,1024]{2,1,0:T(8,128)(2,1)} %param.12), channel_id=1, source_target_pairs={{0,4},{1,5},{2,6},{3,7},{4,8},{5,9},{6,10},{7,11},{8,12},{9,13},{1... | collective-permute-start | bytes 688136 | tf_op jit(solution)/shard_map/ppermute | solution.py:270
  3.7 2.6 %collective-permute-start.1 = (bf16[2,56,1024]{2,1,0:T(8,128)(2,1)}, bf16[2,56,1024]{2,1,0:T(8,128)(2,1)S(1)}, u32[]{:S(2)}, u32[]{:S(2)}) collective-permute-start(bf16[2,56,1024]{2,1,0:T(8,128)(2,1)} %param.12), channel_id=1, source_target_pairs={{0,8},{1,9},{2,10},{3,11},{4,12},{5,13},{6,14},{7,15},{8,0},{9,1},... | collective-permute-start | bytes 688136 | tf_op jit(solution)/shard_map/ppermute | solution.py:270
  6.3 1.3 collective-permute-start.2
  7.7 0.8 copy.35
  8.5 0.1 copy.36
  8.6 0.8 copy.33
  9.4 0.1 copy.34
  9.5 0.1 convert_reduce_fusion
  9.9 0.1 copy.37
  10.1 1.2 copy.45
  11.2 1.2 copy.44
  12.4 0.2 multiply_convert_fusion.src_ref
  12.6 0.1 maximum_bitcast_fusion
  12.7 0.2 copy.38
  13.0 2.0 %pick_rows.2 = bf16[16,64,896]{2,1,0:T(8,128)(2,1)} custom-call(s32[16]{0:T(128)S(1)} %reshape_squeeze.6.rows_ref, bf16[8,64,896]{2,1,0:T(8,128)(2,1)S(1)} %multiply_convert_fusion.src_ref), custom_call_target="tpu_custom_call" | custom-call | tf_op jit(solution)/shard_map/pick_rows/pallas_call | solution.py:78
  14.9 0.9 dynamic-slice_bitcast_fusion
  15.8 5.7 %collective-permute-done.1 = bf16[2,56,1024]{2,1,0:T(8,128)(2,1)S(1)} collective-permute-done((bf16[2,56,1024]{2,1,0:T(8,128)(2,1)}, bf16[2,56,1024]{2,1,0:T(8,128)(2,1)S(1)}, u32[]{:S(2)}, u32[]{:S(2)}) %collective-permute-start.1) | collective-permute-done | bytes 229408 | tf_op jit(solution)/shard_map/ppermute | solution.py:270
  21.6 0.7 copy-done.8
  22.2 0.1 copy-done.9
  22.3 7.5 %all-to-all-start = ((bf16[8,2,64,896]{3,2,1,0:T(8,128)(2,1)}), bf16[8,2,64,896]{3,2,1,0:T(8,128)(2,1)}, u32[]{:S(2)}, u32[]{:S(2)}) async-start(bf16[8,2,64,896]{3,2,1,0:T(8,128)(2,1)} %bitcast.14), calls=%async_computation | async-start | bytes 3670016 | tf_op jit(solution)/shard_map/all_to_all | solution.py:265
  29.8 1.7 collective-permute-start.3
  31.5 0.7 constant_dynamic-update-slice_fusion.3
  32.2 0.7 constant_dynamic-update-slice_fusion.2
  32.9 1.6 constant_dynamic-update-slice_fusion.1
  34.6 1.6 constant_dynamic-update-slice_fusion.w_ref
  36.2 2.0 %collective-permute-start.4 = (bf16[8,56,1024]{2,1,0:T(8,128)(2,1)}, bf16[8,56,1024]{2,1,0:T(8,128)(2,1)}, u32[]{:S(2)}, u32[]{:S(2)}) collective-permute-start(bf16[8,56,1024]{2,1,0:T(8,128)(2,1)} %constant_dynamic-update-slice_fusion.w_ref), channel_id=1, source_target_pairs={{0,2},{1,3},{2,0},{3,1},{4,6},{5,7},{6,4},{7,5},{8,10},{9,11},{10,... | collective-permute-start | bytes 2752520 | tf_op jit(solution)/shard_map/ppermute | solution.py:258
  38.2 1.5 collective-permute-start.5
  39.7 2.3 %by_parity.4 = (bf16[8,56,512]{2,1,0:T(8,128)(2,1)}, bf16[8,56,512]{2,1,0:T(8,128)(2,1)}) custom-call(s32[1]{0:T(128)} %bitcast.1.core_ref, bf16[8,56,1024]{2,1,0:T(8,128)(2,1)} %constant_dynamic-update-slice_fusion.w_ref), custom_call_target="tpu_custom_call" | custom-call | tf_op jit(solution)/shard_map/by_parity/pallas_call | solution.py:60
  42.1 0.2 and_reduce_fusion
  42.5 0.6 reshape.115.row_ref
  43.1 0.6 reshape.116.far_ref
  43.8 0.4 collective-permute-done.6
  44.2 1.7 maximum_select_fusion.w_own
  45.9 24.4 %collective-permute-done.3.src_ref = bf16[8,64,896]{2,1,0:T(8,128)(2,1)S(1)} collective-permute-done((bf16[8,64,896]{2,1,0:T(8,128)(2,1)S(1)}, bf16[8,64,896]{2,1,0:T(8,128)(2,1)S(1)}, u32[]{:S(2)}, u32[]{:S(2)}) %collective-permute-start.3) | collective-permute-done | bytes 917536 | tf_op jit(solution)/shard_map/ppermute | solution.py:258
  70.4 2.1 %collective-permute-done.4.w_ref = bf16[8,56,1024]{2,1,0:T(8,128)(2,1)} collective-permute-done((bf16[8,56,1024]{2,1,0:T(8,128)(2,1)}, bf16[8,56,1024]{2,1,0:T(8,128)(2,1)}, u32[]{:S(2)}, u32[]{:S(2)}) %collective-permute-start.4) | collective-permute-done | bytes 917536 | tf_op jit(solution)/shard_map/ppermute | solution.py:258
  72.5 2.0 %pick_rows.3 = bf16[16,64,896]{2,1,0:T(8,128)(2,1)} custom-call(s32[16]{0:T(128)S(1)} %reshape_squeeze.7.rows_ref, bf16[8,64,896]{2,1,0:T(8,128)(2,1)S(1)} %collective-permute-done.3.src_ref), custom_call_target="tpu_custom_call" | custom-call | tf_op jit(solution)/shard_map/pick_rows/pallas_call | solution.py:78
  74.5 4.3 %all-to-all-start.1 = ((bf16[8,2,64,896]{3,2,1,0:T(8,128)(2,1)}), bf16[8,2,64,896]{3,2,1,0:T(8,128)(2,1)}, u32[]{:S(2)}, u32[]{:S(2)}) async-start(bf16[8,2,64,896]{3,2,1,0:T(8,128)(2,1)} %bitcast.18), calls=%async_computation.1 | async-start | bytes 3670016 | tf_op jit(solution)/shard_map/all_to_all | solution.py:265
  78.9 1.6 collective-permute-start.8
  80.4 2.4 %by_parity.5 = (bf16[8,56,512]{2,1,0:T(8,128)(2,1)}, bf16[8,56,512]{2,1,0:T(8,128)(2,1)}) custom-call(s32[1]{0:T(128)} %bitcast.1.core_ref, bf16[8,56,1024]{2,1,0:T(8,128)(2,1)} %collective-permute-done.4.w_ref), custom_call_target="tpu_custom_call" | custom-call | tf_op jit(solution)/shard_map/by_parity/pallas_call | solution.py:60
  82.9 2.3 %by_parity.6 = (bf16[8,56,512]{2,1,0:T(8,128)(2,1)}, bf16[8,56,512]{2,1,0:T(8,128)(2,1)}) custom-call(s32[1]{0:T(128)} %bitcast.1.core_ref, bf16[8,56,1024]{2,1,0:T(8,128)(2,1)} %collective-permute-done.5.w_ref), custom_call_target="tpu_custom_call" | custom-call | tf_op jit(solution)/shard_map/by_parity/pallas_call | solution.py:60
  85.1 0.5 collective-permute-start.10
  85.6 1.8 collective-permute-start.7
  87.4 0.8 copy-done.6
  88.3 1.7 maximum_select_fusion.1.w_x
  90.0 1.3 maximum_select_fusion.2.w_y
  91.3 19.6 %collective-permute-done.7 = bf16[4,2,128,256]{3,2,1,0:T(8,128)(2,1)} collective-permute-done((bf16[4,2,128,256]{3,2,1,0:T(8,128)(2,1)}, bf16[4,2,128,256]{3,2,1,0:T(8,128)(2,1)}, u32[]{:S(2)}, u32[]{:S(2)}) %collective-permute-start.7) | collective-permute-done | bytes 524320 | tf_op jit(solution)/shard_map/ppermute | solution.py:258
  110.9 2.0 %all-to-all-done.1 = bf16[8,2,64,896]{3,2,1,0:T(8,128)(2,1)} async-done(((bf16[8,2,64,896]{3,2,1,0:T(8,128)(2,1)}), bf16[8,2,64,896]{3,2,1,0:T(8,128)(2,1)}, u32[]{:S(2)}, u32[]{:S(2)}) %all-to-all-start.1) | async-done | bytes 1835040 | tf_op jit(solution)/shard_map/all_to_all | solution.py:265
  113.0 2.9 %choose.1 = (bf16[4,64,896]{2,1,0:T(8,128)(2,1)}, bf16[4,64,896]{2,1,0:T(8,128)(2,1)}) custom-call(s32[8]{0:T(128)} %reshape.116.far_ref, s32[8]{0:T(128)} %reshape.115.row_ref, bf16[16,64,896]{2,1,0:T(8,128)(2,1)} %bitcast.15.near, bf16[16,64,896]{2,1,0:T(8,128)(2,1)} %bitcast.19.far), custom_call_target="tpu_custom_call" | custom-call | tf_op jit(solution)/shard_map/choose/pallas_call | solution.py:110
  115.9 2.2 %pad_maximum_fusion = bf16[4,2,2,128,256]{4,3,2,1,0:T(8,128)(2,1)} fusion(bf16[4,1,2,128,256]{4,3,2,1,0:T(8,128)(2,1)} %bitcast.27, bf16[4,1,2,128,256]{4,3,2,1,0:T(8,128)(2,1)S(1)} %bitcast.52), kind=kLoop, calls=%fused_computation.2 | loop fusion | flops 524288 | bytes 2097152 | tf_op jit(solution)/shard_map/stack | solution.py:350
  118.1 4.2 %all-to-all-start.2 = ((bf16[4,2,2,128,256]{4,3,2,1,0:T(8,128)(2,1)}), bf16[4,2,2,128,256]{4,3,2,1,0:T(8,128)(2,1)S(1)}, u32[]{:S(2)}, u32[]{:S(2)}) async-start(bf16[4,2,2,128,256]{4,3,2,1,0:T(8,128)(2,1)} %pad_maximum_fusion), calls=%async_computation.2 | async-start | bytes 2097152 | tf_op jit(solution)/shard_map/all_to_all | solution.py:349
  122.3 1.5 collective-permute-start.11
  123.8 2.3 %by_parity.7 = (bf16[8,56,512]{2,1,0:T(8,128)(2,1)}, bf16[8,56,512]{2,1,0:T(8,128)(2,1)}) custom-call(s32[1]{0:T(128)} %bitcast.1.core_ref, bf16[8,56,1024]{2,1,0:T(8,128)(2,1)} %copy-done.4), custom_call_target="tpu_custom_call" | custom-call | tf_op jit(solution)/shard_map/by_parity/pallas_call | solution.py:60
  126.1 0.5 collective-permute-start.14
  126.6 7.8 %collective-permute-done.11 = bf16[4,64,896]{2,1,0:T(8,128)(2,1)} collective-permute-done((bf16[4,64,896]{2,1,0:T(8,128)(2,1)}, bf16[4,64,896]{2,1,0:T(8,128)(2,1)}, u32[]{:S(2)}, u32[]{:S(2)}) %collective-permute-start.11) | collective-permute-done | bytes 458784 | tf_op jit(solution)/shard_map/ppermute | solution.py:261
  134.4 2.1 %collective-permute-done.13.sb = bf16[2,128,896]{2,1,0:T(8,128)(2,1)} collective-permute-done((bf16[2,128,896]{2,1,0:T(8,128)(2,1)}, bf16[2,128,896]{2,1,0:T(8,128)(2,1)}, u32[]{:S(2)}, u32[]{:S(2)}) %collective-permute-start.13) | collective-permute-done | bytes 458784 | tf_op jit(solution)/shard_map/ppermute | solution.py:258
  136.5 1.2 copy-done
  137.7 1.0 copy-done.2
  138.7 9.7 %attend.1 = bf16[8,2,128,256]{3,2,1,0:T(8,128)(2,1)S(1)} custom-call(s32[4]{0:T(128)S(1)} %pad_add_fusion.2.place_ref, bf16[2,128,896]{2,1,0:T(8,128)(2,1)S(1)} %bitcast.45, bf16[2,128,896]{2,1,0:T(8,128)(2,1)} %bitcast.25.nb, bf16[2,128,896]{2,1,0:T(8,128)(2,1)} %collective-permute-done.12.sa, bf16[2,128,896]{2,1,0:T(8,128)(2,1)} %collective-permute-done.13.sb, ...), custom_call_target="tpu_custom_call" | custom-call | tf_op jit(solution)/shard_map/attend/pallas_call | solution.py:225
  148.4 30.4 %all_to_all.20 = bf16[8,2,128,256]{3,2,1,0:T(8,128)(2,1)S(1)} all-to-all(bf16[8,2,128,256]{3,2,1,0:T(8,128)(2,1)S(1)} %attend.1), channel_id=1, replica_groups={{0,2,4,6,8,10,12,14},{1,3,5,7,9,11,13,15},{16,18,20,22,24,26,28,30},{17..., dimensions={0} | all-to-all | bytes 2097152 | tf_op jit(solution)/shard_map/all_to_all | solution.py:362
  178.8 0.1 fusion
  178.9 0.3 copy.40
  179.1 1.0 copy.42
  180.2 0.3 copy.41
  180.4 1.0 copy.43
  (47 shorter events, 1.1 us)
Async XLA Ops:
  0.6 11.8 %copy-start.3 = (bf16[8,64,896]{2,1,0:T(8,128)(2,1)S(1)}, bf16[8,64,896]{2,1,0:T(8,128)(2,1)}, u32[]{:S(2)}) copy-start(bf16[8,64,896]{2,1,0:T(8,128)(2,1)} %param.10) | copy-start | bytes 2752516
  0.6 11.8 %copy-start.10 = (f32[8,64]{1,0:T(8,128)S(1)}, f32[8,64]{1,0:T(8,128)}, u32[]{:S(2)}) copy-start(f32[8,64]{1,0:T(8,128)} %param.11) | copy-start | bytes 6148
  0.6 15.2 %collective-permute-start = (bf16[2,56,1024]{2,1,0:T(8,128)(2,1)}, bf16[2,56,1024]{2,1,0:T(8,128)(2,1)S(1)}, u32[]{:S(2)}, u32[]{:S(2)}) collective-permute-start(bf16[2,56,1024]{2,1,0:T(8,128)(2,1)} %param.12), channel_id=1, source_target_pairs={{0,4},{1,5},{2,6},{3,7},{4,8},{5,9},{6,10},{7,11},{8,12},{9,13},{1... | collective-permute-start | bytes 688136 | tf_op jit(solution)/shard_map/ppermute | solution.py:270
  3.7 17.8 %collective-permute-start.1 = (bf16[2,56,1024]{2,1,0:T(8,128)(2,1)}, bf16[2,56,1024]{2,1,0:T(8,128)(2,1)S(1)}, u32[]{:S(2)}, u32[]{:S(2)}) collective-permute-start(bf16[2,56,1024]{2,1,0:T(8,128)(2,1)} %param.12), channel_id=1, source_target_pairs={{0,8},{1,9},{2,10},{3,11},{4,12},{5,13},{6,14},{7,15},{8,0},{9,1},... | collective-permute-start | bytes 688136 | tf_op jit(solution)/shard_map/ppermute | solution.py:270
  6.3 15.2 %collective-permute-start.2 = (bf16[2,56,1024]{2,1,0:T(8,128)(2,1)}, bf16[2,56,1024]{2,1,0:T(8,128)(2,1)S(1)}, u32[]{:S(2)}, u32[]{:S(2)}) collective-permute-start(bf16[2,56,1024]{2,1,0:T(8,128)(2,1)} %param.12), channel_id=1, source_target_pairs={{0,12},{1,13},{2,14},{3,15},{4,0},{5,1},{6,2},{7,3},{8,4},{9,5},{1... | collective-permute-start | bytes 688136 | tf_op jit(solution)/shard_map/ppermute | solution.py:270
  21.5 0.7 copy-start.8
  21.5 0.8 copy-start.9
  21.5 10.0 %copy-start.7 = (bf16[2,56,1024]{2,1,0:T(8,128)(2,1)S(1)}, bf16[2,56,1024]{2,1,0:T(8,128)(2,1)}, u32[]{:S(2)}) copy-start(bf16[2,56,1024]{2,1,0:T(8,128)(2,1)} %param.12) | copy-start | bytes 688132
  22.3 50.2 %all-to-all-start = ((bf16[8,2,64,896]{3,2,1,0:T(8,128)(2,1)}), bf16[8,2,64,896]{3,2,1,0:T(8,128)(2,1)}, u32[]{:S(2)}, u32[]{:S(2)}) async-start(bf16[8,2,64,896]{3,2,1,0:T(8,128)(2,1)} %bitcast.14), calls=%async_computation | async-start | bytes 3670016 | tf_op jit(solution)/shard_map/all_to_all | solution.py:265
  29.8 40.5 %collective-permute-start.3 = (bf16[8,64,896]{2,1,0:T(8,128)(2,1)S(1)}, bf16[8,64,896]{2,1,0:T(8,128)(2,1)S(1)}, u32[]{:S(2)}, u32[]{:S(2)}) collective-permute-start(bf16[8,64,896]{2,1,0:T(8,128)(2,1)S(1)} %multiply_convert_fusion.src_ref), channel_id=1, source_target_pairs={{0,8},{1,9},{2,10},{3,11},{4,12},{5,13},{6,14},{7,15},{8,0},{9,1},... | collective-permute-start | bytes 2752520 | tf_op jit(solution)/shard_map/ppermute | solution.py:258
  36.2 36.3 %collective-permute-start.4 = (bf16[8,56,1024]{2,1,0:T(8,128)(2,1)}, bf16[8,56,1024]{2,1,0:T(8,128)(2,1)}, u32[]{:S(2)}, u32[]{:S(2)}) collective-permute-start(bf16[8,56,1024]{2,1,0:T(8,128)(2,1)} %constant_dynamic-update-slice_fusion.w_ref), channel_id=1, source_target_pairs={{0,2},{1,3},{2,0},{3,1},{4,6},{5,7},{6,4},{7,5},{8,10},{9,11},{10,... | collective-permute-start | bytes 2752520 | tf_op jit(solution)/shard_map/ppermute | solution.py:258
  38.2 34.3 %collective-permute-start.5 = (bf16[8,56,1024]{2,1,0:T(8,128)(2,1)}, bf16[8,56,1024]{2,1,0:T(8,128)(2,1)}, u32[]{:S(2)}, u32[]{:S(2)}) collective-permute-start(bf16[8,56,1024]{2,1,0:T(8,128)(2,1)} %constant_dynamic-update-slice_fusion.w_ref), channel_id=1, source_target_pairs={{0,16},{16,0},{1,17},{17,1},{2,18},{18,2},{3,19},{19,3},{4,20},{20... | collective-permute-start | bytes 2752520 | tf_op jit(solution)/shard_map/ppermute | solution.py:261
  42.1 2.2 %collective-permute-start.6 = (bf16[8,56,512]{2,1,0:T(8,128)(2,1)}, bf16[8,56,512]{2,1,0:T(8,128)(2,1)}, u32[]{:S(2)}, u32[]{:S(2)}) collective-permute-start(bf16[8,56,512]{2,1,0:T(8,128)(2,1)} %get-tuple-element.42), channel_id=1, source_target_pairs={{0,1},{1,0},{2,3},{3,2},{4,5},{5,4},{6,7},{7,6},{8,9},{9,8},{10,11... | collective-permute-start | bytes 1376264 | tf_op jit(solution)/shard_map/ppermute | solution.py:258
  74.5 38.4 %all-to-all-start.1 = ((bf16[8,2,64,896]{3,2,1,0:T(8,128)(2,1)}), bf16[8,2,64,896]{3,2,1,0:T(8,128)(2,1)}, u32[]{:S(2)}, u32[]{:S(2)}) async-start(bf16[8,2,64,896]{3,2,1,0:T(8,128)(2,1)} %bitcast.18), calls=%async_computation.1 | async-start | bytes 3670016 | tf_op jit(solution)/shard_map/all_to_all | solution.py:265
  78.9 32.1 %collective-permute-start.8 = (bf16[8,56,1024]{2,1,0:T(8,128)(2,1)}, bf16[8,56,1024]{2,1,0:T(8,128)(2,1)S(1)}, u32[]{:S(2)}, u32[]{:S(2)}) collective-permute-start(bf16[8,56,1024]{2,1,0:T(8,128)(2,1)} %collective-permute-done.4.w_ref), channel_id=1, source_target_pairs={{0,16},{16,0},{1,17},{17,1},{2,18},{18,2},{3,19},{19,3},{4,20},{20... | collective-permute-start | bytes 2752520 | tf_op jit(solution)/shard_map/ppermute | solution.py:261
  82.8 4.6 %collective-permute-start.9 = (bf16[8,56,512]{2,1,0:T(8,128)(2,1)}, bf16[8,56,512]{2,1,0:T(8,128)(2,1)S(1)}, u32[]{:S(2)}, u32[]{:S(2)}) collective-permute-start(bf16[8,56,512]{2,1,0:T(8,128)(2,1)} %get-tuple-element.50), channel_id=1, source_target_pairs={{0,1},{1,0},{2,3},{3,2},{4,5},{5,4},{6,7},{7,6},{8,9},{9,8},{10,11... | collective-permute-start | bytes 1376264 | tf_op jit(solution)/shard_map/ppermute | solution.py:258
  85.1 4.9 %copy-start.5 = (bf16[8,56,512]{2,1,0:T(8,128)(2,1)S(1)}, bf16[8,56,512]{2,1,0:T(8,128)(2,1)}, u32[]{:S(2)}) copy-start(bf16[8,56,512]{2,1,0:T(8,128)(2,1)} %get-tuple-element.52) | copy-start | bytes 1376260
  85.1 4.9 %collective-permute-start.10 = (bf16[8,56,512]{2,1,0:T(8,128)(2,1)}, bf16[8,56,512]{2,1,0:T(8,128)(2,1)S(1)}, u32[]{:S(2)}, u32[]{:S(2)}) collective-permute-start(bf16[8,56,512]{2,1,0:T(8,128)(2,1)} %get-tuple-element.53), channel_id=1, source_target_pairs={{0,1},{1,0},{2,3},{3,2},{4,5},{5,4},{6,7},{7,6},{8,9},{9,8},{10,11... | collective-permute-start | bytes 1376264 | tf_op jit(solution)/shard_map/ppermute | solution.py:258
  85.6 25.3 %collective-permute-start.7 = (bf16[4,2,128,256]{3,2,1,0:T(8,128)(2,1)}, bf16[4,2,128,256]{3,2,1,0:T(8,128)(2,1)}, u32[]{:S(2)}, u32[]{:S(2)}) collective-permute-start(bf16[4,2,128,256]{3,2,1,0:T(8,128)(2,1)} %get-tuple-element.47), channel_id=1, source_target_pairs={{0,8},{1,9},{2,10},{3,11},{4,12},{5,13},{6,14},{7,15},{8,0},{9,1},... | collective-permute-start | bytes 1572872 | tf_op jit(solution)/shard_map/ppermute | solution.py:258
  87.4 0.8 copy-start.6
  110.9 5.0 %copy-start.4 = (bf16[8,56,1024]{2,1,0:T(8,128)(2,1)}, bf16[8,56,1024]{2,1,0:T(8,128)(2,1)S(1)}, u32[]{:S(2)}) copy-start(bf16[8,56,1024]{2,1,0:T(8,128)(2,1)S(1)} %collective-permute-done.8.w_ref) | copy-start | bytes 2752516
  115.9 7.9 %copy-start.1 = (bf16[4,64,896]{2,1,0:T(8,128)(2,1)S(1)}, bf16[4,64,896]{2,1,0:T(8,128)(2,1)}, u32[]{:S(2)}) copy-start(bf16[4,64,896]{2,1,0:T(8,128)(2,1)} %get-tuple-element.55) | copy-start | bytes 1376260
  118.1 18.4 %all-to-all-start.2 = ((bf16[4,2,2,128,256]{4,3,2,1,0:T(8,128)(2,1)}), bf16[4,2,2,128,256]{4,3,2,1,0:T(8,128)(2,1)S(1)}, u32[]{:S(2)}, u32[]{:S(2)}) async-start(bf16[4,2,2,128,256]{4,3,2,1,0:T(8,128)(2,1)} %pad_maximum_fusion), calls=%async_computation.2 | async-start | bytes 2097152 | tf_op jit(solution)/shard_map/all_to_all | solution.py:349
  122.3 12.1 %collective-permute-start.11 = (bf16[4,64,896]{2,1,0:T(8,128)(2,1)}, bf16[4,64,896]{2,1,0:T(8,128)(2,1)}, u32[]{:S(2)}, u32[]{:S(2)}) collective-permute-start(bf16[4,64,896]{2,1,0:T(8,128)(2,1)} %get-tuple-element.58), channel_id=1, source_target_pairs={{0,16},{16,0},{1,17},{17,1},{2,18},{18,2},{3,19},{19,3},{4,20},{20... | collective-permute-start | bytes 1376264 | tf_op jit(solution)/shard_map/ppermute | solution.py:261
  123.8 10.6 %collective-permute-start.12 = (bf16[2,128,896]{2,1,0:T(8,128)(2,1)S(1)}, bf16[2,128,896]{2,1,0:T(8,128)(2,1)}, u32[]{:S(2)}, u32[]{:S(2)}) collective-permute-start(bf16[2,128,896]{2,1,0:T(8,128)(2,1)S(1)} %bitcast.44), channel_id=1, source_target_pairs={{0,1},{1,0},{2,3},{3,2},{4,5},{5,4},{6,7},{7,6},{8,9},{9,8},{10,11... | collective-permute-start | bytes 1376264 | tf_op jit(solution)/shard_map/ppermute | solution.py:258
  126.1 8.3 %collective-permute-start.14 = (bf16[8,56,512]{2,1,0:T(8,128)(2,1)}, bf16[8,56,512]{2,1,0:T(8,128)(2,1)}, u32[]{:S(2)}, u32[]{:S(2)}) collective-permute-start(bf16[8,56,512]{2,1,0:T(8,128)(2,1)} %get-tuple-element.64), channel_id=1, source_target_pairs={{0,1},{1,0},{2,3},{3,2},{4,5},{5,4},{6,7},{7,6},{8,9},{9,8},{10,11... | collective-permute-start | bytes 1376264 | tf_op jit(solution)/shard_map/ppermute | solution.py:258
  134.3 2.2 %collective-permute-start.13 = (bf16[2,128,896]{2,1,0:T(8,128)(2,1)}, bf16[2,128,896]{2,1,0:T(8,128)(2,1)}, u32[]{:S(2)}, u32[]{:S(2)}) collective-permute-start(bf16[2,128,896]{2,1,0:T(8,128)(2,1)} %bitcast.25.nb), channel_id=1, source_target_pairs={{0,1},{1,0},{2,3},{3,2},{4,5},{5,4},{6,7},{7,6},{8,9},{9,8},{10,11... | collective-permute-start | bytes 1376264 | tf_op jit(solution)/shard_map/ppermute | solution.py:258
  136.5 1.2 copy-start
  137.7 1.0 copy-start.2
